TPU v7x, 32 devices: a whole 2x2x4 slice. The times are simulated.
32 devices in a mesh: dp: 4 (over y, core), row: 2 (over x), col: 4 (over z).
Axes of the slice: x: 2, y: 2, z: 4, core: 2. Of those that a mesh axis runs over, the one named last changes fastest.
Arguments:
- image_in: bfloat16 [3584, 1536], P(('dp', 'row'), 'col'), may hold values from -16 to 16
- text_in: bfloat16 [1232, 1536], P(('dp', 'row'), 'col'), may hold values from -16 to 16
- condition: float32 [8, 1536], P('dp', 'row'), may hold values from -6 to 6
- image_mod_weight: bfloat16 [1536, 6, 1536], P('row', None, 'col'), may hold values from -0.15625 to 0.15625
- image_mod_bias: float32 [6, 1536], P(None, 'col'), may hold values from -1 to 1
- image_qkv_weight: bfloat16 [1536, 4608], P('col', 'row'), may hold values from -0.15625 to 0.15625
- image_qv_bias: float32 [24, 2, 64], P(('row', 'col')), may hold values from -1.2 to 1.2
- image_out_weight: bfloat16 [1536, 1536], P('row', 'col'), may hold values from -0.875 to 0.875
- image_out_bias: float32 [1536], P('col'), may hold values from -1.8 to 1.8
- image_up_weight: bfloat16 [1536, 6144], P('col', 'row'), may hold values from -0.15625 to 0.15625
- image_up_bias: float32 [6144], P('row'), may hold values from -3 to 3
- image_down_weight: bfloat16 [6144, 1536], P('row', 'col'), may hold values from -0.078125 to 0.078125
- image_down_bias: float32 [1536], P('col'), may hold values from -1.8 to 1.8
- text_mod_weight: bfloat16 [1536, 6, 1536], P('row', None, 'col'), may hold values from -0.15625 to 0.15625
- text_mod_bias: float32 [6, 1536], P(None, 'col'), may hold values from -1 to 1
- text_qkv_weight: bfloat16 [1536, 4608], P('col', 'row'), may hold values from -0.15625 to 0.15625
- text_qv_bias: float32 [24, 2, 64], P(('row', 'col')), may hold values from -1.2 to 1.2
- text_out_weight: bfloat16 [1536, 1536], P('row', 'col'), may hold values from -0.875 to 0.875
- text_out_bias: float32 [1536], P('col'), may hold values from -1.8 to 1.8
- text_up_weight: bfloat16 [1536, 6144], P('col', 'row'), may hold values from -0.15625 to 0.15625
- text_up_bias: float32 [6144], P('row'), may hold values from -3 to 3
- text_down_weight: bfloat16 [6144, 1536], P('row', 'col'), may hold values from -0.078125 to 0.078125
- text_down_bias: float32 [1536], P('col'), may hold values from -1.8 to 1.8
- image_cotangent: bfloat16 [3584, 1536], P(('dp', 'row'), 'col'), may hold values from -6 to 6
- text_cotangent: bfloat16 [1232, 1536], P(('dp', 'row'), 'col'), may hold values from -6 to 6
Outputs:
- image_out: bfloat16 [3584, 1536], P(('dp', 'row'), 'col')
- text_out: bfloat16 [1232, 1536], P(('dp', 'row'), 'col')
- image_in_grad: float32 [3584, 1536], P(('dp', 'row'), 'col')
- text_in_grad: float32 [1232, 1536], P(('dp', 'row'), 'col')
- condition_grad: float32 [8, 1536], P('dp', 'row')
- image_mod_weight_grad: float32 [2, 768, 6, 1536], P('row', 'dp', None, 'col')
- image_mod_bias_grad: float32 [4, 384, 6], P('col', 'dp')
- image_qkv_weight_grad: float32 [4, 384, 4608], P('col', 'dp', 'row')
- image_qv_bias_grad: float32 [64, 24, 2], P('dp', ('row', 'col'))
- image_out_weight_grad: float32 [2, 768, 1536], P('row', 'dp', 'col')
- image_out_bias_grad: float32 [4, 384], P('col', 'dp')
- image_up_weight_grad: float32 [4, 384, 6144], P('col', 'dp', 'row')
- image_up_bias_grad: float32 [2, 3072], P('row', 'dp')
- image_down_weight_grad: float32 [2, 3072, 1536], P('row', 'dp', 'col')
- image_down_bias_grad: float32 [4, 384], P('col', 'dp')
- text_mod_weight_grad: float32 [2, 768, 6, 1536], P('row', 'dp', None, 'col')
- text_mod_bias_grad: float32 [4, 384, 6], P('col', 'dp')
- text_qkv_weight_grad: float32 [4, 384, 4608], P('col', 'dp', 'row')
- text_qv_bias_grad: float32 [64, 24, 2], P('dp', ('row', 'col'))
- text_out_weight_grad: float32 [2, 768, 1536], P('row', 'dp', 'col')
- text_out_bias_grad: float32 [4, 384], P('col', 'dp')
- text_up_weight_grad: float32 [4, 384, 6144], P('col', 'dp', 'row')
- text_up_bias_grad: float32 [2, 3072], P('row', 'dp')
- text_down_weight_grad: float32 [2, 3072, 1536], P('row', 'dp', 'col')
- text_down_bias_grad: float32 [4, 384], P('col', 'dp')
All inputs are finite; a program needn't handle non-finite values.
Results may differ from a plain program's by a relative error of at most 0.019.
The roundings to bfloat16 on the way count: a program that leaves them out, or rounds other values in their place, can miss the bound.
Values may be sent and summed in bfloat16 or wider, within the bound.
No kernel may reach another device: no remote copies, remote signals or barrier semaphores. Data moves between devices by JAX's collectives and lax.ppermute only.
A program may use at most 192 MiB of HBM per device.

v0:
```python
import jax
import jax.numpy as jnp
from jax import lax
from jax.sharding import PartitionSpec as P

EPS = 1e-06
GELU_C = 0.7978845608028654
GELU_K = 0.044715


def gelu_parts(hidden):
    tangent = jnp.tanh(GELU_C * (hidden + GELU_K * hidden * hidden * hidden))
    gelu_value = 0.5 * hidden * (1.0 + tangent)
    gelu_slope = 0.5 * (1.0 + tangent) + 0.5 * hidden * (1.0 - tangent * tangent) * GELU_C * (
        1.0 + 3.0 * GELU_K * hidden * hidden
    )
    return (gelu_value, gelu_slope)


def product(left_side, right_side):
    return jnp.dot(left_side, right_side, preferred_element_type=jnp.float32)


def transposed_left(left_side, right_side):
    return lax.dot_general(
        left_side, right_side, (((0,), (0,)), ((), ())), preferred_element_type=jnp.float32
    )


def transposed_right(left_side, right_side):
    return lax.dot_general(
        left_side, right_side, (((1,), (1,)), ((), ())), preferred_element_type=jnp.float32
    )


def flatten(values):
    return values.reshape(-1, values.shape[-1])


def mod_field(modulation, position):
    return modulation[:, position][:, None, :]


def bias_rows(qv_bias):
    zero_rows = jnp.zeros(qv_bias[:, 0].shape, jnp.float32)
    return jnp.stack([qv_bias[:, 0], zero_rows, qv_bias[:, 1]], axis=1)


def gather_rows(part_one, part_two):
    return (
        lax.all_gather(part_one, "row", axis=0, tiled=True),
        lax.all_gather(part_two, "row", axis=0, tiled=True),
    )


def scatter_rows(part_one, part_two):
    return (
        lax.psum_scatter(part_one, "row", scatter_dimension=0, tiled=True),
        lax.psum_scatter(part_two, "row", scatter_dimension=0, tiled=True),
    )


def gather_cols(part_one, part_two):
    return (
        lax.all_gather(part_one, "col", axis=0, tiled=True),
        lax.all_gather(part_two, "col", axis=0, tiled=True),
    )


def scatter_cols(part_one, part_two):
    return (
        lax.psum_scatter(part_one, "col", scatter_dimension=0, tiled=True),
        lax.psum_scatter(part_two, "col", scatter_dimension=0, tiled=True),
    )


def gather_heads(part_one, part_two):
    return (
        lax.all_gather(part_one, "col", axis=1, tiled=True),
        lax.all_gather(part_two, "col", axis=1, tiled=True),
    )


def scatter_heads(part_one, part_two):
    return (
        lax.psum_scatter(part_one, "col", scatter_dimension=1, tiled=True),
        lax.psum_scatter(part_two, "col", scatter_dimension=1, tiled=True),
    )


def feature_totals(part_one, part_two, part_three, part_four):
    return lax.psum((part_one, part_two, part_three, part_four), "col")


def norm_apply(values, sum_total, squares, full_width):
    average = (sum_total / full_width)[..., None]
    variance = (squares / full_width)[..., None] - average * average
    inv_std = lax.rsqrt(variance + EPS)
    return ((values - average) * inv_std, inv_std)


def norm_pair(image_vals, text_vals, full_width):
    totals = feature_totals(
        jnp.sum(image_vals, axis=-1),
        jnp.sum(image_vals * image_vals, axis=-1),
        jnp.sum(text_vals, axis=-1),
        jnp.sum(text_vals * text_vals, axis=-1),
    )
    return (
        norm_apply(image_vals, totals[0], totals[1], full_width),
        norm_apply(text_vals, totals[2], totals[3], full_width),
    )


def norm_back_apply(grad_hat, normed, inv_std, first_sum, second_sum, full_width):
    return inv_std * (
        grad_hat
        - (first_sum / full_width)[..., None]
        - normed * (second_sum / full_width)[..., None]
    )


def norm_back_pair(image_hat, image_norm, text_hat, text_norm, full_width):
    totals = feature_totals(
        jnp.sum(image_hat, axis=-1),
        jnp.sum(image_hat * image_norm[0], axis=-1),
        jnp.sum(text_hat, axis=-1),
        jnp.sum(text_hat * text_norm[0], axis=-1),
    )
    return (
        norm_back_apply(image_hat, image_norm[0], image_norm[1], totals[0], totals[1], full_width),
        norm_back_apply(text_hat, text_norm[0], text_norm[1], totals[2], totals[3], full_width),
    )


def attend_sequence(packed):
    queries = packed[:, :, 0]
    key_rows = packed[:, :, 1]
    value_rows = packed[:, :, 2]
    score_scale = packed.shape[-1] ** (-0.5)
    scores = (
        jnp.einsum("qhd,khd->hqk", queries, key_rows, preferred_element_type=jnp.float32)
        * score_scale
    )
    log_total = jnp.log(jnp.sum(jnp.exp(scores), axis=-1))
    attn_probs = jnp.exp(scores - log_total[..., None]).astype(jnp.bfloat16)
    attended = jnp.einsum(
        "hqk,khd->qhd", attn_probs, value_rows, preferred_element_type=jnp.float32
    ).astype(jnp.bfloat16)
    return (attended, log_total)


def attend_back(seq_items):
    packed, attended, log_total, d_attended = seq_items
    queries = packed[:, :, 0]
    key_rows = packed[:, :, 1]
    value_rows = packed[:, :, 2]
    score_scale = packed.shape[-1] ** (-0.5)
    scores = (
        jnp.einsum("qhd,khd->hqk", queries, key_rows, preferred_element_type=jnp.float32)
        * score_scale
    )
    soft_weights = jnp.exp(scores - log_total[..., None])
    row_delta = jnp.transpose(
        jnp.sum(d_attended.astype(jnp.float32) * attended.astype(jnp.float32), axis=-1)
    )
    d_values = jnp.einsum(
        "hqk,qhd->khd",
        soft_weights.astype(jnp.bfloat16),
        d_attended,
        preferred_element_type=jnp.float32,
    )
    d_probs = jnp.einsum("qhd,khd->hqk", d_attended, value_rows, preferred_element_type=jnp.float32)
    d_scores = (soft_weights * (d_probs - row_delta[..., None]) * score_scale).astype(jnp.bfloat16)
    d_queries = jnp.einsum("hqk,khd->qhd", d_scores, key_rows, preferred_element_type=jnp.float32)
    d_keys = jnp.einsum("hqk,qhd->khd", d_scores, queries, preferred_element_type=jnp.float32)
    return jnp.stack([d_queries, d_keys, d_values], axis=2).astype(jnp.bfloat16)


def shards(
    image_in,
    text_in,
    condition,
    image_mod_weight,
    image_mod_bias,
    image_qkv_weight,
    image_qv_bias,
    image_out_weight,
    image_out_bias,
    image_up_weight,
    image_up_bias,
    image_down_weight,
    image_down_bias,
    text_mod_weight,
    text_mod_bias,
    text_qkv_weight,
    text_qv_bias,
    text_out_weight,
    text_out_bias,
    text_up_weight,
    text_up_bias,
    text_down_weight,
    text_down_bias,
    image_cotangent,
    text_cotangent,
):
    weights = (
        (
            image_mod_weight,
            image_mod_bias,
            image_qkv_weight,
            image_qv_bias,
            image_out_weight,
            image_out_bias,
            image_up_weight,
            image_up_bias,
            image_down_weight,
            image_down_bias,
        ),
        (
            text_mod_weight,
            text_mod_bias,
            text_qkv_weight,
            text_qv_bias,
            text_out_weight,
            text_out_bias,
            text_up_weight,
            text_up_bias,
            text_down_weight,
            text_down_bias,
        ),
    )
    row_count = lax.axis_size("row")
    col_count = lax.axis_size("col")
    seq_count = condition.shape[0]
    local_count = seq_count // row_count
    col_width = image_in.shape[1]
    full_width = col_width * col_count
    head_count = image_qv_bias.shape[0]
    head_size = image_qv_bias.shape[2]
    image_len = image_in.shape[0] // local_count
    mod_rows = image_mod_weight.shape[0]
    streams = (0, 1)
    act_cond = (condition * jax.nn.sigmoid(condition)).astype(jnp.bfloat16)
    mod_pair = lax.psum(
        (
            product(act_cond, image_mod_weight.reshape(mod_rows, -1)),
            product(act_cond, text_mod_weight.reshape(mod_rows, -1)),
        ),
        "row",
    )
    row_index = lax.axis_index("row")
    modulation = []
    for stream in streams:
        full_mod = mod_pair[stream].reshape(seq_count, 6, col_width) + weights[stream][1][None]
        modulation.append(
            lax.dynamic_slice_in_dim(full_mod, row_index * local_count, local_count, 0)
        )
    values = [
        image_in.astype(jnp.float32).reshape(local_count, -1, col_width),
        text_in.astype(jnp.float32).reshape(local_count, -1, col_width),
    ]
    norm_one = norm_pair(values[0], values[1], full_width)
    mod_in = [
        flatten(
            norm_one[stream][0] * (1.0 + mod_field(modulation[stream], 1))
            + mod_field(modulation[stream], 0)
        ).astype(jnp.bfloat16)
        for stream in streams
    ]
    mod_in_all = gather_rows(mod_in[0], mod_in[1])
    qkv_local = scatter_heads(
        product(mod_in_all[0], image_qkv_weight), product(mod_in_all[1], text_qkv_weight)
    )
    packed = []
    for stream in streams:
        biased = qkv_local[stream].reshape(-1, head_count, 3, head_size) + bias_rows(
            weights[stream][3]
        )
        packed.append(biased.astype(jnp.bfloat16).reshape(seq_count, -1, head_count, 3, head_size))
    joint_qkv = jnp.concatenate(packed, axis=1)
    attended, log_total = lax.map(attend_sequence, joint_qkv)
    attn_all = gather_heads(
        attended[:, :image_len].reshape(-1, head_count * head_size),
        attended[:, image_len:].reshape(-1, head_count * head_size),
    )
    out_sum = scatter_rows(
        product(attn_all[0], image_out_weight), product(attn_all[1], text_out_weight)
    )
    branch_one = [
        (out_sum[stream] + weights[stream][5]).reshape(local_count, -1, col_width)
        for stream in streams
    ]
    middle = [
        values[stream] + mod_field(modulation[stream], 2) * branch_one[stream] for stream in streams
    ]
    norm_two = norm_pair(middle[0], middle[1], full_width)
    mod_two = [
        flatten(
            norm_two[stream][0] * (1.0 + mod_field(modulation[stream], 4))
            + mod_field(modulation[stream], 3)
        ).astype(jnp.bfloat16)
        for stream in streams
    ]
    mod_two_all = gather_rows(mod_two[0], mod_two[1])
    hidden_sum = scatter_cols(
        product(mod_two_all[0], image_up_weight), product(mod_two_all[1], text_up_weight)
    )
    gelu_both = [gelu_parts(hidden_sum[stream] + weights[stream][7]) for stream in streams]
    gelu_all = gather_cols(
        gelu_both[0][0].astype(jnp.bfloat16), gelu_both[1][0].astype(jnp.bfloat16)
    )
    down_sum = scatter_rows(
        product(gelu_all[0], image_down_weight), product(gelu_all[1], text_down_weight)
    )
    branch_two = [
        (down_sum[stream] + weights[stream][9]).reshape(local_count, -1, col_width)
        for stream in streams
    ]
    outputs = [
        flatten(middle[stream] + mod_field(modulation[stream], 5) * branch_two[stream]).astype(
            jnp.bfloat16
        )
        for stream in streams
    ]
    grad_out = [
        image_cotangent.astype(jnp.float32).reshape(local_count, -1, col_width),
        text_cotangent.astype(jnp.float32).reshape(local_count, -1, col_width),
    ]
    d_gate_two = [jnp.sum(grad_out[stream] * branch_two[stream], axis=1) for stream in streams]
    d_branch_two = [
        flatten(grad_out[stream] * mod_field(modulation[stream], 5)).astype(jnp.bfloat16)
        for stream in streams
    ]
    d_branch_two_all = gather_rows(d_branch_two[0], d_branch_two[1])
    down_w_grad = [
        transposed_left(gelu_all[stream], d_branch_two_all[stream]) for stream in streams
    ]
    down_b_grad = [
        jnp.sum(d_branch_two_all[stream].astype(jnp.float32), axis=0) for stream in streams
    ]
    d_gelu = scatter_cols(
        transposed_right(d_branch_two_all[0], image_down_weight),
        transposed_right(d_branch_two_all[1], text_down_weight),
    )
    d_hidden = [(d_gelu[stream] * gelu_both[stream][1]).astype(jnp.bfloat16) for stream in streams]
    d_hidden_all = gather_cols(d_hidden[0], d_hidden[1])
    up_w_grad = [transposed_left(mod_two_all[stream], d_hidden_all[stream]) for stream in streams]
    up_b_grad = [jnp.sum(d_hidden_all[stream].astype(jnp.float32), axis=0) for stream in streams]
    d_mod_two_sum = scatter_rows(
        transposed_right(d_hidden_all[0], image_up_weight),
        transposed_right(d_hidden_all[1], text_up_weight),
    )
    d_mod_two = [d_mod_two_sum[stream].reshape(local_count, -1, col_width) for stream in streams]
    d_shift_two = [jnp.sum(d_mod_two[stream], axis=1) for stream in streams]
    d_scale_two = [jnp.sum(d_mod_two[stream] * norm_two[stream][0], axis=1) for stream in streams]
    back_two = norm_back_pair(
        d_mod_two[0] * (1.0 + mod_field(modulation[0], 4)),
        norm_two[0],
        d_mod_two[1] * (1.0 + mod_field(modulation[1], 4)),
        norm_two[1],
        full_width,
    )
    d_middle = [grad_out[stream] + back_two[stream] for stream in streams]
    d_gate_one = [jnp.sum(d_middle[stream] * branch_one[stream], axis=1) for stream in streams]
    d_branch_one = [
        flatten(d_middle[stream] * mod_field(modulation[stream], 2)).astype(jnp.bfloat16)
        for stream in streams
    ]
    d_branch_one_all = gather_rows(d_branch_one[0], d_branch_one[1])
    out_w_grad = [transposed_left(attn_all[stream], d_branch_one_all[stream]) for stream in streams]
    out_b_grad = [
        jnp.sum(d_branch_one_all[stream].astype(jnp.float32), axis=0) for stream in streams
    ]
    d_attn_sum = scatter_heads(
        transposed_right(d_branch_one_all[0], image_out_weight),
        transposed_right(d_branch_one_all[1], text_out_weight),
    )
    d_attn_joint = jnp.concatenate(
        [
            d_attn_sum[stream].astype(jnp.bfloat16).reshape(seq_count, -1, head_count, head_size)
            for stream in streams
        ],
        axis=1,
    )
    d_packed = lax.map(attend_back, (joint_qkv, attended, log_total, d_attn_joint))
    d_parts = [d_packed[:, :image_len], d_packed[:, image_len:]]
    qv_b_grad = []
    for stream in streams:
        d_sums = jnp.sum(d_parts[stream].astype(jnp.float32), axis=(0, 1))
        qv_b_grad.append(jnp.transpose(jnp.stack([d_sums[:, 0], d_sums[:, 2]], axis=1), (2, 0, 1)))
    d_qkv_all = gather_heads(
        d_parts[0].reshape(-1, head_count * 3 * head_size),
        d_parts[1].reshape(-1, head_count * 3 * head_size),
    )
    qkv_w_grad = [transposed_left(mod_in_all[stream], d_qkv_all[stream]) for stream in streams]
    d_mod_one_sum = scatter_rows(
        transposed_right(d_qkv_all[0], image_qkv_weight),
        transposed_right(d_qkv_all[1], text_qkv_weight),
    )
    d_mod_one = [d_mod_one_sum[stream].reshape(local_count, -1, col_width) for stream in streams]
    d_shift_one = [jnp.sum(d_mod_one[stream], axis=1) for stream in streams]
    d_scale_one = [jnp.sum(d_mod_one[stream] * norm_one[stream][0], axis=1) for stream in streams]
    back_one = norm_back_pair(
        d_mod_one[0] * (1.0 + mod_field(modulation[0], 1)),
        norm_one[0],
        d_mod_one[1] * (1.0 + mod_field(modulation[1], 1)),
        norm_one[1],
        full_width,
    )
    in_grads = [flatten(d_middle[stream] + back_one[stream]) for stream in streams]
    d_mod_local = [
        jnp.stack(
            [
                d_shift_one[stream],
                d_scale_one[stream],
                d_gate_one[stream],
                d_shift_two[stream],
                d_scale_two[stream],
                d_gate_two[stream],
            ],
            axis=1,
        ).astype(jnp.bfloat16)
        for stream in streams
    ]
    d_mod_all = gather_rows(d_mod_local[0], d_mod_local[1])
    mod_b_grad = [
        jnp.transpose(jnp.sum(d_mod_all[stream].astype(jnp.float32), axis=0)) for stream in streams
    ]
    d_mod_flat = [d_mod_all[stream].reshape(seq_count, -1) for stream in streams]
    mod_w_grad = [
        transposed_left(act_cond, d_mod_flat[stream]).reshape(mod_rows, 6, col_width)
        for stream in streams
    ]
    cond_part = transposed_right(
        d_mod_flat[0], image_mod_weight.reshape(mod_rows, -1)
    ) + transposed_right(d_mod_flat[1], text_mod_weight.reshape(mod_rows, -1))
    cond_sum = lax.psum(cond_part, "col")
    sigmoid_cond = jax.nn.sigmoid(condition)
    condition_grad = cond_sum * sigmoid_cond * (1.0 + condition * (1.0 - sigmoid_cond))
    reduced = (
        lax.psum_scatter(
            mod_w_grad[0].astype(jnp.bfloat16), "dp", scatter_dimension=0, tiled=True
        ).astype(jnp.float32),
        lax.psum_scatter(
            mod_b_grad[0].astype(jnp.bfloat16), "dp", scatter_dimension=0, tiled=True
        ).astype(jnp.float32),
        lax.psum_scatter(
            qkv_w_grad[0].astype(jnp.bfloat16), "dp", scatter_dimension=0, tiled=True
        ).astype(jnp.float32),
        lax.psum_scatter(
            qv_b_grad[0].astype(jnp.bfloat16), "dp", scatter_dimension=0, tiled=True
        ).astype(jnp.float32),
        lax.psum_scatter(
            out_w_grad[0].astype(jnp.bfloat16), "dp", scatter_dimension=0, tiled=True
        ).astype(jnp.float32),
        lax.psum_scatter(
            out_b_grad[0].astype(jnp.bfloat16), "dp", scatter_dimension=0, tiled=True
        ).astype(jnp.float32),
        lax.psum_scatter(
            up_w_grad[0].astype(jnp.bfloat16), "dp", scatter_dimension=0, tiled=True
        ).astype(jnp.float32),
        lax.psum_scatter(
            up_b_grad[0].astype(jnp.bfloat16), "dp", scatter_dimension=0, tiled=True
        ).astype(jnp.float32),
        lax.psum_scatter(
            down_w_grad[0].astype(jnp.bfloat16), "dp", scatter_dimension=0, tiled=True
        ).astype(jnp.float32),
        lax.psum_scatter(
            down_b_grad[0].astype(jnp.bfloat16), "dp", scatter_dimension=0, tiled=True
        ).astype(jnp.float32),
        lax.psum_scatter(
            mod_w_grad[1].astype(jnp.bfloat16), "dp", scatter_dimension=0, tiled=True
        ).astype(jnp.float32),
        lax.psum_scatter(
            mod_b_grad[1].astype(jnp.bfloat16), "dp", scatter_dimension=0, tiled=True
        ).astype(jnp.float32),
        lax.psum_scatter(
            qkv_w_grad[1].astype(jnp.bfloat16), "dp", scatter_dimension=0, tiled=True
        ).astype(jnp.float32),
        lax.psum_scatter(
            qv_b_grad[1].astype(jnp.bfloat16), "dp", scatter_dimension=0, tiled=True
        ).astype(jnp.float32),
        lax.psum_scatter(
            out_w_grad[1].astype(jnp.bfloat16), "dp", scatter_dimension=0, tiled=True
        ).astype(jnp.float32),
        lax.psum_scatter(
            out_b_grad[1].astype(jnp.bfloat16), "dp", scatter_dimension=0, tiled=True
        ).astype(jnp.float32),
        lax.psum_scatter(
            up_w_grad[1].astype(jnp.bfloat16), "dp", scatter_dimension=0, tiled=True
        ).astype(jnp.float32),
        lax.psum_scatter(
            up_b_grad[1].astype(jnp.bfloat16), "dp", scatter_dimension=0, tiled=True
        ).astype(jnp.float32),
        lax.psum_scatter(
            down_w_grad[1].astype(jnp.bfloat16), "dp", scatter_dimension=0, tiled=True
        ).astype(jnp.float32),
        lax.psum_scatter(
            down_b_grad[1].astype(jnp.bfloat16), "dp", scatter_dimension=0, tiled=True
        ).astype(jnp.float32),
    )
    return (
        outputs[0],
        outputs[1],
        in_grads[0],
        in_grads[1],
        condition_grad,
        reduced[0][None],
        reduced[1][None],
        reduced[2][None],
        reduced[3],
        reduced[4][None],
        reduced[5][None],
        reduced[6][None],
        reduced[7][None],
        reduced[8][None],
        reduced[9][None],
        reduced[10][None],
        reduced[11][None],
        reduced[12][None],
        reduced[13],
        reduced[14][None],
        reduced[15][None],
        reduced[16][None],
        reduced[17][None],
        reduced[18][None],
        reduced[19][None],
    )


def solution(mesh):
    in_specs = (
        P(("dp", "row"), "col"),
        P(("dp", "row"), "col"),
        P("dp", "row"),
        P("row", None, "col"),
        P(None, "col"),
        P("col", "row"),
        P(("row", "col"), None, None),
        P("row", "col"),
        P("col"),
        P("col", "row"),
        P("row"),
        P("row", "col"),
        P("col"),
        P("row", None, "col"),
        P(None, "col"),
        P("col", "row"),
        P(("row", "col"), None, None),
        P("row", "col"),
        P("col"),
        P("col", "row"),
        P("row"),
        P("row", "col"),
        P("col"),
        P(("dp", "row"), "col"),
        P(("dp", "row"), "col"),
    )
    out_specs = (
        P(("dp", "row"), "col"),
        P(("dp", "row"), "col"),
        P(("dp", "row"), "col"),
        P(("dp", "row"), "col"),
        P("dp", "row"),
        P("row", "dp", None, "col"),
        P("col", "dp", None),
        P("col", "dp", "row"),
        P("dp", ("row", "col"), None),
        P("row", "dp", "col"),
        P("col", "dp"),
        P("col", "dp", "row"),
        P("row", "dp"),
        P("row", "dp", "col"),
        P("col", "dp"),
        P("row", "dp", None, "col"),
        P("col", "dp", None),
        P("col", "dp", "row"),
        P("dp", ("row", "col"), None),
        P("row", "dp", "col"),
        P("col", "dp"),
        P("col", "dp", "row"),
        P("row", "dp"),
        P("row", "dp", "col"),
        P("col", "dp"),
    )
    return jax.shard_map(shards, mesh=mesh, in_specs=in_specs, out_specs=out_specs, check_vma=False)
```

profile of v0, /device:TPU:0, one launch (start us, length us, event | category | flops | bytes accessed | tf_op | source)
XLA Modules:
  0.0 1929.3 jit_solution(11863720460083385374)
XLA Ops:
  77.2 48.4 %reduce-scatter.85.cloned.1.call-done = f32[576,308]{1,0:T(8,128)} async-done(((f32[2304,308]{1,0:T(8,128)}), f32[576,308]{1,0:T(8,128)}) %reduce-scatter.85.cloned.1.call-update) | async-done | bytes 709648
  131.5 139.2 %reduce-scatter.47.cloned.1.call-done = f32[896,576]{0,1:T(8,128)} async-done(((f32[896,2304]{0,1:T(8,128)}), f32[896,576]{0,1:T(8,128)}) %reduce-scatter.47.cloned.1.call-update) | async-done | bytes 2064400 | tf_op jit(solution)/shard_map/reduce_scatter | solution.py:86
  290.3 34.3 %all-gather.15.cloned.1.call-done = bf16[896,768]{0,1:T(8,128)(2,1)} async-done(((bf16[896,192]{0,1:T(8,128)(2,1)}), bf16[896,768]{0,1:T(8,128)(2,1)}) %all-gather.15.cloned.1.call-update) | async-done | bytes 1376272 | tf_op jit(solution)/shard_map/all_gather | solution.py:79
  421.7 124.1 %reduce-scatter.55.cloned.1.call-done = f32[224,3072]{1,0:T(8,128)} async-done(((f32[896,3072]{1,0:T(8,128)}), f32[224,3072]{1,0:T(8,128)}) %reduce-scatter.55.cloned.1.call-update) | async-done | bytes 2752528 | tf_op jit(solution)/shard_map/reduce_scatter | solution.py:72
  545.7 190.9 %reduce-scatter.51.cloned.1.call-done = f32[224,3072]{1,0:T(8,128)} async-done(((f32[896,3072]{1,0:T(8,128)}), f32[224,3072]{1,0:T(8,128)}) %reduce-scatter.51.cloned.1.call-update) | async-done | bytes 2752528 | tf_op jit(solution)/shard_map/reduce_scatter | solution.py:72
  766.3 246.3 %fusion.100 = (f32[80,3072]{1,0:T(8,128)}, f32[80,3072]{1,0:T(8,128)}) fusion(f32[308,3072]{1,0:T(8,128)} %fusion.115, f32[308,3072]{1,0:T(8,128)} %fusion.120), kind=kCustom, calls=%all-reduce-scatter.6 | all-reduce-scatter fusion | flops 1966081 | bytes 9536000
  1014.2 39.8 %collective-permute-start.3 = (f32[9,3072]{1,0:T(8,128)}, f32[9,3072]{1,0:T(8,128)}, u32[]{:S(2)}, u32[]{:S(2)}) collective-permute-start(f32[9,3072]{1,0:T(8,128)} %slice.151), channel_id=1, source_target_pairs={{0,1},{1,2},{2,3},{4,5},{5,6},{6,7},{8,9},{9,10},{10,11},{12,13},{... | collective-permute-start | bytes 331784
  1091.7 29.2 %all-gather.25.cloned.1.call-done = bf16[4,77,3072]{2,1,0:T(8,128)(2,1)} async-done(((bf16[1,77,3072]{2,1,0:T(8,128)(2,1)}), bf16[4,77,3072]{2,1,0:T(8,128)(2,1)}) %all-gather.25.cloned.1.call-update) | async-done | bytes 1892368 | tf_op jit(solution)/shard_map/all_gather | solution.py:66
  1214.6 53.4 %reduce-scatter.59.cloned.1.call-done = f32[896,192]{0,1:T(8,128)} async-done(((f32[896,768]{0,1:T(8,128)}), f32[896,192]{0,1:T(8,128)}) %reduce-scatter.59.cloned.1.call-update) | async-done | bytes 688144 | tf_op jit(solution)/shard_map/reduce_scatter | solution.py:86
  1293.7 75.5 %all-gather.21.cloned.1.call-done = bf16[896,2304]{0,1:T(8,128)(2,1)} async-done(((bf16[896,576]{0,1:T(8,128)(2,1)}), bf16[896,2304]{0,1:T(8,128)(2,1)}) %all-gather.21.cloned.1.call-update) | async-done | bytes 4128784 | tf_op jit(solution)/shard_map/all_gather | solution.py:79
  1375.6 37.7 %all-gather.23.cloned.1.call-done = bf16[4,77,3072]{2,1,0:T(8,128)(2,1)} async-done(((bf16[1,77,3072]{2,1,0:T(8,128)(2,1)}), bf16[4,77,3072]{2,1,0:T(8,128)(2,1)}) %all-gather.23.cloned.1.call-update) | async-done | bytes 1892368 | tf_op jit(solution)/shard_map/all_gather | solution.py:66
  1459.9 26.8 %fusion.101 = (f32[160,384]{1,0:T(8,128)S(1)}, f32[160,384]{1,0:T(8,128)S(1)}) fusion(f32[308,384]{1,0:T(8,128)} %fusion.116, f32[308,384]{1,0:T(8,128)} %fusion.124), kind=kCustom, calls=%all-reduce-scatter.7 | all-reduce-scatter fusion | flops 245761 | bytes 1438208
  1529.8 29.2 %reduce-scatter.81.cloned.1.call-done = bf16[96,3072]{1,0:T(8,128)(2,1)} async-done(((bf16[384,3072]{1,0:T(8,128)(2,1)}), bf16[96,3072]{1,0:T(8,128)(2,1)}) %reduce-scatter.81.cloned.1.call-update) | async-done | bytes 589840 | tf_op jit(solution)/shard_map/reduce_scatter | solution.py:490
  1585.3 23.7 %reduce-scatter.69.cloned.1.call-done = bf16[192,384]{1,0:T(8,128)(2,1)} async-done(((bf16[768,384]{1,0:T(8,128)(2,1)}), bf16[192,384]{1,0:T(8,128)(2,1)}) %reduce-scatter.69.cloned.1.call-update) | async-done | bytes 147472 | tf_op jit(solution)/shard_map/reduce_scatter | solution.py:454
  1610.7 34.2 %reduce-scatter.73.cloned.1.call-done = bf16[768,384]{1,0:T(8,128)(2,1)} async-done(((bf16[3072,384]{1,0:T(8,128)(2,1)}), bf16[768,384]{1,0:T(8,128)(2,1)}) %reduce-scatter.73.cloned.1.call-update) | async-done | bytes 589840 | tf_op jit(solution)/shard_map/reduce_scatter | solution.py:466
  1647.0 33.5 %reduce-scatter.71.cloned.1.call-done = bf16[96,3072]{1,0:T(8,128)(2,1)} async-done(((bf16[384,3072]{1,0:T(8,128)(2,1)}), bf16[96,3072]{1,0:T(8,128)(2,1)}) %reduce-scatter.71.cloned.1.call-update) | async-done | bytes 589840 | tf_op jit(solution)/shard_map/reduce_scatter | solution.py:460
  1682.6 19.6 %reduce-scatter.93.cloned.1.call-done = bf16[16,6]{1,0:T(8,128)(2,1)} async-done(((bf16[64,6]{1,0:T(8,128)(2,1)}), bf16[16,6]{1,0:T(8,128)(2,1)}) %reduce-scatter.93.cloned.1.call-update) | async-done | bytes 208
  1703.7 20.3 %reduce-scatter.89.cloned.1.call-done = bf16[16,6]{1,0:T(8,128)(2,1)} async-done(((bf16[64,6]{1,0:T(8,128)(2,1)}), bf16[16,6]{1,0:T(8,128)(2,1)}) %reduce-scatter.89.cloned.1.call-update) | async-done | bytes 208
  1725.4 21.1 %reduce-scatter.91.cloned.1.call-done = bf16[96,6]{1,0:T(8,128)(2,1)} async-done(((bf16[384,6]{1,0:T(8,128)(2,1)}), bf16[96,6]{1,0:T(8,128)(2,1)}) %reduce-scatter.91.cloned.1.call-update) | async-done | bytes 1168
  1747.9 31.2 %reduce-scatter.77.cloned.1.call-done = bf16[96,2304]{1,0:T(8,128)(2,1)} async-done(((bf16[384,2304]{1,0:T(8,128)(2,1)}), bf16[96,2304]{1,0:T(8,128)(2,1)}) %reduce-scatter.77.cloned.1.call-update) | async-done | bytes 442384 | tf_op jit(solution)/shard_map/reduce_scatter | solution.py:478
  1785.3 18.7 all-reduce.18
  1808.1 36.0 %reduce-scatter.75.cloned.1.call-done = bf16[192,6,384]{2,0,1:T(8,128)(2,1)} async-done(((bf16[768,6,384]{2,0,1:T(8,128)(2,1)}), bf16[192,6,384]{2,0,1:T(8,128)(2,1)}) %reduce-scatter.75.cloned.1.call-update) | async-done | bytes 884752 | tf_op jit(solution)/shard_map/reduce_scatter | solution.py:472
  1846.8 29.9 %reduce-scatter.67.cloned.1.call-done = bf16[96,2304]{1,0:T(8,128)(2,1)} async-done(((bf16[384,2304]{1,0:T(8,128)(2,1)}), bf16[96,2304]{1,0:T(8,128)(2,1)}) %reduce-scatter.67.cloned.1.call-update) | async-done | bytes 442384 | tf_op jit(solution)/shard_map/reduce_scatter | solution.py:448
  1878.7 41.1 %reduce-scatter.65.cloned.1.call-done = bf16[192,6,384]{2,0,1:T(8,128)(2,1)} async-done(((bf16[768,6,384]{2,0,1:T(8,128)(2,1)}), bf16[192,6,384]{2,0,1:T(8,128)(2,1)}) %reduce-scatter.65.cloned.1.call-update) | async-done | bytes 884752 | tf_op jit(solution)/shard_map/reduce_scatter | solution.py:442
  (543 shorter events, 548.5 us)
Async XLA Ops:
  61.8 208.9 %reduce-scatter.47.cloned.1.call-start = ((), (), s32[]{:S(2)}) async-start(), calls=%async_computation.24 | async-start | bytes 10321920 | tf_op jit(solution)/shard_map/reduce_scatter | solution.py:86
  76.5 248.1 %all-gather.15.cloned.1.call-start = ((), (), s32[]{:S(2)}) async-start(), calls=%async_computation.25 | async-start | bytes 1720320 | tf_op jit(solution)/shard_map/all_gather | solution.py:79
  328.1 217.6 %reduce-scatter.55.cloned.1.call-start = ((), (), s32[]{:S(2)}) async-start(), calls=%async_computation.30 | async-start | bytes 13762560 | tf_op jit(solution)/shard_map/reduce_scatter | solution.py:72
  353.2 383.4 %reduce-scatter.51.cloned.1.call-start = ((), (), s32[]{:S(2)}) async-start(), calls=%async_computation.27 | async-start | bytes 13762560 | tf_op jit(solution)/shard_map/reduce_scatter | solution.py:72
  421.6 655.6 %all-gather.19.cloned.1.call-start = ((), (), s32[]{:S(2)}) async-start(), calls=%async_computation.31 | async-start | bytes 6881280 | tf_op jit(solution)/shard_map/all_gather | solution.py:65
  741.5 342.4 %all-gather.17.cloned.1.call-start = ((), (), s32[]{:S(2)}) async-start(), calls=%async_computation.28 | async-start | bytes 6881280 | tf_op jit(solution)/shard_map/all_gather | solution.py:65
  742.3 378.7 %all-gather.25.cloned.1.call-start = ((), (), s32[]{:S(2)}) async-start(), calls=%async_computation.48 | async-start | bytes 2457600 | tf_op jit(solution)/shard_map/all_gather | solution.py:66
  1196.5 172.7 %all-gather.21.cloned.1.call-start = ((), (), s32[]{:S(2)}) async-start(), calls=%async_computation.35 | async-start | bytes 5160960 | tf_op jit(solution)/shard_map/all_gather | solution.py:79
  1290.2 161.5 %all-gather.27.cloned.1.call-start = ((), (), s32[]{:S(2)}) async-start(), calls=%async_computation.49 | async-start | bytes 1996800 | tf_op jit(solution)/shard_map/all_gather | solution.py:80
  1293.6 210.8 %reduce-scatter.63.cloned.1.call-start = ((), (), s32[]{:S(2)}) async-start(), calls=%async_computation.36 | async-start | bytes 2064384 | tf_op jit(solution)/shard_map/reduce_scatter | solution.py:58
  1375.4 149.3 %reduce-scatter.83.cloned.1.call-start = ((), (), s32[]{:S(2)}) async-start(), calls=%async_computation.46 | async-start | bytes 2949120 | tf_op jit(solution)/shard_map/reduce_scatter | solution.py:496
  1419.8 139.2 %reduce-scatter.81.cloned.1.call-start = ((), (), s32[]{:S(2)}) async-start(), calls=%async_computation.45 | async-start | bytes 2949120 | tf_op jit(solution)/shard_map/reduce_scatter | solution.py:490
  1424.2 159.4 %reduce-scatter.79.cloned.1.call-start = ((), (), s32[]{:S(2)}) async-start(), calls=%async_computation.44 | async-start | bytes 737280 | tf_op jit(solution)/shard_map/reduce_scatter | solution.py:484
  1426.7 182.3 %reduce-scatter.69.cloned.1.call-start = ((), (), s32[]{:S(2)}) async-start(), calls=%async_computation.39 | async-start | bytes 737280 | tf_op jit(solution)/shard_map/reduce_scatter | solution.py:454
  1428.5 216.3 %reduce-scatter.73.cloned.1.call-start = ((), (), s32[]{:S(2)}) async-start(), calls=%async_computation.41 | async-start | bytes 2949120 | tf_op jit(solution)/shard_map/reduce_scatter | solution.py:466
  1435.9 244.5 %reduce-scatter.71.cloned.1.call-start = ((), (), s32[]{:S(2)}) async-start(), calls=%async_computation.40 | async-start | bytes 2949120 | tf_op jit(solution)/shard_map/reduce_scatter | solution.py:460
  1443.7 258.5 %reduce-scatter.93.cloned.1.call-start = ((), (), s32[]{:S(2)}) async-start(), calls=%async_computation.54 | async-start | bytes 20480
  1449.7 274.2 %reduce-scatter.89.cloned.1.call-start = ((), (), s32[]{:S(2)}) async-start(), calls=%async_computation.52 | async-start | bytes 20480
  1489.8 256.7 %reduce-scatter.91.cloned.1.call-start = ((), (), s32[]{:S(2)}) async-start(), calls=%async_computation.53 | async-start | bytes 122880
  1501.9 277.2 %reduce-scatter.77.cloned.1.call-start = ((), (), s32[]{:S(2)}) async-start(), calls=%async_computation.43 | async-start | bytes 2211840 | tf_op jit(solution)/shard_map/reduce_scatter | solution.py:478
  1504.3 302.4 %reduce-scatter.87.cloned.1.call-start = ((), (), s32[]{:S(2)}) async-start(), calls=%async_computation.51 | async-start | bytes 122880
  1511.3 332.8 %reduce-scatter.75.cloned.1.call-start = ((), (), s32[]{:S(2)}) async-start(), calls=%async_computation.42 | async-start | bytes 4423680 | tf_op jit(solution)/shard_map/reduce_scatter | solution.py:472
  1514.4 362.3 %reduce-scatter.67.cloned.1.call-start = ((), (), s32[]{:S(2)}) async-start(), calls=%async_computation.38 | async-start | bytes 2211840 | tf_op jit(solution)/shard_map/reduce_scatter | solution.py:448
  1520.9 398.8 %reduce-scatter.65.cloned.1.call-start = ((), (), s32[]{:S(2)}) async-start(), calls=%async_computation.37 | async-start | bytes 4423680 | tf_op jit(solution)/shard_map/reduce_scatter | solution.py:442
  (120 other events, 4676.5 us)
Sparse Core Ops, SparseCore 0:
  61.9 63.6 reduce-scatter.84
  127.9 142.6 reduce-scatter.46
  290.0 34.5 all-gather.14
  357.1 188.5 reduce-scatter.54
  547.9 188.6 reduce-scatter.50
  741.6 176.9 all-gather.18
  920.2 140.8 all-gather.16
  1076.7 44.1 all-gather.24
  1123.0 28.0 reduce-scatter.56
  1154.0 26.7 reduce-scatter.52
  1183.6 29.1 reduce-scatter.60
  1215.1 52.8 reduce-scatter.58
  1289.7 79.4 all-gather.20
  1371.2 42.0 all-gather.22
  1415.3 36.3 all-gather.26
  1454.4 33.2 reduce-scatter.62
  1490.2 33.0 reduce-scatter.82
  1525.9 33.0 reduce-scatter.80
  1611.7 33.0 reduce-scatter.72
  1647.4 33.0 reduce-scatter.70
  1749.7 29.3 reduce-scatter.76
  1803.6 40.4 reduce-scatter.74
  1847.3 29.3 reduce-scatter.66
  1879.3 40.4 reduce-scatter.64
  (7 shorter events, 148.1 us)
where the time goes:
time: 1940 us; the launch traced here: 1930 us
  waiting for transfers between devices  1080 us (56%)
  blocking collectives  472 us (24%)
  matrix products  134 us (7%)
  local copies, waits for them, and re-layouts  92.8 us (5%)
  other arithmetic  72.1 us (4%)
  starting transfers between devices  54.4 us (3%)
    reduce_scatter x2, waiting for transfers between devices, scatter_cols(): lax.psum_scatter(part_one, 'col', scatter_dimension=0, tiled=True)  315 us
    unnamed x5, blocking collectives  312 us
    reduce_scatter x2, waiting for transfers between devices, scatter_heads(): lax.psum_scatter(part_one, 'col', scatter_dimension=1, tiled=True)  193 us
    unnamed x42, waiting for transfers between devices  113 us
    all_gather x2, waiting for transfers between devices, gather_heads(): lax.all_gather(part_one, 'col', axis=1, tiled=True)  110 us
    all_gather x2, waiting for transfers between devices, gather_cols(): lax.all_gather(part_two, 'col', axis=0, tiled=True)  66.9 us
    unnamed x245, local copies, waits for them, and re-layouts  66.7 us
    psum x4, blocking collectives, feature_totals(): return lax.psum((part_one, part_two, part_three, part_four), 'col')  55.2 us
  transfers between devices with their start and end apart: 37, of which 28 were waited for; matrix products, arithmetic and copies ran while one was open for 26% of the time, Pallas kernels for 0%

commit v1 on v0

v1 whole, which is shorter than its diff:
```python
import jax
import jax.numpy as jnp
from jax import lax
from jax.sharding import PartitionSpec as P

EPS = 1e-06
GELU_C = 0.7978845608028654
GELU_K = 0.044715
BF = jnp.bfloat16
F32 = jnp.float32
PLANE = ("dp", "col")
IMAGE, TEXT = 0, 1


def gelu_parts(hidden):
    tangent = jnp.tanh(GELU_C * (hidden + GELU_K * hidden * hidden * hidden))
    gelu_value = 0.5 * hidden * (1.0 + tangent)
    gelu_slope = 0.5 * (1.0 + tangent) + 0.5 * hidden * (1.0 - tangent * tangent) * GELU_C * (
        1.0 + 3.0 * GELU_K * hidden * hidden
    )
    return (gelu_value, gelu_slope)


def product(left_side, right_side):
    return jnp.dot(left_side, right_side, preferred_element_type=F32)


def transposed_left(left_side, right_side):
    return lax.dot_general(
        left_side, right_side, (((0,), (0,)), ((), ())), preferred_element_type=F32
    )


def transposed_right(left_side, right_side):
    return lax.dot_general(
        left_side, right_side, (((1,), (1,)), ((), ())), preferred_element_type=F32
    )


class Grid:
    def __init__(self):
        self.dps = lax.axis_size("dp")
        self.cols = lax.axis_size("col")
        self.dp = lax.axis_index("dp")
        self.row = lax.axis_index("row")
        self.col = lax.axis_index("col")

    def hop(self, dp, block):
        mixed = (dp % self.cols) ^ block
        return (mixed % 2) * 2 + mixed // 2

    def along_plane(self, target):
        pairs = []
        for dp in range(self.dps):
            for col in range(self.cols):
                to_dp, to_col = target(dp, col)
                pairs.append((dp * self.cols + col, to_dp * self.cols + to_col % self.cols))
        return pairs

    def spread(self, values, block):
        return lax.ppermute(
            values, PLANE, self.along_plane(lambda d, c: (d, c + self.hop(d, block)))
        )

    def bring_back(self, values, block):
        return lax.ppermute(
            values, PLANE, self.along_plane(lambda d, c: (d, c - self.hop(d, block)))
        )

    def swap_dp(self, values, bit):
        return lax.ppermute(values, "dp", [(d, d ^ bit) for d in range(self.dps)])

    def swap_row(self, values):
        return lax.ppermute(values, "row", [(0, 1), (1, 0)])

    def col_others(self, values):
        return [
            lax.ppermute(
                values, "col", [(i, (i + shift) % self.cols) for i in range(self.cols)]
            )
            for shift in range(1, self.cols)
        ]

    def gather(self, values):
        blocks = [self.spread(values, block) for block in range(self.cols)]
        return (
            jnp.concatenate([blocks[0], blocks[2]], axis=1),
            jnp.concatenate([blocks[1], blocks[3]], axis=1),
        )

    def scatter(self, even, odd):
        width = even.shape[1] // 2
        blocks = [even[:, :width], odd[:, :width], even[:, width:], odd[:, width:]]
        total = None
        for block in range(self.cols):
            part = self.bring_back(blocks[block], block).astype(F32)
            total = part if total is None else total + part
        return total

    def fetch(self, shard, axis):
        width = shard.shape[axis] // self.cols
        index = (self.col + self.hop(self.dp, 0)) % self.cols
        piece = lax.dynamic_slice_in_dim(shard, index * width, width, axis)
        return self.spread(piece, 0)

    def fetch_pair(self, mine, axis, by_row):
        other = self.swap_row(mine) if by_row else self.swap_dp(mine, 2)
        return jnp.concatenate([mine, other], axis=axis if by_row else 1 - axis)

    def fold(self, total, axis, by_row):
        cut = axis if by_row else 1 - axis
        half = total.shape[cut] // 2
        keep = lax.slice_in_dim(total, 0, half, axis=cut)
        send = lax.slice_in_dim(total, half, 2 * half, axis=cut).astype(BF)
        other = self.swap_row(send) if by_row else self.swap_dp(send, 2)
        return keep.astype(F32) + other.astype(F32)

    def fold_rest(self, total):
        bit = self.dps // 2
        while bit >= self.cols:
            half = total.shape[0] // 2
            upper = (self.dp // bit) % 2
            keep = lax.dynamic_slice_in_dim(total, upper * half, half, 0)
            send = lax.dynamic_slice_in_dim(total, (1 - upper) * half, half, 0).astype(BF)
            total = keep + self.swap_dp(send, bit).astype(F32)
            bit //= 2
        return total.astype(BF)

    def place_rows(self, part):
        share = self.dps // self.cols
        moved = lax.ppermute(
            part,
            PLANE,
            self.along_plane(
                lambda d, c: (c * share + d // self.cols, c - self.hop(d, 0))
            ),
        )
        return moved.astype(F32)[None]

    def place_cols(self, part):
        count = part.shape[0] // self.cols
        low = self.dp % self.cols
        pieces, places = [], []
        for flip in range(self.cols):
            piece = lax.dynamic_slice_in_dim(part, (low ^ flip) * count, count, 0)
            pieces.append(
                lax.ppermute(
                    piece,
                    PLANE,
                    self.along_plane(lambda d, c: (d ^ flip, c - self.hop(d, 0))),
                )
            )
            places.append((self.col + self.hop(low ^ flip, 0)) % self.cols)
        columns = []
        for place in range(self.cols):
            chosen = pieces[0]
            for flip in range(1, self.cols):
                chosen = jnp.where(places[flip] == place, pieces[flip], chosen)
            columns.append(chosen.astype(F32))
        return jnp.concatenate(columns, axis=1)[None]


def after(values, *earlier):
    return lax.optimization_barrier((values, *earlier))[0]


def norm_forward(grid, values):
    width = values.shape[1]
    own_mean = jnp.mean(values, axis=1)
    centred = values - own_mean[:, None]
    packed = jnp.stack([own_mean, jnp.sum(centred * centred, axis=1)])
    everyone = [packed] + grid.col_others(packed)
    mean = sum(item[0] for item in everyone) / grid.cols
    squares = sum(item[1] + width * (item[0] - mean) ** 2 for item in everyone)
    inv_std = lax.rsqrt(squares / (width * grid.cols) + EPS)
    return ((values - mean[:, None]) * inv_std[:, None], inv_std[:, None])


def norm_backward(grid, grad_hat, normed, inv_std):
    full_width = grad_hat.shape[1] * grid.cols
    packed = jnp.stack([jnp.sum(grad_hat, axis=1), jnp.sum(grad_hat * normed, axis=1)])
    total = (packed + sum(grid.col_others(packed))) / full_width
    return inv_std * (grad_hat - total[0][:, None] - normed * total[1][:, None])


def attend(packed):
    queries = packed[:, :, 0]
    key_rows = packed[:, :, 1]
    value_rows = packed[:, :, 2]
    score_scale = packed.shape[-1] ** (-0.5)
    scores = jnp.einsum("qhd,khd->hqk", queries, key_rows, preferred_element_type=F32) * score_scale
    log_total = jnp.log(jnp.sum(jnp.exp(scores), axis=-1))
    attn_probs = jnp.exp(scores - log_total[..., None]).astype(BF)
    attended = jnp.einsum("hqk,khd->qhd", attn_probs, value_rows, preferred_element_type=F32)
    return (attended.astype(BF), log_total)


def attend_back(packed, attended, log_total, d_attended):
    queries = packed[:, :, 0]
    key_rows = packed[:, :, 1]
    value_rows = packed[:, :, 2]
    score_scale = packed.shape[-1] ** (-0.5)
    scores = jnp.einsum("qhd,khd->hqk", queries, key_rows, preferred_element_type=F32) * score_scale
    soft_weights = jnp.exp(scores - log_total[..., None])
    row_delta = jnp.transpose(jnp.sum(d_attended.astype(F32) * attended.astype(F32), axis=-1))
    d_values = jnp.einsum(
        "hqk,qhd->khd", soft_weights.astype(BF), d_attended, preferred_element_type=F32
    )
    d_probs = jnp.einsum("qhd,khd->hqk", d_attended, value_rows, preferred_element_type=F32)
    d_scores = (soft_weights * (d_probs - row_delta[..., None]) * score_scale).astype(BF)
    d_queries = jnp.einsum("hqk,khd->qhd", d_scores, key_rows, preferred_element_type=F32)
    d_keys = jnp.einsum("hqk,qhd->khd", d_scores, queries, preferred_element_type=F32)
    return jnp.stack([d_queries, d_keys, d_values], axis=2).astype(BF)


def shards(
    image_in,
    text_in,
    condition,
    image_mod_weight,
    image_mod_bias,
    image_qkv_weight,
    image_qv_bias,
    image_out_weight,
    image_out_bias,
    image_up_weight,
    image_up_bias,
    image_down_weight,
    image_down_bias,
    text_mod_weight,
    text_mod_bias,
    text_qkv_weight,
    text_qv_bias,
    text_out_weight,
    text_out_bias,
    text_up_weight,
    text_up_bias,
    text_down_weight,
    text_down_bias,
    image_cotangent,
    text_cotangent,
):
    grid = Grid()
    streams = (IMAGE, TEXT)
    seq_count = condition.shape[0]
    col_width = image_in.shape[1]
    lengths = (image_in.shape[0], text_in.shape[0])
    heads = image_qv_bias.shape[0]
    head_size = image_qv_bias.shape[2]
    mod_weights = (image_mod_weight, text_mod_weight)
    mod_rows = image_mod_weight.shape[0]

    def join(parts):
        return jnp.concatenate(parts, axis=0)

    def rows_of(values):
        return (values[: lengths[0]], values[lengths[0] :])

    by_row_first = (True, False)

    def fetch(weights, axis):
        return [grid.fetch(weight, axis) for weight in weights]

    def fetch_first(parts, axis):
        return [grid.fetch_pair(parts[s], axis, by_row_first[s]) for s in streams]

    def fetch_last(parts, axis):
        evens = [grid.fetch_pair(parts[s], axis, not by_row_first[s]) for s in streams]
        return [(even, grid.swap_dp(even, 1)) for even in evens]

    def all_after(parts, *earlier):
        return [after(part, *earlier) for part in parts]

    def fold_core(grads):
        return [even.astype(F32) + grid.swap_dp(odd, 1).astype(F32) for even, odd in grads]

    def fold_first(totals, axis):
        return [grid.fold(totals[s], axis, by_row_first[s]) for s in streams]

    def fold_last(totals, axis):
        return [
            grid.fold_rest(grid.fold(totals[s], axis, not by_row_first[s])) for s in streams
        ]

    qkv_mine = fetch((image_qkv_weight, text_qkv_weight), 1)
    qkv_w = fetch_last(fetch_first(qkv_mine, 1), 1)

    act_cond = (condition * jax.nn.sigmoid(condition)).astype(BF)
    partial_mod = jnp.stack(
        [
            jnp.stack([product(act_cond, weight[:, j]) for j in range(6)], axis=1)
            for weight in mod_weights
        ],
        axis=1,
    )
    own_mod = lax.dynamic_index_in_dim(partial_mod, grid.row, 0, False)
    other_mod = lax.dynamic_index_in_dim(partial_mod, 1 - grid.row, 0, False)
    modulation = own_mod + grid.swap_row(other_mod) + jnp.stack([image_mod_bias, text_mod_bias])

    def field(position):
        return join(
            [
                jnp.broadcast_to(modulation[s, position], (lengths[s], col_width))
                for s in streams
            ]
        )

    def token_sums(values):
        return jnp.stack([jnp.sum(part, axis=0) for part in rows_of(values)])

    own_bias = jnp.stack([image_qv_bias, text_qv_bias])
    qv_bias = jnp.concatenate([own_bias, grid.swap_row(own_bias)], axis=1)
    bias_rows = jnp.stack(
        [qv_bias[:, :, 0], jnp.zeros(qv_bias[:, :, 0].shape, F32), qv_bias[:, :, 1]], axis=2
    ).reshape(2, -1)
    up_count = image_up_bias.shape[0] // grid.cols
    own_up = lax.dynamic_slice_in_dim(
        jnp.stack([image_up_bias, text_up_bias]), grid.col * up_count, up_count, 1
    )
    up_bias = jnp.concatenate([own_up, grid.swap_row(own_up)], axis=1)
    out_bias = (image_out_bias, text_out_bias)
    down_bias = (image_down_bias, text_down_bias)

    def with_bias(values, bias):
        return join([part + bias[s][None, :] for s, part in enumerate(rows_of(values))])

    def forward(gathered, weight):
        even, odd = (rows_of(part) for part in gathered)
        return [
            product(even[s], weight[s][0]) + product(odd[s], weight[s][1]) for s in streams
        ]

    def partials(inputs, weight):
        return tuple(
            join([product(inputs[s], weight[s][half]).astype(BF) for s in streams])
            for half in range(2)
        )

    def forward_back(gathered, weight):
        even, odd = (rows_of(part) for part in gathered)
        return [
            transposed_right(even[s], weight[s][0]) + transposed_right(odd[s], weight[s][1])
            for s in streams
        ]

    def partials_back(inputs, weight):
        return tuple(
            join([transposed_right(inputs[s], weight[s][half]).astype(BF) for s in streams])
            for half in range(2)
        )

    def tokens_by_features(gathered, grads):
        even, odd = (rows_of(part) for part in gathered)
        return [
            tuple(transposed_left(part[s], grads[s]).astype(BF) for part in (even, odd))
            for s in streams
        ]

    def features_by_tokens(inputs, gathered):
        even, odd = (rows_of(part) for part in gathered)
        return [
            tuple(transposed_left(inputs[s], part[s]).astype(BF) for part in (even, odd))
            for s in streams
        ]

    values = join([image_in, text_in]).astype(F32)
    xhat1, inv1 = norm_forward(grid, values)
    scale1 = 1.0 + field(1)
    normed1_own = (xhat1 * scale1 + field(0)).astype(BF)
    out_mine = fetch(all_after((image_out_weight, text_out_weight), normed1_own), 0)
    normed1 = grid.gather(normed1_own)
    up_mine = fetch(all_after((image_up_weight, text_up_weight), *normed1), 1)
    out_w = fetch_last(fetch_first(all_after(out_mine, *normed1), 0), 0)
    qkv_sum = forward(normed1, qkv_w)
    packed = join([(qkv_sum[s] + bias_rows[s][None, :]).astype(BF) for s in streams])
    down_mine = fetch(all_after((image_down_weight, text_down_weight), packed), 0)
    up_pair = fetch_first(all_after(up_mine, packed), 1)
    packed = packed.reshape(-1, 2 * heads, 3, head_size)
    attended, log_total = attend(packed)
    attn = rows_of(attended.reshape(attended.shape[0], -1))
    attn_out = partials(attn, out_w)
    branch1 = with_bias(grid.scatter(*attn_out), out_bias)
    up_w = fetch_last(all_after(up_pair, *attn_out), 1)

    gate1 = field(2)
    middle = values + gate1 * branch1
    down_pair = fetch_first(all_after(down_mine, middle), 0)
    xhat2, inv2 = norm_forward(grid, middle)
    scale2 = 1.0 + field(4)
    gate2 = field(5)
    normed2_own = (xhat2 * scale2 + field(3)).astype(BF)
    normed2 = grid.gather(normed2_own)
    grad_out = join([image_cotangent, text_cotangent]).astype(F32)
    d_branch2_own = (grad_out * gate2).astype(BF)
    d_branch2 = grid.gather(after(d_branch2_own, middle))
    down_w = fetch_last(all_after(down_pair, normed2_own), 0)
    hidden = forward(normed2, up_w)
    gelu_both = [gelu_parts(hidden[s] + up_bias[s][None, :]) for s in streams]
    gelu = [gelu_both[s][0].astype(BF) for s in streams]

    d_gelu = forward_back(d_branch2, down_w)
    d_hidden = [(d_gelu[s] * gelu_both[s][1]).astype(BF) for s in streams]
    hidden_back = partials_back(d_hidden, up_w)
    down_grad = features_by_tokens(all_after(gelu, *hidden_back), d_branch2)
    up_grad = tokens_by_features(normed2, all_after(d_hidden, *hidden_back))
    d_normed2 = grid.scatter(*hidden_back)
    down_fold = fold_first(fold_core(down_grad), 0)
    up_fold = fold_first(fold_core(up_grad), 1)
    gelu_down = partials(all_after(gelu, d_normed2), down_w)
    branch2 = with_bias(grid.scatter(*gelu_down), down_bias)
    outputs = rows_of((middle + gate2 * branch2).astype(BF))
    d_gate2 = token_sums(grad_out * branch2)
    d_shift2 = token_sums(d_normed2)
    d_scale2 = token_sums(d_normed2 * xhat2)
    d_middle = grad_out + norm_backward(grid, d_normed2 * scale2, xhat2, inv2)

    d_gate1 = token_sums(d_middle * branch1)
    d_branch1_own = (d_middle * gate1).astype(BF)
    d_branch1 = grid.gather(d_branch1_own)
    down_fold = fold_last(all_after(down_fold, d_branch1_own), 0)
    up_fold = fold_last(all_after(up_fold, d_branch1_own), 1)
    d_attn = join([part.astype(BF) for part in forward_back(d_branch1, out_w)])
    down_total = [grid.place_rows(part) for part in all_after(down_fold, d_attn)]
    up_total = [grid.place_cols(part) for part in all_after(up_fold, d_attn)]
    d_packed = attend_back(packed, attended, log_total, d_attn.reshape(attended.shape))
    d_qkv = rows_of(d_packed.reshape(d_packed.shape[0], -1))
    qkv_back = partials_back(d_qkv, qkv_w)
    d_normed1 = grid.scatter(*qkv_back)
    qkv_grad = tokens_by_features(normed1, all_after(d_qkv, *qkv_back))
    qkv_fold = fold_last(fold_first(fold_core(qkv_grad), 1), 1)
    out_grad = features_by_tokens(all_after(attn, *qkv_back), d_branch1)
    out_fold = fold_last(fold_first(fold_core(out_grad), 0), 0)
    d_shift1 = token_sums(d_normed1)
    d_scale1 = token_sums(d_normed1 * xhat1)
    in_grads = rows_of(d_middle + norm_backward(grid, d_normed1 * scale1, xhat1, inv1))
    qkv_total = [grid.place_cols(part) for part in qkv_fold]
    out_total = [grid.place_rows(part) for part in out_fold]

    up_sums = jnp.stack([jnp.sum(d_hidden[s].astype(F32), axis=0) for s in streams])
    head_sums = jnp.stack([jnp.sum(d_qkv[s].astype(F32), axis=0) for s in streams])
    head_sums = head_sums.reshape(2, 2, heads, 3, head_size)
    head_sums = jnp.stack([head_sums[:, :, :, 0], head_sums[:, :, :, 2]], axis=3)
    vectors = jnp.concatenate(
        [
            jnp.stack([d_shift1, d_scale1, d_gate1, d_shift2, d_scale2, d_gate2], axis=1),
            token_sums(d_branch1_own.astype(F32))[:, None],
            token_sums(d_branch2_own.astype(F32))[:, None],
            head_sums.reshape(2, -1, col_width),
            up_sums.reshape(2, -1, col_width),
        ],
        axis=1,
    ).astype(BF)
    everyone = lax.all_gather(vectors, ("dp", "row"), axis=0, tiled=False)
    vector_sums = jnp.sum(everyone.astype(F32), axis=0)
    feature_share = col_width // grid.dps
    shares = lax.dynamic_slice_in_dim(vector_sums, grid.dp * feature_share, feature_share, 2)

    def over_rows(rows, shape):
        parts = jnp.sum(rows.astype(F32).reshape(grid.dps, 2, 2, 2, *shape), axis=0)
        return jnp.where(
            grid.row == 0, parts[0, :, 0] + parts[1, :, 1], parts[1, :, 0] + parts[0, :, 1]
        )

    head_rows = 2 * heads * 2 * head_size // col_width
    head_total = over_rows(everyone[:, :, 8 : 8 + head_rows], (heads, 2, head_size))
    up_total_own = over_rows(everyone[:, :, 8 + head_rows :], (up_count,))
    head_share = head_size // grid.dps
    head_total = lax.dynamic_slice_in_dim(head_total, grid.dp * head_share, head_share, 3)
    qv_b_grad = jnp.transpose(head_total, (0, 3, 1, 2))

    d_mod = everyone[:, :, :6]
    mod_share = mod_rows // grid.dps
    act_all = lax.all_gather(act_cond, "dp", axis=0, tiled=True)
    act_share = lax.dynamic_slice_in_dim(act_all, grid.dp * mod_share, mod_share, 1)
    mod_w_grad = [
        jnp.stack([transposed_left(act_share, d_mod[:, s, j]) for j in range(6)], axis=1)[None]
        for s in streams
    ]
    own_d_mod = lax.dynamic_slice_in_dim(d_mod, grid.dp * seq_count, seq_count, 0)
    cond_part = sum(
        transposed_right(own_d_mod[:, s, j], mod_weights[s][:, j])
        for s in streams
        for j in range(6)
    )
    last = jnp.stack([cond_part, up_total_own])
    lasts = [last] + grid.col_others(last)
    cond_sum = sum(item[0] for item in lasts)
    up_share = up_count * grid.cols // grid.dps
    up_from = (grid.col - grid.dp * grid.cols // grid.dps) % grid.cols
    up_chosen = sum(jnp.where(up_from == j, lasts[j][1], 0.0) for j in range(grid.cols))
    up_start = (grid.dp % (grid.dps // grid.cols)) * up_share
    up_b_grad = lax.dynamic_slice_in_dim(up_chosen, up_start, up_share, 1)
    sigmoid_cond = jax.nn.sigmoid(condition)
    condition_grad = cond_sum * sigmoid_cond * (1.0 + condition * (1.0 - sigmoid_cond))

    grads = []
    for s in streams:
        grads += [
            mod_w_grad[s],
            jnp.transpose(shares[s, :6])[None],
            qkv_total[s],
            qv_b_grad[s],
            out_total[s],
            shares[s, 6][None],
            up_total[s],
            up_b_grad[s][None],
            down_total[s],
            shares[s, 7][None],
        ]
    return (*outputs, *in_grads, condition_grad, *grads)


def solution(mesh):
    in_specs = (
        P(("dp", "row"), "col"),
        P(("dp", "row"), "col"),
        P("dp", "row"),
        P("row", None, "col"),
        P(None, "col"),
        P("col", "row"),
        P(("row", "col"), None, None),
        P("row", "col"),
        P("col"),
        P("col", "row"),
        P("row"),
        P("row", "col"),
        P("col"),
        P("row", None, "col"),
        P(None, "col"),
        P("col", "row"),
        P(("row", "col"), None, None),
        P("row", "col"),
        P("col"),
        P("col", "row"),
        P("row"),
        P("row", "col"),
        P("col"),
        P(("dp", "row"), "col"),
        P(("dp", "row"), "col"),
    )
    out_specs = (
        P(("dp", "row"), "col"),
        P(("dp", "row"), "col"),
        P(("dp", "row"), "col"),
        P(("dp", "row"), "col"),
        P("dp", "row"),
        P("row", "dp", None, "col"),
        P("col", "dp", None),
        P("col", "dp", "row"),
        P("dp", ("row", "col"), None),
        P("row", "dp", "col"),
        P("col", "dp"),
        P("col", "dp", "row"),
        P("row", "dp"),
        P("row", "dp", "col"),
        P("col", "dp"),
        P("row", "dp", None, "col"),
        P("col", "dp", None),
        P("col", "dp", "row"),
        P("dp", ("row", "col"), None),
        P("row", "dp", "col"),
        P("col", "dp"),
        P("col", "dp", "row"),
        P("row", "dp"),
        P("row", "dp", "col"),
        P("col", "dp"),
    )
    return jax.shard_map(shards, mesh=mesh, in_specs=in_specs, out_specs=out_specs, check_vma=False)
```

time: 1940 us -> 897 us (0.46)
  the two profiles are of different devices: /device:TPU:0 before, /device:TPU:3 now
where the time goes in v1:
time: 897 us; the launch traced here: 887 us
  waiting for transfers between devices  320 us (36%)
  starting transfers between devices  290 us (32%)
  matrix products  119 us (13%)
  other arithmetic  69.1 us (8%)
  local copies, waits for them, and re-layouts  60.9 us (7%)
  blocking collectives  23.5 us (3%)
    ppermute x24, starting transfers between devices, spread(): lax.ppermute(values, PLANE, self.along_plane(lambda d, c: (d, c + self.ho...  85.3 us
    ppermute x24, waiting for transfers between devices, spread(): lax.ppermute(values, PLANE, self.along_plane(lambda d, c: (d, c + self.ho...  81.5 us
    ppermute x16, waiting for transfers between devices, bring_back(): lax.ppermute(values, PLANE, self.along_plane(lambda d, c: (d, c - self.ho...  77.5 us
    ppermute x32, starting transfers between devices, swap_dp(): return lax.ppermute(values, 'dp', [(d, d ^ bit) for d in range(self.dps)])  56.7 us
    ppermute x16, starting transfers between devices, bring_back(): lax.ppermute(values, PLANE, self.along_plane(lambda d, c: (d, c - self.ho...  50.9 us
    ppermute x19, waiting for transfers between devices, swap_row(): return lax.ppermute(values, 'row', [(0, 1), (1, 0)])  50.1 us
    ppermute x32, waiting for transfers between devices, swap_dp(): return lax.ppermute(values, 'dp', [(d, d ^ bit) for d in range(self.dps)])  50 us
    dot_general x28, matrix products, transposed_left(): lax.dot_general(left_side, right_side, (((0,), (0,)), ((), ())), preferre...  42.5 us
  transfers between devices with their start and end apart: 126, of which 45 were waited for; matrix products, arithmetic and copies ran while one was open for 24% of the time, Pallas kernels for 0%

profile of v1, /device:TPU:3, one launch (start us, length us, event | category | flops | bytes accessed | tf_op | source)
XLA Modules:
  0.0 886.5 jit_solution(12103465464532888816)
XLA Ops:
  39.3 13.2 %collective-permute-done.13 = bf16[384,576]{0,1:T(8,128)(2,1)S(1)} collective-permute-done((bf16[384,576]{0,1:T(8,128)(2,1)}, bf16[384,576]{0,1:T(8,128)(2,1)S(1)}, u32[]{:S(2)}, u32[]{:S(2)}) %collective-permute-start.13) | collective-permute-done | bytes 442400 | tf_op jit(solution)/shard_map/ppermute | solution.py:61
  98.6 15.9 %collective-permute-start.17 = (bf16[192,384]{1,0:T(8,128)(2,1)S(1)}, bf16[192,384]{1,0:T(8,128)(2,1)S(1)}, u32[]{:S(2)}, u32[]{:S(2)}) collective-permute-start(bf16[192,384]{1,0:T(8,128)(2,1)S(1)} %constant_dynamic-slice_fusion.41), channel_id=1, source_target_pairs={{0,0},{1,1},{2,2},{3,3},{8,10},{9,11},{10,8},{11,9},{16,17},{17,18... | collective-permute-start | bytes 442376 | tf_op jit(solution)/shard_map/ppermute | solution.py:61
  116.2 12.1 %collective-permute-start.21 = (bf16[192,384]{1,0:T(8,128)(2,1)S(1)}, bf16[192,384]{1,0:T(8,128)(2,1)S(1)}, u32[]{:S(2)}, u32[]{:S(2)}) collective-permute-start(bf16[192,384]{1,0:T(8,128)(2,1)S(1)} %collective-permute-done.20), channel_id=1, source_target_pairs={{0,16},{8,24},{16,0},{24,8},{1,17},{9,25},{17,1},{25,9},{2,18},{10... | collective-permute-start | bytes 442376 | tf_op jit(solution)/shard_map/ppermute | solution.py:71
  182.7 9.9 %collective-permute-done.28 = bf16[602,384]{1,0:T(8,128)(2,1)S(1)} collective-permute-done((bf16[602,384]{1,0:T(8,128)(2,1)S(1)}, bf16[602,384]{1,0:T(8,128)(2,1)S(1)}, u32[]{:S(2)}, u32[]{:S(2)}) %collective-permute-start.28) | collective-permute-done | bytes 462368 | tf_op jit(solution)/shard_map/ppermute | solution.py:66
  194.5 11.2 %collective-permute-start.54 = (bf16[384,768]{1,0:T(8,128)(2,1)}, bf16[384,768]{1,0:T(8,128)(2,1)S(1)}, u32[]{:S(2)}, u32[]{:S(2)}) collective-permute-start(bf16[384,768]{1,0:T(8,128)(2,1)} %collective-permute-done.53), channel_id=1, source_target_pairs={{0,16},{8,24},{16,0},{24,8},{1,17},{9,25},{17,1},{25,9},{2,18},{10... | collective-permute-start | bytes 1769480 | tf_op jit(solution)/shard_map/ppermute | solution.py:71
  205.7 10.3 %collective-permute-done.23 = bf16[602,384]{1,0:T(8,128)(2,1)S(1)} collective-permute-done((bf16[602,384]{1,0:T(8,128)(2,1)S(1)}, bf16[602,384]{1,0:T(8,128)(2,1)S(1)}, u32[]{:S(2)}, u32[]{:S(2)}) %collective-permute-start.23) | collective-permute-done | bytes 462368 | tf_op jit(solution)/shard_map/ppermute | solution.py:66
  229.6 11.4 %collective-permute-done.30 = f32[2,602]{1,0:T(2,128)S(1)} collective-permute-done((f32[2,602]{1,0:T(2,128)S(1)}, f32[2,602]{1,0:T(2,128)S(1)}, u32[]{:S(2)}, u32[]{:S(2)}) %collective-permute-start.30) | collective-permute-done | bytes 4848 | tf_op jit(solution)/shard_map/ppermute | solution.py:78
  251.1 22.3 %collective-permute-done.55 = bf16[768,768]{1,0:T(8,128)(2,1)S(1)} collective-permute-done((bf16[768,768]{1,0:T(8,128)(2,1)S(1)}, bf16[768,768]{1,0:T(8,128)(2,1)S(1)}, u32[]{:S(2)}, u32[]{:S(2)}) %collective-permute-start.55) | collective-permute-done | bytes 1179680 | tf_op jit(solution)/shard_map/ppermute | solution.py:74
  302.1 9.1 %collective-permute-done.38 = bf16[602,384]{1,0:T(8,128)(2,1)S(1)} collective-permute-done((bf16[602,384]{1,0:T(8,128)(2,1)S(1)}, bf16[602,384]{1,0:T(8,128)(2,1)S(1)}, u32[]{:S(2)}, u32[]{:S(2)}) %collective-permute-start.38) | collective-permute-done | bytes 462368 | tf_op jit(solution)/shard_map/ppermute | solution.py:61
  311.2 10.7 %collective-permute-start.32 = (bf16[602,384]{1,0:T(8,128)(2,1)S(1)}, bf16[602,384]{1,0:T(8,128)(2,1)S(1)}, u32[]{:S(2)}, u32[]{:S(2)}) collective-permute-start(bf16[602,384]{1,0:T(8,128)(2,1)S(1)} %fusion.103), channel_id=1, source_target_pairs={{0,0},{1,1},{2,2},{3,3},{8,10},{9,11},{10,8},{11,9},{16,17},{17,18... | collective-permute-start | bytes 1387016 | tf_op jit(solution)/shard_map/ppermute | solution.py:61
  324.4 13.6 %collective-permute-done.32 = bf16[602,384]{1,0:T(8,128)(2,1)S(1)} collective-permute-done((bf16[602,384]{1,0:T(8,128)(2,1)S(1)}, bf16[602,384]{1,0:T(8,128)(2,1)S(1)}, u32[]{:S(2)}, u32[]{:S(2)}) %collective-permute-start.32) | collective-permute-done | bytes 462368 | tf_op jit(solution)/shard_map/ppermute | solution.py:61
  402.0 12.7 %collective-permute-done.57 = bf16[602,384]{1,0:T(8,128)(2,1)} collective-permute-done((bf16[602,384]{1,0:T(8,128)(2,1)}, bf16[602,384]{1,0:T(8,128)(2,1)}, u32[]{:S(2)}, u32[]{:S(2)}) %collective-permute-start.57) | collective-permute-done | bytes 462368 | tf_op jit(solution)/shard_map/ppermute | solution.py:66
  435.7 10.0 %collective-permute-done.63 = bf16[602,384]{1,0:T(8,128)(2,1)S(1)} collective-permute-done((bf16[602,384]{1,0:T(8,128)(2,1)S(1)}, bf16[602,384]{1,0:T(8,128)(2,1)S(1)}, u32[]{:S(2)}, u32[]{:S(2)}) %collective-permute-start.63) | collective-permute-done | bytes 462368 | tf_op jit(solution)/shard_map/ppermute | solution.py:66
  445.7 16.6 %collective-permute-done.61 = bf16[602,384]{1,0:T(8,128)(2,1)S(1)} collective-permute-done((bf16[602,384]{1,0:T(8,128)(2,1)S(1)}, bf16[602,384]{1,0:T(8,128)(2,1)S(1)}, u32[]{:S(2)}, u32[]{:S(2)}) %collective-permute-start.61) | collective-permute-done | bytes 462368 | tf_op jit(solution)/shard_map/ppermute | solution.py:66
  487.9 25.9 %collective-permute-done.68 = bf16[602,384]{1,0:T(8,128)(2,1)S(1)} collective-permute-done((bf16[602,384]{1,0:T(8,128)(2,1)S(1)}, bf16[602,384]{1,0:T(8,128)(2,1)S(1)}, u32[]{:S(2)}, u32[]{:S(2)}) %collective-permute-start.68) | collective-permute-done | bytes 462368 | tf_op jit(solution)/shard_map/ppermute | solution.py:61
  545.7 10.3 %collective-permute-start.75 = (bf16[602,384]{1,0:T(8,128)(2,1)}, bf16[602,384]{1,0:T(8,128)(2,1)}, u32[]{:S(2)}, u32[]{:S(2)}) collective-permute-start(bf16[602,384]{1,0:T(8,128)(2,1)} %get-tuple-element.201), channel_id=1, source_target_pairs={{0,1},{1,2},{2,3},{3,0},{8,11},{9,8},{10,9},{11,10},{16,18},{17,19... | collective-permute-start | bytes 1387016 | tf_op jit(solution)/shard_map/ppermute | solution.py:66
  577.8 14.5 %collective-permute-done.72 = bf16[602,384]{1,0:T(8,128)(2,1)} collective-permute-done((bf16[602,384]{1,0:T(8,128)(2,1)}, bf16[602,384]{1,0:T(8,128)(2,1)}, u32[]{:S(2)}, u32[]{:S(2)}) %collective-permute-start.72) | collective-permute-done | bytes 462368 | tf_op jit(solution)/shard_map/ppermute | solution.py:66
  609.4 16.5 %all_gather.7 = bf16[8,2,14,384]{3,1,2,0:T(2,128)(2,1)S(1)} all-gather(bf16[1,2,14,384]{3,1,2,0:T(2,128)(2,1)S(1)} %copy.268), channel_id=1, replica_groups=mesh['dp'=4,'row'=2,'col'=4] {'dp','row'}, dimensions={0}, use_global_device_ids=true | all-gather | bytes 193536 | tf_op jit(solution)/shard_map/all_gather | solution.py:453
  717.5 11.7 %collective-permute-done.101 = bf16[768,768]{1,0:T(8,128)(2,1)} collective-permute-done((bf16[768,768]{1,0:T(8,128)(2,1)}, bf16[768,768]{1,0:T(8,128)(2,1)}, u32[]{:S(2)}, u32[]{:S(2)}) %collective-permute-start.101) | collective-permute-done | bytes 1179680 | tf_op jit(solution)/shard_map/ppermute | solution.py:74
  735.7 17.0 %collective-permute-done.123 = bf16[1536,384]{1,0:T(8,128)(2,1)} collective-permute-done((bf16[1536,384]{1,0:T(8,128)(2,1)}, bf16[1536,384]{1,0:T(8,128)(2,1)}, u32[]{:S(2)}, u32[]{:S(2)}) %collective-permute-start.123) | collective-permute-done | bytes 1179680 | tf_op jit(solution)/shard_map/ppermute | solution.py:71
  761.7 9.9 %collective-permute-done.105 = bf16[384,1152]{1,0:T(8,128)(2,1)} collective-permute-done((bf16[384,1152]{1,0:T(8,128)(2,1)}, bf16[384,1152]{1,0:T(8,128)(2,1)}, u32[]{:S(2)}, u32[]{:S(2)}) %collective-permute-start.105) | collective-permute-done | bytes 884768 | tf_op jit(solution)/shard_map/ppermute | solution.py:71
  774.4 9.9 %collective-permute-done.95 = bf16[384,768]{1,0:T(8,128)(2,1)} collective-permute-done((bf16[384,768]{1,0:T(8,128)(2,1)}, bf16[384,768]{1,0:T(8,128)(2,1)}, u32[]{:S(2)}, u32[]{:S(2)}) %collective-permute-start.95) | collective-permute-done | bytes 589856 | tf_op jit(solution)/shard_map/ppermute | solution.py:71
  790.1 9.9 %collective-permute-done.102 = bf16[768,384]{1,0:T(8,128)(2,1)} collective-permute-done((bf16[768,384]{1,0:T(8,128)(2,1)}, bf16[768,384]{1,0:T(8,128)(2,1)}, u32[]{:S(2)}, u32[]{:S(2)}) %collective-permute-start.102) | collective-permute-done | bytes 589856 | tf_op jit(solution)/shard_map/ppermute | solution.py:71
  873.1 11.1 %collective-permute-done.125 = bf16[768,384]{1,0:T(8,128)(2,1)} collective-permute-done((bf16[768,384]{1,0:T(8,128)(2,1)}, bf16[768,384]{1,0:T(8,128)(2,1)}, u32[]{:S(2)}, u32[]{:S(2)}) %collective-permute-start.125) | collective-permute-done | bytes 589856 | tf_op jit(solution)/shard_map/ppermute | solution.py:131
  (890 shorter events, 565.8 us)
Async XLA Ops:
  86.8 61.9 %collective-permute-start.16 = (bf16[768,1152]{0,1:T(8,128)(2,1)S(1)}, bf16[768,1152]{0,1:T(8,128)(2,1)S(1)}, u32[]{:S(2)}, u32[]{:S(2)}) collective-permute-start(bf16[768,1152]{0,1:T(8,128)(2,1)S(1)} %pad_maximum_fusion.1), channel_id=1, source_target_pairs={{0,8},{8,0},{16,24},{24,16},{1,9},{9,1},{17,25},{25,17},{2,10},{10... | collective-permute-start | bytes 5308424 | tf_op jit(solution)/shard_map/ppermute | solution.py:71
  90.3 59.3 %collective-permute-start.11 = (bf16[768,1152]{1,0:T(8,128)(2,1)S(1)}, bf16[768,1152]{1,0:T(8,128)(2,1)S(1)}, u32[]{:S(2)}, u32[]{:S(2)}) collective-permute-start(bf16[768,1152]{1,0:T(8,128)(2,1)S(1)} %pad_maximum_fusion), channel_id=1, source_target_pairs={{0,8},{8,0},{16,24},{24,16},{1,9},{9,1},{17,25},{25,17},{2,10},{10... | collective-permute-start | bytes 5308424 | tf_op jit(solution)/shard_map/ppermute | solution.py:71
  137.0 40.3 %collective-permute-start.34 = (bf16[384,768]{1,0:T(8,128)(2,1)}, bf16[384,768]{1,0:T(8,128)(2,1)}, u32[]{:S(2)}, u32[]{:S(2)}) collective-permute-start(bf16[384,768]{1,0:T(8,128)(2,1)} %constant_dynamic-slice_fusion.39), channel_id=1, source_target_pairs={{0,0},{1,1},{2,2},{3,3},{8,10},{9,11},{10,8},{11,9},{16,17},{17,18... | collective-permute-start | bytes 1769480 | tf_op jit(solution)/shard_map/ppermute | solution.py:61
  177.3 38.7 %collective-permute-start.23 = (bf16[602,384]{1,0:T(8,128)(2,1)S(1)}, bf16[602,384]{1,0:T(8,128)(2,1)S(1)}, u32[]{:S(2)}, u32[]{:S(2)}) collective-permute-start(bf16[602,384]{1,0:T(8,128)(2,1)S(1)} %get-tuple-element.210), channel_id=1, source_target_pairs={{0,0},{1,1},{2,2},{3,3},{8,10},{9,11},{10,8},{11,9},{16,19},{17,16... | collective-permute-start | bytes 1387016 | tf_op jit(solution)/shard_map/ppermute | solution.py:66
  180.3 66.4 %collective-permute-start.35 = (bf16[384,768]{1,0:T(8,128)(2,1)}, bf16[384,768]{1,0:T(8,128)(2,1)S(1)}, u32[]{:S(2)}, u32[]{:S(2)}) collective-permute-start(bf16[384,768]{1,0:T(8,128)(2,1)} %collective-permute-done.34), channel_id=1, source_target_pairs={{0,4},{4,0},{1,5},{5,1},{2,6},{6,2},{3,7},{7,3},{8,12},{12,8},{9,1... | collective-permute-start | bytes 1769480 | tf_op jit(solution)/shard_map/ppermute | solution.py:74
  192.5 55.4 %collective-permute-start.43 = (bf16[768,384]{1,0:T(8,128)(2,1)S(1)}, bf16[768,384]{1,0:T(8,128)(2,1)S(1)}, u32[]{:S(2)}, u32[]{:S(2)}) collective-permute-start(bf16[768,384]{1,0:T(8,128)(2,1)S(1)} %constant_dynamic-slice_fusion.38), channel_id=1, source_target_pairs={{0,0},{1,1},{2,2},{3,3},{8,10},{9,11},{10,8},{11,9},{16,17},{17,18... | collective-permute-start | bytes 1769480 | tf_op jit(solution)/shard_map/ppermute | solution.py:61
  194.5 46.6 %collective-permute-start.54 = (bf16[384,768]{1,0:T(8,128)(2,1)}, bf16[384,768]{1,0:T(8,128)(2,1)S(1)}, u32[]{:S(2)}, u32[]{:S(2)}) collective-permute-start(bf16[384,768]{1,0:T(8,128)(2,1)} %collective-permute-done.53), channel_id=1, source_target_pairs={{0,16},{8,24},{16,0},{24,8},{1,17},{9,25},{17,1},{25,9},{2,18},{10... | collective-permute-start | bytes 1769480 | tf_op jit(solution)/shard_map/ppermute | solution.py:71
  283.9 57.6 %collective-permute-start.56 = (bf16[768,1536]{1,0:T(8,128)(2,1)S(1)}, bf16[768,1536]{1,0:T(8,128)(2,1)S(1)}, u32[]{:S(2)}, u32[]{:S(2)}) collective-permute-start(bf16[768,1536]{1,0:T(8,128)(2,1)S(1)} %constant_dynamic-update-slice_fusion.24), channel_id=1, source_target_pairs={{0,8},{8,0},{16,24},{24,16},{1,9},{9,1},{17,25},{25,17},{2,10},{10... | collective-permute-start | bytes 7077896 | tf_op jit(solution)/shard_map/ppermute | solution.py:71
  291.8 50.2 %collective-permute-start.39 = (bf16[768,1536]{1,0:T(8,128)(2,1)S(1)}, bf16[768,1536]{1,0:T(8,128)(2,1)S(1)}, u32[]{:S(2)}, u32[]{:S(2)}) collective-permute-start(bf16[768,1536]{1,0:T(8,128)(2,1)S(1)} %constant_dynamic-update-slice_fusion.12), channel_id=1, source_target_pairs={{0,8},{8,0},{16,24},{24,16},{1,9},{9,1},{17,25},{25,17},{2,10},{10... | collective-permute-start | bytes 7077896 | tf_op jit(solution)/shard_map/ppermute | solution.py:71
  300.7 40.5 %collective-permute-start.51 = (bf16[768,768]{1,0:T(8,128)(2,1)S(1)}, bf16[768,768]{1,0:T(8,128)(2,1)S(1)}, u32[]{:S(2)}, u32[]{:S(2)}) collective-permute-start(bf16[768,768]{1,0:T(8,128)(2,1)S(1)} %pad_maximum_fusion.12), channel_id=1, source_target_pairs={{0,4},{4,0},{1,5},{5,1},{2,6},{6,2},{3,7},{7,3},{8,12},{12,8},{9,1... | collective-permute-start | bytes 3538952 | tf_op jit(solution)/shard_map/ppermute | solution.py:74
  394.3 272.2 %collective-permute-start.93 = (bf16[768,1536]{1,0:T(8,128)(2,1)}, bf16[768,1536]{1,0:T(8,128)(2,1)}, u32[]{:S(2)}, u32[]{:S(2)}) collective-permute-start(bf16[768,1536]{1,0:T(8,128)(2,1)} %convolution_convert_fusion.10), channel_id=1, source_target_pairs={{0,8},{8,0},{16,24},{24,16},{1,9},{9,1},{17,25},{25,17},{2,10},{10... | collective-permute-start | bytes 7077896 | tf_op jit(solution)/shard_map/ppermute | solution.py:71
  574.7 94.5 %collective-permute-start.100 = (bf16[1536,768]{1,0:T(8,128)(2,1)}, bf16[1536,768]{1,0:T(8,128)(2,1)}, u32[]{:S(2)}, u32[]{:S(2)}) collective-permute-start(bf16[1536,768]{1,0:T(8,128)(2,1)} %convolution_convert_fusion.8), channel_id=1, source_target_pairs={{0,8},{8,0},{16,24},{24,16},{1,9},{9,1},{17,25},{25,17},{2,10},{10... | collective-permute-start | bytes 7077896 | tf_op jit(solution)/shard_map/ppermute | solution.py:71
  604.1 50.4 %collective-permute-start.89 = (bf16[384,768]{1,0:T(8,128)(2,1)}, bf16[384,768]{1,0:T(8,128)(2,1)}, u32[]{:S(2)}, u32[]{:S(2)}) collective-permute-start(bf16[384,768]{1,0:T(8,128)(2,1)} %convolution_convert_fusion.22), channel_id=1, source_target_pairs={{0,8},{8,0},{16,24},{24,16},{1,9},{9,1},{17,25},{25,17},{2,10},{10... | collective-permute-start | bytes 1769480 | tf_op jit(solution)/shard_map/ppermute | solution.py:71
  666.6 42.4 %collective-permute-start.104 = (bf16[768,1152]{1,0:T(8,128)(2,1)}, bf16[768,1152]{1,0:T(8,128)(2,1)}, u32[]{:S(2)}, u32[]{:S(2)}) collective-permute-start(bf16[768,1152]{1,0:T(8,128)(2,1)} %convolution_convert_fusion.4), channel_id=1, source_target_pairs={{0,8},{8,0},{16,24},{24,16},{1,9},{9,1},{17,25},{25,17},{2,10},{10... | collective-permute-start | bytes 5308424 | tf_op jit(solution)/shard_map/ppermute | solution.py:71
  683.5 45.6 %collective-permute-start.101 = (bf16[768,768]{1,0:T(8,128)(2,1)}, bf16[768,768]{1,0:T(8,128)(2,1)}, u32[]{:S(2)}, u32[]{:S(2)}) collective-permute-start(bf16[768,768]{1,0:T(8,128)(2,1)} %slice.1437), channel_id=1, source_target_pairs={{0,4},{4,0},{1,5},{5,1},{2,6},{6,2},{3,7},{7,3},{8,12},{12,8},{9,1... | collective-permute-start | bytes 3538952 | tf_op jit(solution)/shard_map/ppermute | solution.py:74
  703.1 49.5 %collective-permute-start.123 = (bf16[1536,384]{1,0:T(8,128)(2,1)}, bf16[1536,384]{1,0:T(8,128)(2,1)}, u32[]{:S(2)}, u32[]{:S(2)}) collective-permute-start(bf16[1536,384]{1,0:T(8,128)(2,1)} %slice.1435), channel_id=1, source_target_pairs={{0,16},{8,24},{16,0},{24,8},{1,17},{9,25},{17,1},{25,9},{2,18},{10... | collective-permute-start | bytes 3538952 | tf_op jit(solution)/shard_map/ppermute | solution.py:71
  709.0 47.2 %collective-permute-start.83 = (bf16[768,576]{0,1:T(8,128)(2,1)}, bf16[768,576]{0,1:T(8,128)(2,1)S(1)}, u32[]{:S(2)}, u32[]{:S(2)}) collective-permute-start(bf16[768,576]{0,1:T(8,128)(2,1)} %copy.281), channel_id=1, source_target_pairs={{0,4},{4,0},{1,5},{5,1},{2,6},{6,2},{3,7},{7,3},{8,12},{12,8},{9,1... | collective-permute-start | bytes 2654216 | tf_op jit(solution)/shard_map/ppermute | solution.py:74
  712.6 59.0 %collective-permute-start.105 = (bf16[384,1152]{1,0:T(8,128)(2,1)}, bf16[384,1152]{1,0:T(8,128)(2,1)}, u32[]{:S(2)}, u32[]{:S(2)}) collective-permute-start(bf16[384,1152]{1,0:T(8,128)(2,1)} %slice.1440), channel_id=1, source_target_pairs={{0,16},{8,24},{16,0},{24,8},{1,17},{9,25},{17,1},{25,9},{2,18},{10... | collective-permute-start | bytes 2654216 | tf_op jit(solution)/shard_map/ppermute | solution.py:71
  729.2 55.1 %collective-permute-start.95 = (bf16[384,768]{1,0:T(8,128)(2,1)}, bf16[384,768]{1,0:T(8,128)(2,1)}, u32[]{:S(2)}, u32[]{:S(2)}) collective-permute-start(bf16[384,768]{1,0:T(8,128)(2,1)} %slice.1444), channel_id=1, source_target_pairs={{0,16},{8,24},{16,0},{24,8},{1,17},{9,25},{17,1},{25,9},{2,18},{10... | collective-permute-start | bytes 1769480 | tf_op jit(solution)/shard_map/ppermute | solution.py:71
  732.5 67.6 %collective-permute-start.102 = (bf16[768,384]{1,0:T(8,128)(2,1)}, bf16[768,384]{1,0:T(8,128)(2,1)}, u32[]{:S(2)}, u32[]{:S(2)}) collective-permute-start(bf16[768,384]{1,0:T(8,128)(2,1)} %slice.1443), channel_id=1, source_target_pairs={{0,16},{8,24},{16,0},{24,8},{1,17},{9,25},{17,1},{25,9},{2,18},{10... | collective-permute-start | bytes 1769480 | tf_op jit(solution)/shard_map/ppermute | solution.py:71
  752.7 50.9 %collective-permute-start.117 = (bf16[384,768]{1,0:T(8,128)(2,1)}, bf16[384,768]{1,0:T(8,128)(2,1)}, u32[]{:S(2)}, u32[]{:S(2)}) collective-permute-start(bf16[384,768]{1,0:T(8,128)(2,1)} %slice.1442), channel_id=1, source_target_pairs={{0,4},{4,0},{1,5},{5,1},{2,6},{6,2},{3,7},{7,3},{8,12},{12,8},{9,1... | collective-permute-start | bytes 1769480 | tf_op jit(solution)/shard_map/ppermute | solution.py:74
  757.1 49.9 %collective-permute-start.124 = (bf16[768,384]{1,0:T(8,128)(2,1)}, bf16[768,384]{1,0:T(8,128)(2,1)}, u32[]{:S(2)}, u32[]{:S(2)}) collective-permute-start(bf16[768,384]{1,0:T(8,128)(2,1)} %slice.1441), channel_id=1, source_target_pairs={{0,4},{4,0},{1,5},{5,1},{2,6},{6,2},{3,7},{7,3},{8,12},{12,8},{9,1... | collective-permute-start | bytes 1769480 | tf_op jit(solution)/shard_map/ppermute | solution.py:74
  771.6 64.0 %collective-permute-start.84 = (bf16[384,576]{1,0:T(8,128)(2,1)S(1)}, bf16[384,576]{1,0:T(8,128)(2,1)S(1)}, u32[]{:S(2)}, u32[]{:S(2)}) collective-permute-start(bf16[384,576]{1,0:T(8,128)(2,1)S(1)} %slice.1446), channel_id=1, source_target_pairs={{0,16},{8,24},{16,0},{24,8},{1,17},{9,25},{17,1},{25,9},{2,18},{10... | collective-permute-start | bytes 1327112 | tf_op jit(solution)/shard_map/ppermute | solution.py:71
  828.8 43.2 %collective-permute-start.103 = (bf16[768,384]{1,0:T(8,128)(2,1)}, bf16[768,384]{1,0:T(8,128)(2,1)S(1)}, u32[]{:S(2)}, u32[]{:S(2)}) collective-permute-start(bf16[768,384]{1,0:T(8,128)(2,1)} %add_convert_fusion.2), channel_id=1, source_target_pairs={{0,0},{1,9},{2,18},{3,27},{8,2},{9,11},{10,16},{11,25},{16,3},{17,... | collective-permute-start | bytes 1769480 | tf_op jit(solution)/shard_map/ppermute | solution.py:131
  (242 other events, 3933.4 us)

commit v2 on v1

v2 whole, which is shorter than its diff:
```python
import jax
import jax.numpy as jnp
from jax import lax
from jax.experimental import pallas as pl
from jax.experimental.pallas import tpu as pltpu
from jax.sharding import PartitionSpec as P

EPS = 1e-06
GELU_C = 0.7978845608028654
GELU_K = 0.044715
BF = jnp.bfloat16
F32 = jnp.float32
PLANE = ("dp", "col")
IMAGE, TEXT = 0, 1


def gelu_parts(hidden):
    tangent = jnp.tanh(GELU_C * (hidden + GELU_K * hidden * hidden * hidden))
    gelu_value = 0.5 * hidden * (1.0 + tangent)
    gelu_slope = 0.5 * (1.0 + tangent) + 0.5 * hidden * (1.0 - tangent * tangent) * GELU_C * (
        1.0 + 3.0 * GELU_K * hidden * hidden
    )
    return (gelu_value, gelu_slope)


def transposed_left(left_side, right_side):
    return lax.dot_general(
        left_side, right_side, (((0,), (0,)), ((), ())), preferred_element_type=F32
    )


def transposed_right(left_side, right_side):
    return lax.dot_general(
        left_side, right_side, (((1,), (1,)), ((), ())), preferred_element_type=F32
    )


def product(left_side, right_side):
    return jnp.dot(left_side, right_side, preferred_element_type=F32)


VMEM_BYTES = 56 * 1024 * 1024
FREE = pl.CostEstimate(flops=0, bytes_accessed=0, transcendentals=0)


def call(body, grid, in_specs, out_specs, out_shape, operands):
    return pl.pallas_call(
        body,
        grid_spec=pltpu.PrefetchScalarGridSpec(
            num_scalar_prefetch=1, grid=grid, in_specs=in_specs, out_specs=out_specs
        ),
        out_shape=out_shape,
        cost_estimate=FREE,
        compiler_params=pltpu.CompilerParams(vmem_limit_bytes=VMEM_BYTES),
    )(*operands)


def whole(shape):
    return pl.BlockSpec(shape, lambda step, order: (0,) * len(shape))


def on_rows(shape):
    return pl.BlockSpec(shape, lambda step, order: (step, 0))


def on_columns(shape):
    return pl.BlockSpec(shape, lambda step, order: (0, step))


def mix(columns, weights, order, split, back, extra, outs, finish):
    tokens, width = columns.shape[1:]
    total = weights[0][0].shape[0 if back else 1]
    block = width
    pair = (block, 2 * width) if back else (2 * width, block)
    ranges = ((0, split), (split, tokens))

    def body(order_ref, columns_ref, *refs):
        multiply = transposed_right if back else product
        for stream, (low, high) in enumerate(ranges):
            blocks = [columns_ref[order_ref[4 * stream + b], low:high] for b in range(4)]
            even = jnp.concatenate([blocks[0], blocks[2]], axis=1)
            odd = jnp.concatenate([blocks[1], blocks[3]], axis=1)
            value = multiply(even, refs[2 * stream][...]) + multiply(odd, refs[2 * stream + 1][...])
            finish(stream, slice(low, high), value, refs[4:])

    return call(
        body,
        (total // block,),
        [whole(columns.shape)]
        + [on_rows(pair) if back else on_columns(pair)] * 4
        + [on_columns((item.shape[0], block)) for item in extra],
        [on_columns((rows, block)) for rows, _ in outs],
        [jax.ShapeDtypeStruct((rows, total), kind) for rows, kind in outs],
        (order, columns, *weights[0], *weights[1], *extra),
    )


def parts(inputs, weights, order, split, back):
    tokens, depth = inputs.shape
    width = weights[0][0].shape[0 if back else 1] // 2
    pair = (width, depth) if back else (depth, width)
    ranges = ((0, split), (split, tokens))

    def body(order_ref, inputs_ref, *refs):
        multiply = transposed_right if back else product
        for half in range(2):
            for stream, (low, high) in enumerate(ranges):
                place = order_ref[4 * stream + 2 * pl.program_id(0) + half]
                value = multiply(inputs_ref[low:high], refs[2 * stream + half][...])
                refs[4][place, low:high] = value.astype(BF)

    return call(
        body,
        (2,),
        [whole(inputs.shape)] + [on_rows(pair) if back else on_columns(pair)] * 4,
        whole((4, tokens, width)),
        jax.ShapeDtypeStruct((4, tokens, width), BF),
        (order, inputs, *weights[0], *weights[1]),
    )


def weight_grads(columns, inputs, order, split, back):
    tokens, width = columns.shape[1:]
    depth = inputs.shape[1]
    shape = (2 * width, depth) if back else (depth, 2 * width)
    pair = (width, depth) if back else (depth, width)
    ranges = ((0, split), (split, tokens))

    def body(order_ref, columns_ref, inputs_ref, *refs):
        for half in range(2):
            for stream, (low, high) in enumerate(ranges):
                place = order_ref[4 * stream + 2 * pl.program_id(0) + half]
                column = columns_ref[place, low:high]
                other = inputs_ref[low:high]
                if back:
                    value = transposed_left(column, other)
                else:
                    value = transposed_left(other, column)
                refs[2 * stream + half][...] = value.astype(BF)

    grads = call(
        body,
        (2,),
        [whole(columns.shape), whole(inputs.shape)],
        [on_rows(pair) if back else on_columns(pair)] * 4,
        [jax.ShapeDtypeStruct(shape, BF)] * 4,
        (order, columns, inputs),
    )
    return [(grads[0], grads[1]), (grads[2], grads[3])]


def steps_for(extents, lanes):
    tile = 128 if lanes else 16
    return 3 if all(extent % (3 * tile) == 0 for extent in extents) else 1


def beside(first, second, axis):
    shape = list(first.shape)
    shape[axis] *= 2
    half = first.shape[axis]
    steps = steps_for([first.shape[1 - axis]], axis == 0)
    other = first.shape[1 - axis] // steps
    spec = on_columns if axis == 0 else on_rows

    def block(rows, columns):
        return spec((rows, other) if axis == 0 else (other, columns))

    def body(order_ref, first_ref, second_ref, out_ref):
        if axis == 0:
            out_ref[:half] = first_ref[...]
            out_ref[half:] = second_ref[...]
        else:
            out_ref[...] = jnp.concatenate([first_ref[...], second_ref[...]], axis=1)

    return call(
        body,
        (steps,),
        [block(*first.shape)] * 2,
        block(*shape),
        jax.ShapeDtypeStruct(tuple(shape), first.dtype),
        (jnp.zeros((1,), jnp.int32), first, second),
    )


def add_and_cut(pairs, cuts):
    over_columns = [pair[0].shape[1] for pair, cut in zip(pairs, cuts) if cut == 0]
    over_rows = [pair[0].shape[0] for pair, cut in zip(pairs, cuts) if cut == 1]
    steps = min(steps_for(over_columns, True), steps_for(over_rows, False))
    in_specs, out_specs, out_shape = [], [], []
    for (first, _), cut in zip(pairs, cuts):
        rows, columns = first.shape
        if cut == 0:
            in_specs += [on_columns((rows, columns // steps))] * 2
            out_specs += [on_columns((rows // 2, columns // steps))] * 2
            out_shape += [jax.ShapeDtypeStruct((rows // 2, columns), BF)] * 2
        else:
            in_specs += [on_rows((rows // steps, columns))] * 2
            out_specs += [on_rows((rows // steps, columns // 2))] * 2
            out_shape += [jax.ShapeDtypeStruct((rows, columns // 2), BF)] * 2

    def body(order_ref, *refs):
        for item, cut in enumerate(cuts):
            total = refs[2 * item][...].astype(F32) + refs[2 * item + 1][...].astype(F32)
            total = total.astype(BF)
            outs = refs[2 * len(cuts) + 2 * item :]
            half = total.shape[cut] // 2
            outs[0][...] = total[:half] if cut == 0 else total[:, :half]
            outs[1][...] = total[half:] if cut == 0 else total[:, half:]

    flat = [array for pair in pairs for array in pair]
    halves = call(
        body, (steps,), in_specs, out_specs, out_shape, (jnp.zeros((1,), jnp.int32), *flat)
    )
    return [(halves[2 * item], halves[2 * item + 1]) for item in range(len(pairs))]


def add_up(pairs):
    steps = steps_for([pair[0].shape[0] for pair in pairs], False)
    specs = [on_rows((pair[0].shape[0] // steps, pair[0].shape[1])) for pair in pairs]

    def body(order_ref, *refs):
        for item in range(len(pairs)):
            total = refs[2 * item][...].astype(F32) + refs[2 * item + 1][...].astype(F32)
            refs[2 * len(pairs) + item][...] = total.astype(BF)

    return call(
        body,
        (steps,),
        [spec for spec in specs for _ in range(2)],
        specs,
        [jax.ShapeDtypeStruct(pair[0].shape, BF) for pair in pairs],
        (jnp.zeros((1,), jnp.int32), *[array for pair in pairs for array in pair]),
    )


def head_parts(packed_ref, head, size):
    start = head * 3 * size
    return [packed_ref[:, start + j * size : start + (j + 1) * size] for j in range(3)]


def attend(packed, order, size, count):
    tokens = packed.shape[0]
    heads = packed.shape[1] // (3 * size)
    scale = size ** (-0.5)

    def body(order_ref, packed_ref, out_ref, log_ref):
        keep = lax.broadcasted_iota(jnp.int32, (tokens, tokens), 0) < count
        for pair in range(heads // 2):
            attended = []
            for head in (2 * pair, 2 * pair + 1):
                query, key, value = head_parts(packed_ref, head, size)
                scores = transposed_right(key, query) * scale
                powers = jnp.where(keep, jnp.exp(scores), 0.0)
                log_total = jnp.log(jnp.sum(powers, axis=0, keepdims=True))
                log_ref[head : head + 1] = log_total
                probs = jnp.where(keep, jnp.exp(scores - log_total), 0.0).astype(BF)
                attended.append(transposed_left(value, probs))
            both = jnp.concatenate(attended, axis=0)
            out_ref[:, 2 * pair * size : 2 * (pair + 1) * size] = both.T.astype(BF)

    return call(
        body,
        (1,),
        [whole(packed.shape)],
        [whole((tokens, heads * size)), whole((heads, tokens))],
        [
            jax.ShapeDtypeStruct((tokens, heads * size), BF),
            jax.ShapeDtypeStruct((heads, tokens), F32),
        ],
        (order, packed),
    )


def attend_back(packed, attended, log_total, d_attended, order, size, count):
    tokens = packed.shape[0]
    heads = packed.shape[1] // (3 * size)
    scale = size ** (-0.5)

    def body(order_ref, packed_ref, attended_ref, log_ref, d_ref, out_ref):
        keep = lax.broadcasted_iota(jnp.int32, (tokens, tokens), 0) < count
        for pair in range(heads // 2):
            lanes = slice(2 * pair * size, 2 * (pair + 1) * size)
            d_pair = d_ref[:, lanes]
            both = d_pair.astype(F32) * attended_ref[:, lanes].astype(F32)
            both = both.T
            grads = []
            for side in range(2):
                head = 2 * pair + side
                delta = jnp.sum(both[side * size : (side + 1) * size], axis=0, keepdims=True)
                query, key, value = head_parts(packed_ref, head, size)
                d_out = d_pair[:, side * size : (side + 1) * size]
                scores = transposed_right(key, query) * scale
                weights = jnp.where(keep, jnp.exp(scores - log_ref[head : head + 1]), 0.0)
                d_value = product(weights.astype(BF), d_out)
                d_probs = transposed_right(value, d_out)
                d_scores = (weights * (d_probs - delta) * scale).astype(BF)
                d_key = product(d_scores, query)
                d_query = transposed_left(key, d_scores).T
                grads += [d_query, d_key, d_value]
            start = 2 * pair * 3 * size
            merged = jnp.concatenate(grads, axis=1).astype(BF)
            out_ref[:, start : start + 6 * size] = merged

    return call(
        body,
        (1,),
        [
            whole(packed.shape),
            whole(attended.shape),
            whole(log_total.shape),
            whole(d_attended.shape),
        ],
        whole(packed.shape),
        jax.ShapeDtypeStruct(packed.shape, BF),
        (order, packed, attended, log_total, d_attended),
    )


class Grid:
    def __init__(self):
        self.dps = lax.axis_size("dp")
        self.cols = lax.axis_size("col")
        self.dp = lax.axis_index("dp")
        self.row = lax.axis_index("row")
        self.col = lax.axis_index("col")

    def hop(self, dp, block, stream):
        mixed = (dp % self.cols) ^ block
        return ((mixed % 2) * 2 + mixed // 2) ^ (2 * stream)

    def along_plane(self, target):
        pairs = []
        for dp in range(self.dps):
            for col in range(self.cols):
                to_dp, to_col = target(dp, col)
                pairs.append((dp * self.cols + col, to_dp * self.cols + to_col % self.cols))
        return pairs

    def spread(self, values, stream):
        return lax.ppermute(
            values, PLANE, self.along_plane(lambda d, c: (d, c + self.hop(d, 0, stream)))
        )

    def bring_back(self, values, stream):
        return lax.ppermute(
            values, PLANE, self.along_plane(lambda d, c: (d, c - self.hop(d, 0, stream)))
        )

    def swap_dp(self, values, bit):
        return lax.ppermute(values, "dp", [(d, d ^ bit) for d in range(self.dps)])

    def swap_row(self, values):
        return lax.ppermute(values, "row", [(0, 1), (1, 0)])

    def copies(self, values):
        return jnp.broadcast_to(values[None], (self.cols, *values.shape))

    def exchange(self, values):
        return lax.all_to_all(values, "col", 0, 0, tiled=True)

    def everyone(self, values):
        return self.exchange(self.copies(values))

    def order(self):
        hops = [
            self.hop(self.dp, block, stream)
            for stream in (IMAGE, TEXT)
            for block in range(self.cols)
        ]
        return jnp.stack([(self.col - hop) % self.cols for hop in hops]).astype(jnp.int32)

    def piece(self, shard, axis, stream):
        width = shard.shape[axis] // self.cols
        index = (self.col + self.hop(self.dp, 0, stream)) % self.cols
        return lax.dynamic_slice_in_dim(shard, index * width, width, axis)

    def move(self, values, by_row):
        return self.swap_row(values) if by_row else self.swap_dp(values, 2)

    def fold_rest(self, total):
        bit = self.dps // 2
        while bit >= self.cols:
            half = total.shape[0] // 2
            upper = (self.dp // bit) % 2
            keep = lax.dynamic_slice_in_dim(total, upper * half, half, 0)
            send = lax.dynamic_slice_in_dim(total, (1 - upper) * half, half, 0).astype(BF)
            total = keep + self.swap_dp(send, bit).astype(F32)
            bit //= 2
        return total.astype(BF)

    def place_rows(self, parts):
        share = self.dps // self.cols
        placed = []
        for stream, part in enumerate(parts):
            pairs = self.along_plane(
                lambda d, c: (c * share + d // self.cols, c - self.hop(d, 0, stream))
            )
            placed.append(lax.ppermute(self.fold_rest(part), PLANE, pairs))
        return placed

    def place_cols(self, parts):
        return [self.bring_back(part, stream) for stream, part in enumerate(parts)]

    def place_cols_end(self, groups):
        widths = [group[0].shape[1] for group in groups]
        moved = jnp.concatenate([jnp.stack(group) for group in groups], axis=2)
        moved = moved.reshape(moved.shape[0], self.dps, -1, moved.shape[2])
        from_dp = lax.all_to_all(moved, "dp", 1, 1, tiled=True).astype(F32)
        from_low = from_dp.reshape(from_dp.shape[0], -1, self.cols, *from_dp.shape[2:])
        from_low = jnp.sum(from_low, axis=1)
        placed = []
        for place in range(self.cols):
            streams = []
            for stream in (IMAGE, TEXT):
                hops = ((place - self.col) % self.cols) ^ (2 * stream)
                low = (hops % 2) * 2 + hops // 2
                streams.append(lax.dynamic_index_in_dim(from_low[stream], low, 0, False))
            placed.append(jnp.stack(streams))
        results, start = [], 0
        for width in widths:
            whole_rows = jnp.concatenate(
                [item[:, :, start : start + width] for item in placed], axis=2
            )
            results.append([whole_rows[s][None] for s in range(whole_rows.shape[0])])
            start += width
        return results


def after(values, *earlier):
    return lax.optimization_barrier((values, earlier))[0]


def added(parts):
    return sum(part.astype(F32) for part in parts)


def column_sum(parts):
    return jnp.sum(parts.astype(F32), axis=0)


def norm_forward(grid, values):
    width = values.shape[1]
    own_mean = jnp.mean(values, axis=1)
    centred = values - own_mean[:, None]
    packed = jnp.stack([own_mean, jnp.sum(centred * centred, axis=1)])
    everyone = grid.everyone(packed)
    mean = jnp.mean(everyone[:, 0], axis=0)
    squares = jnp.sum(everyone[:, 1] + width * (everyone[:, 0] - mean) ** 2, axis=0)
    inv_std = lax.rsqrt(squares / (width * grid.cols) + EPS)
    return ((values - mean[:, None]) * inv_std[:, None], inv_std[:, None])


def norm_backward(grid, grad_hat, normed, inv_std):
    full_width = grad_hat.shape[1] * grid.cols
    packed = jnp.stack([jnp.sum(grad_hat, axis=1), jnp.sum(grad_hat * normed, axis=1)])
    total = jnp.sum(grid.everyone(packed), axis=0) / full_width
    return inv_std * (grad_hat - total[0][:, None] - normed * total[1][:, None])


def shards(
    image_in,
    text_in,
    condition,
    image_mod_weight,
    image_mod_bias,
    image_qkv_weight,
    image_qv_bias,
    image_out_weight,
    image_out_bias,
    image_up_weight,
    image_up_bias,
    image_down_weight,
    image_down_bias,
    text_mod_weight,
    text_mod_bias,
    text_qkv_weight,
    text_qv_bias,
    text_out_weight,
    text_out_bias,
    text_up_weight,
    text_up_bias,
    text_down_weight,
    text_down_bias,
    image_cotangent,
    text_cotangent,
):
    grid = Grid()
    streams = (IMAGE, TEXT)
    seq_count = condition.shape[0]
    col_width = image_in.shape[1]
    order = grid.order()
    split = image_in.shape[0]
    count = split + text_in.shape[0]
    padding = -count % 16
    lengths = (split, text_in.shape[0] + padding)
    heads = image_qv_bias.shape[0]
    head_size = image_qv_bias.shape[2]
    mod_weights = (image_mod_weight, text_mod_weight)
    mod_rows = image_mod_weight.shape[0]

    def join(parts):
        return jnp.concatenate(parts, axis=0)

    def padded(parts):
        zeros = jnp.zeros((padding, col_width), F32)
        return join([part.astype(F32) for part in parts] + [zeros])

    def rows_of(values):
        return (values[:split], values[split:])

    def unpadded(values):
        return (values[:split], values[split:count])

    by_row_first = (True, False)

    def pieces(weights, axis):
        return [grid.piece(weight, axis, s) for s, weight in enumerate(weights)]

    def fetch(parts):
        return [grid.spread(part, s) for s, part in enumerate(parts)]

    def fetch_pairs(parts, axis, first):
        pairs = []
        for s in streams:
            by_row = by_row_first[s] == first
            other = grid.move(parts[s], by_row)
            pairs.append(beside(parts[s], other, axis if by_row else 1 - axis))
        return pairs

    def fetch_last(evens):
        return [(even, grid.swap_dp(even, 1)) for even in evens]

    def fold_core(grads):
        return [(even, grid.swap_dp(odd, 1)) for even, odd in grads]

    def cut_axes(axis, first):
        return [axis if by_row == first else 1 - axis for by_row in by_row_first]

    def fold(pairs, axes, first):
        flat = [pair for group in pairs for pair in group]
        halves = add_and_cut(flat, [cut for axis in axes for cut in cut_axes(axis, first)])
        return [halves[2 * group : 2 * group + 2] for group in range(len(pairs))]

    def move(groups, first):
        return [
            [(keep, grid.move(send, by_row_first[s] == first)) for s, (keep, send) in enumerate(group)]
            for group in groups
        ]

    def fold_end(groups):
        sums = add_up([pair for group in groups for pair in group])
        return [sums[2 * group : 2 * group + 2] for group in range(len(groups))]

    qkv_pieces = pieces((image_qkv_weight, text_qkv_weight), 1)
    qkv_mine = fetch(qkv_pieces)
    qkv_pair = fetch_pairs(qkv_mine, 1, True)
    image_in, text_in, condition = after((image_in, text_in, condition), qkv_pieces)

    act_cond = (condition * jax.nn.sigmoid(condition)).astype(BF)
    partial_mod = jnp.stack(
        [
            jnp.stack([product(act_cond, weight[:, j]) for j in range(6)], axis=1)
            for weight in mod_weights
        ],
        axis=1,
    )
    own_mod = lax.dynamic_index_in_dim(partial_mod, grid.row, 0, False)
    other_mod = lax.dynamic_index_in_dim(partial_mod, 1 - grid.row, 0, False)
    up_count = image_up_bias.shape[0] // grid.cols
    own_qv = jnp.stack([image_qv_bias, text_qv_bias])
    own_up = lax.dynamic_slice_in_dim(
        jnp.stack([image_up_bias, text_up_bias]), grid.col * up_count, up_count, 1
    )
    to_row = [values.reshape(-1, col_width) for values in (other_mod, own_qv, own_up)]
    cuts = (to_row[0].shape[0], to_row[0].shape[0] + to_row[1].shape[0])
    from_row = jnp.split(grid.swap_row(after(jnp.concatenate(to_row), qkv_mine)), cuts)
    modulation = own_mod + from_row[0].reshape(own_mod.shape)
    modulation = modulation + jnp.stack([image_mod_bias, text_mod_bias])

    def field(position):
        return join(
            [
                jnp.broadcast_to(modulation[s, position], (lengths[s], col_width))
                for s in streams
            ]
        )

    def token_sums(values):
        return jnp.stack([jnp.sum(part, axis=0) for part in rows_of(values)])

    qv_bias = jnp.concatenate([own_qv, from_row[1].reshape(own_qv.shape)], axis=1)
    bias_rows = jnp.stack(
        [qv_bias[:, :, 0], jnp.zeros(qv_bias[:, :, 0].shape, F32), qv_bias[:, :, 1]], axis=2
    ).reshape(2, -1)
    up_bias = jnp.concatenate([own_up, from_row[2].reshape(own_up.shape)], axis=1)
    out_bias = (image_out_bias, text_out_bias)
    down_bias = (image_down_bias, text_down_bias)

    def with_bias(values, bias):
        return join([part + bias[s][None, :] for s, part in enumerate(rows_of(values))])

    def keep_bf16(stream, rows, value, refs):
        refs[-1][rows] = value.astype(BF)

    def add_bias(stream, rows, value, refs):
        refs[1][rows] = (value + refs[0][stream : stream + 1]).astype(BF)

    def into_gelu(stream, rows, value, refs):
        gelu_value, gelu_slope = gelu_parts(value + refs[0][stream : stream + 1])
        refs[1][rows] = gelu_value.astype(BF)
        refs[2][rows] = gelu_slope

    def times_slope(stream, rows, value, refs):
        d_hidden = (value * refs[0][rows]).astype(BF)
        refs[1][rows] = d_hidden
        refs[2][stream : stream + 1] = jnp.sum(d_hidden.astype(F32), axis=0, keepdims=True)

    values = padded([image_in, text_in])
    xhat1, inv1 = norm_forward(grid, values)
    scale1 = 1.0 + field(1)
    normed1_own = (xhat1 * scale1 + field(0)).astype(BF)
    normed1_copies = after(grid.copies(normed1_own), qkv_mine)
    normed1 = grid.exchange(normed1_copies)
    qkv_even = fetch_pairs(after(qkv_pair, normed1_copies), 1, False)
    late_weights = after(
        (
            (image_out_weight, text_out_weight),
            (image_up_weight, text_up_weight),
            (image_down_weight, text_down_weight),
        ),
        qkv_mine,
    )
    out_mine = fetch(pieces(late_weights[0], 0))
    up_pieces = pieces(late_weights[1], 1)
    down_pieces = pieces(late_weights[2], 0)
    out_pair = fetch_pairs(after(out_mine, normed1_copies), 0, True)
    normed1, qkv_even, out_pair, up_pieces, down_pieces = lax.optimization_barrier(
        (normed1, qkv_even, out_pair, up_pieces, down_pieces)
    )
    out_even = fetch_pairs(out_pair, 0, False)
    qkv_w = fetch_last(qkv_even)
    up_mine = fetch(up_pieces)
    down_mine = fetch(down_pieces)
    tokens = values.shape[0]
    (packed,) = mix(
        normed1, qkv_w, order, split, False, [bias_rows], [(tokens, BF)], add_bias
    )
    attn, log_total = attend(packed, order, head_size, count)
    out_w = fetch_last(after(out_even, packed))
    attn_out = parts(attn, out_w, order, split, False)
    attn_out, up_mine = lax.optimization_barrier((attn_out, up_mine))
    parts_out = grid.exchange(attn_out)
    up_pair = fetch_pairs(up_mine, 1, True)
    parts_out, up_pair, down_mine = lax.optimization_barrier((parts_out, up_pair, down_mine))
    branch1 = with_bias(column_sum(parts_out), out_bias)

    gate1 = field(2)
    middle = values + gate1 * branch1
    xhat2, inv2 = norm_forward(grid, middle)
    scale2 = 1.0 + field(4)
    gate2 = field(5)
    normed2_copies = grid.copies((xhat2 * scale2 + field(3)).astype(BF))
    normed2 = grid.exchange(normed2_copies)
    grad_out = padded([image_cotangent, text_cotangent])
    d_branch2_own = (grad_out * gate2).astype(BF)
    d_branch2_copies = grid.copies(after(d_branch2_own, normed2_copies))
    up_even = fetch_pairs(up_pair, 1, False)
    down_pair = fetch_pairs(down_mine, 0, True)
    normed2, down_pair, d_branch2_copies, up_even = lax.optimization_barrier(
        (normed2, down_pair, d_branch2_copies, up_even)
    )
    d_branch2 = grid.exchange(d_branch2_copies)
    up_w = fetch_last(up_even)
    down_even = fetch_pairs(down_pair, 0, False)
    gelu, slope = mix(
        normed2, up_w, order, split, False, [up_bias], [(tokens, BF), (tokens, F32)], into_gelu
    )

    d_branch2, gelu, down_even = lax.optimization_barrier((d_branch2, gelu, down_even))
    down_w = fetch_last(down_even)
    d_hidden, up_sums = mix(
        d_branch2, down_w, order, split, True, [slope], [(tokens, BF), (2, F32)], times_slope
    )
    hidden_back = parts(d_hidden, up_w, order, split, True)
    parts_normed2 = grid.exchange(hidden_back)
    gelu_late, d_hidden_late = after((gelu, d_hidden), hidden_back)
    down_fold = fold_core(weight_grads(d_branch2, gelu_late, order, split, False))
    up_fold = fold_core(weight_grads(normed2, d_hidden_late, order, split, True))
    gelu_down = parts(gelu_late, down_w, order, split, False)
    folds = fold([down_fold, up_fold], (0, 1), True)
    parts_normed2, folds, gelu_down = lax.optimization_barrier((parts_normed2, folds, gelu_down))
    folds = move(folds, True)
    d_normed2 = column_sum(parts_normed2)
    d_shift2 = token_sums(d_normed2)
    d_scale2 = token_sums(d_normed2 * xhat2)
    d_middle = grad_out + norm_backward(grid, d_normed2 * scale2, xhat2, inv2)

    d_gate1 = token_sums(d_middle * branch1)
    d_branch1_own = (d_middle * gate1).astype(BF)
    d_branch1 = grid.exchange(grid.copies(d_branch1_own))
    down_fold, up_fold = folds
    d_branch1, gelu_down, down_fold = lax.optimization_barrier((d_branch1, gelu_down, down_fold))
    parts_branch2 = grid.exchange(gelu_down)
    (d_attn,) = mix(d_branch1, out_w, order, split, True, [], [(tokens, BF)], keep_bf16)
    down_fold = move(fold([down_fold], (0,), False), False)
    d_qkv = attend_back(packed, attn, log_total, d_attn, order, head_size, count)
    qkv_back = parts(d_qkv, qkv_w, order, split, True)
    qkv_back, parts_branch2, up_fold = lax.optimization_barrier((qkv_back, parts_branch2, up_fold))
    folds = down_fold + move(fold([up_fold], (1,), False), False)
    parts_normed1 = grid.exchange(qkv_back)
    d_qkv_late, attn_late = after((d_qkv, attn), qkv_back)
    qkv_fold = fold_core(weight_grads(normed1, d_qkv_late, order, split, True))
    out_fold = fold_core(weight_grads(d_branch1, attn_late, order, split, False))
    late_folds = fold([qkv_fold, out_fold], (1, 0), True)
    parts_normed1, late_folds = lax.optimization_barrier((parts_normed1, late_folds))
    folds = after(folds, parts_normed1)
    late_folds = move(late_folds, True)
    down_fold, up_fold = fold_end(folds)
    d_normed1 = column_sum(parts_normed1)
    d_shift1 = token_sums(d_normed1)
    d_scale1 = token_sums(d_normed1 * xhat1)
    norm_back1 = norm_backward(grid, d_normed1 * scale1, xhat1, inv1)
    branch2 = with_bias(column_sum(parts_branch2), down_bias)
    outputs = unpadded((middle + gate2 * branch2).astype(BF))
    d_gate2 = token_sums(grad_out * branch2)
    norm_back1, late_folds, down_fold, up_fold, d_gate2 = lax.optimization_barrier(
        (norm_back1, late_folds, down_fold, up_fold, d_gate2)
    )
    down_placed, up_placed = grid.place_rows(down_fold), grid.place_cols(up_fold)
    late_folds = move(fold(late_folds, (1, 0), False), False)

    head_sums = token_sums(d_qkv.astype(F32))
    head_sums = head_sums.reshape(2, 2, heads, 3, head_size)
    head_sums = jnp.stack([head_sums[:, :, :, 0], head_sums[:, :, :, 2]], axis=3)
    vectors = jnp.concatenate(
        [
            jnp.stack([d_shift1, d_scale1, d_gate1, d_shift2, d_scale2, d_gate2], axis=1),
            token_sums(d_branch1_own.astype(F32))[:, None],
            token_sums(d_branch2_own.astype(F32))[:, None],
            head_sums.reshape(2, -1, col_width),
            up_sums.reshape(2, -1, col_width),
        ],
        axis=1,
    ).astype(BF)
    act_all = act_cond
    everyone = jnp.stack([vectors, grid.swap_row(vectors)])
    bit = grid.dps // 2
    while bit:
        everyone = jnp.concatenate([everyone, grid.swap_dp(everyone, bit)])
        act_all = jnp.concatenate([act_all, grid.swap_dp(after(act_all, vectors), bit)])
        bit //= 2
    everyone, late_folds = lax.optimization_barrier((everyone, late_folds))
    qkv_fold, out_fold = fold_end(late_folds)
    qkv_placed, out_placed = grid.place_cols(qkv_fold), grid.place_rows(out_fold)
    in_grads = unpadded(d_middle + norm_back1)
    vector_sums = jnp.sum(everyone.astype(F32), axis=0)
    feature_share = col_width // grid.dps
    shares = lax.dynamic_slice_in_dim(vector_sums, grid.dp * feature_share, feature_share, 2)

    def over_rows(rows, shape):
        halves = rows.reshape(grid.dps, 2, 2, 2, -1).astype(F32)
        total = jnp.sum(halves[:, 0, :, 0] + halves[:, 1, :, 1], axis=0)
        return total.reshape(2, *shape)

    head_rows = 2 * heads * 2 * head_size // col_width
    head_total = over_rows(everyone[:, :, 8 : 8 + head_rows], (heads, 2, head_size))
    up_total_own = over_rows(everyone[:, :, 8 + head_rows :], (up_count,))
    head_share = head_size // grid.dps
    head_total = lax.dynamic_slice_in_dim(head_total, grid.dp * head_share, head_share, 3)
    qv_b_grad = jnp.transpose(head_total, (0, 3, 1, 2))

    by_row = everyone[:, :, :6].reshape(grid.dps, 2, 2, 6, col_width)
    d_mod = jnp.where(grid.row == 0, by_row, by_row[:, ::-1]).reshape(-1, 2, 6, col_width)
    mod_share = mod_rows // grid.dps
    act_share = lax.dynamic_slice_in_dim(act_all, grid.dp * mod_share, mod_share, 1)
    mod_w_grad = [
        jnp.stack([transposed_left(act_share, d_mod[:, s, j]) for j in range(6)], axis=1)[None]
        for s in streams
    ]
    own_d_mod = d_mod[:seq_count]
    cond_part = sum(
        transposed_right(own_d_mod[:, s, j], mod_weights[s][:, j])
        for s in streams
        for j in range(6)
    )
    lasts = grid.everyone(jnp.stack([cond_part, up_total_own]))
    cond_sum = jnp.sum(lasts[:, 0], axis=0)
    up_share = up_count * grid.cols // grid.dps
    up_chosen = lax.dynamic_index_in_dim(
        lasts[:, 1], grid.dp * grid.cols // grid.dps, 0, False
    )
    up_start = (grid.dp % (grid.dps // grid.cols)) * up_share
    up_b_grad = lax.dynamic_slice_in_dim(up_chosen, up_start, up_share, 1)
    qkv_total, up_total = grid.place_cols_end([qkv_placed, up_placed])
    down_total = [down_placed[s].astype(F32)[None] for s in streams]
    out_total = [out_placed[s].astype(F32)[None] for s in streams]
    sigmoid_cond = jax.nn.sigmoid(condition)
    condition_grad = cond_sum * sigmoid_cond * (1.0 + condition * (1.0 - sigmoid_cond))

    grads = []
    for s in streams:
        grads += [
            mod_w_grad[s],
            jnp.transpose(shares[s, :6])[None],
            qkv_total[s],
            qv_b_grad[s],
            out_total[s],
            shares[s, 6][None],
            up_total[s],
            up_b_grad[s][None],
            down_total[s],
            shares[s, 7][None],
        ]
    return (*outputs, *in_grads, condition_grad, *grads)


def solution(mesh):
    in_specs = (
        P(("dp", "row"), "col"),
        P(("dp", "row"), "col"),
        P("dp", "row"),
        P("row", None, "col"),
        P(None, "col"),
        P("col", "row"),
        P(("row", "col"), None, None),
        P("row", "col"),
        P("col"),
        P("col", "row"),
        P("row"),
        P("row", "col"),
        P("col"),
        P("row", None, "col"),
        P(None, "col"),
        P("col", "row"),
        P(("row", "col"), None, None),
        P("row", "col"),
        P("col"),
        P("col", "row"),
        P("row"),
        P("row", "col"),
        P("col"),
        P(("dp", "row"), "col"),
        P(("dp", "row"), "col"),
    )
    out_specs = (
        P(("dp", "row"), "col"),
        P(("dp", "row"), "col"),
        P(("dp", "row"), "col"),
        P(("dp", "row"), "col"),
        P("dp", "row"),
        P("row", "dp", None, "col"),
        P("col", "dp", None),
        P("col", "dp", "row"),
        P("dp", ("row", "col"), None),
        P("row", "dp", "col"),
        P("col", "dp"),
        P("col", "dp", "row"),
        P("row", "dp"),
        P("row", "dp", "col"),
        P("col", "dp"),
        P("row", "dp", None, "col"),
        P("col", "dp", None),
        P("col", "dp", "row"),
        P("dp", ("row", "col"), None),
        P("row", "dp", "col"),
        P("col", "dp"),
        P("col", "dp", "row"),
        P("row", "dp"),
        P("row", "dp", "col"),
        P("col", "dp"),
    )
    return jax.shard_map(shards, mesh=mesh, in_specs=in_specs, out_specs=out_specs, check_vma=False)
```

time: 897 us -> 840 us (0.936)
  the two profiles are of different devices: /device:TPU:3 before, /device:TPU:0 now
where the time goes in v2:
time: 840 us; the launch traced here: 824 us
  waiting for transfers between devices  292 us (35%)
  Pallas kernels  207 us (25%)
  starting transfers between devices  156 us (19%)
  local copies, waits for them, and re-layouts  60.7 us (7%)
  other arithmetic  43 us (5%)
  matrix products  33.4 us (4%)
  blocking collectives  28.9 us (3%)
    pallas_call x37, Pallas kernels, call(): pl.pallas_call(body, grid_spec=pltpu.PrefetchScalarGridSpec(num_scalar_pr...  207 us
    ppermute x18, waiting for transfers between devices, swap_row(): return lax.ppermute(values, 'row', [(0, 1), (1, 0)])  90.6 us
    ppermute x8, waiting for transfers between devices, spread(): lax.ppermute(values, PLANE, self.along_plane(lambda d, c: (d, c + self.ho...  83.6 us
    ppermute x36, waiting for transfers between devices, swap_dp(): return lax.ppermute(values, 'dp', [(d, d ^ bit) for d in range(self.dps)])  59.1 us
    all_to_all x10, starting transfers between devices, exchange(): return lax.all_to_all(values, 'col', 0, 0, tiled=True)  47.6 us
    all_to_all x10, waiting for transfers between devices, exchange(): return lax.all_to_all(values, 'col', 0, 0, tiled=True)  32.4 us
    all_to_all x3, blocking collectives, exchange(): return lax.all_to_all(values, 'col', 0, 0, tiled=True)  28.9 us
    ppermute x36, starting transfers between devices, swap_dp(): return lax.ppermute(values, 'dp', [(d, d ^ bit) for d in range(self.dps)])  24.1 us
  transfers between devices with their start and end apart: 81, of which 27 were waited for; matrix products, arithmetic and copies ran while one was open for 11% of the time, Pallas kernels for 22%

profile of v2, /device:TPU:0, one launch (start us, length us, event | category | flops | bytes accessed | tf_op | source)
XLA Modules:
  0.0 823.6 jit_solution(390492931078540330)
XLA Ops:
  35.9 11.2 %all_to_all.70 = f32[4,2,608]{2,1,0:T(2,128)S(1)} all-to-all(f32[4,2,608]{2,1,0:T(2,128)S(1)} %broadcast_in_dim.166), channel_id=1, replica_groups=mesh['dp'=4,'row'=2,'col'=4] {'col'}, dimensions={0} | all-to-all | bytes 38912 | tf_op jit(solution)/shard_map/all_to_all | solution.py:359
  55.4 9.0 %collective-permute-done.4.second_ref = bf16[384,576]{1,0:T(8,128)(2,1)S(1)} collective-permute-done((bf16[384,576]{1,0:T(8,128)(2,1)S(1)}, bf16[384,576]{1,0:T(8,128)(2,1)S(1)}, u32[]{:S(2)}, u32[]{:S(2)}) %collective-permute-start.4) | collective-permute-done | bytes 442400 | tf_op jit(solution)/shard_map/ppermute | solution.py:350
  80.8 20.4 %collective-permute-done.8.first_ref = bf16[192,384]{1,0:T(8,128)(2,1)S(1)} collective-permute-done((bf16[192,384]{1,0:T(8,128)(2,1)S(1)}, bf16[192,384]{1,0:T(8,128)(2,1)S(1)}, u32[]{:S(2)}, u32[]{:S(2)}) %collective-permute-start.8) | collective-permute-done | bytes 147488 | tf_op jit(solution)/shard_map/ppermute | solution.py:340
  165.4 13.3 %collective-permute-done.18.first_ref = bf16[384,768]{1,0:T(8,128)(2,1)S(1)} collective-permute-done((bf16[384,768]{1,0:T(8,128)(2,1)S(1)}, bf16[384,768]{1,0:T(8,128)(2,1)S(1)}, u32[]{:S(2)}, u32[]{:S(2)}) %collective-permute-start.18) | collective-permute-done | bytes 589856 | tf_op jit(solution)/shard_map/ppermute | solution.py:340
  206.5 45.7 %collective-permute-done.22.first_ref = bf16[768,384]{1,0:T(8,128)(2,1)S(1)} collective-permute-done((bf16[768,384]{1,0:T(8,128)(2,1)}, bf16[768,384]{1,0:T(8,128)(2,1)S(1)}, u32[]{:S(2)}, u32[]{:S(2)}) %collective-permute-start.22) | collective-permute-done | bytes 589856 | tf_op jit(solution)/shard_map/ppermute | solution.py:340
  275.0 35.4 %collective-permute-done.23.second_ref = bf16[768,384]{1,0:T(8,128)(2,1)S(1)} collective-permute-done((bf16[768,384]{1,0:T(8,128)(2,1)}, bf16[768,384]{1,0:T(8,128)(2,1)S(1)}, u32[]{:S(2)}, u32[]{:S(2)}) %collective-permute-start.23) | collective-permute-done | bytes 589856 | tf_op jit(solution)/shard_map/ppermute | solution.py:353
  338.9 24.6 %collective-permute-done.29.second_ref = bf16[1536,384]{1,0:T(8,128)(2,1)} collective-permute-done((bf16[1536,384]{1,0:T(8,128)(2,1)}, bf16[1536,384]{1,0:T(8,128)(2,1)}, u32[]{:S(2)}, u32[]{:S(2)}) %collective-permute-start.29) | collective-permute-done | bytes 1179680 | tf_op jit(solution)/shard_map/ppermute | solution.py:350
  371.3 11.8 %shard_map.449 = (bf16[608,1536]{1,0:T(8,128)(2,1)}, f32[608,1536]{1,0:T(8,128)}) custom-call(s32[8]{0:T(128)} %stack.381.order_ref, bf16[4,608,384]{2,1,0:T(8,128)(2,1)} %all-to-all-done.4.columns_ref, bf16[768,1536]{1,0:T(8,128)(2,1)} %shard_map.447.refs_0_, bf16[768,1536]{1,0:T(8,128)(2,1)} %collective-permute-done.27.refs_1_, ...), custom_call_target="tpu_custom_call" | custom-call | tf_op jit(solution)/shard_map/pallas_call | solution.py:47
  392.8 10.3 %shard_map.452 = (bf16[608,1536]{1,0:T(8,128)(2,1)}, f32[2,1536]{1,0:T(2,128)}) custom-call(s32[8]{0:T(128)} %stack.381.order_ref, bf16[4,608,384]{2,1,0:T(8,128)(2,1)} %all-to-all-done.5.columns_ref, bf16[1536,768]{1,0:T(8,128)(2,1)} %shard_map.450.refs_0_, bf16[1536,768]{1,0:T(8,128)(2,1)} %copy-done.17, bf16[1536,768]{1,0:T(8,128)(2,1)} %shard_map.451.refs_2_, ...), custom_call_target="tpu_custom_call" | custom-call | tf_op jit(solution)/shard_map/pallas_call | solution.py:47
  403.1 9.8 %shard_map.453 = bf16[4,608,384]{2,1,0:T(8,128)(2,1)} custom-call(s32[8]{0:T(128)} %stack.381.order_ref, bf16[608,1536]{1,0:T(8,128)(2,1)} %get-tuple-element.255.inputs_ref, bf16[768,1536]{1,0:T(8,128)(2,1)} %shard_map.447.refs_0_, bf16[768,1536]{1,0:T(8,128)(2,1)} %collective-permute-done.27.refs_1_, bf16[768,1536]{1,0:T(8,128)(2,1)} %shard_map.448.refs_2_, ...), custom_call_target="tpu_custom_call" | custom-call | tf_op jit(solution)/shard_map/pallas_call | solution.py:47
  427.3 9.9 %shard_map.454 = (bf16[1536,768]{1,0:T(8,128)(2,1)}, bf16[1536,768]{1,0:T(8,128)(2,1)}, bf16[1536,768]{1,0:T(8,128)(2,1)}, bf16[1536,768]{1,0:T(8,128)(2,1)}) custom-call(s32[8]{0:T(128)} %stack.381.order_ref, bf16[4,608,384]{2,1,0:T(8,128)(2,1)} %all-to-all-done.5.columns_ref, bf16[608,1536]{1,0:T(8,128)(2,1)} %get-tuple-element.250.inputs_ref), custom_call_target="tpu_custom_call" | custom-call | tf_op jit(solution)/shard_map/pallas_call | solution.py:47
  437.8 9.5 %shard_map.457 = bf16[4,608,384]{2,1,0:T(8,128)(2,1)} custom-call(s32[8]{0:T(128)} %stack.381.order_ref, bf16[608,1536]{1,0:T(8,128)(2,1)} %get-tuple-element.250.inputs_ref, bf16[1536,768]{1,0:T(8,128)(2,1)} %shard_map.450.refs_0_, bf16[1536,768]{1,0:T(8,128)(2,1)} %copy-done.17, bf16[1536,768]{1,0:T(8,128)(2,1)} %shard_map.451.refs_2_, ...), custom_call_target="tpu_custom_call" | custom-call | tf_op jit(solution)/shard_map/pallas_call | solution.py:47
  449.4 11.4 %shard_map.456 = (bf16[768,768]{1,0:T(8,128)(2,1)}, bf16[768,768]{1,0:T(8,128)(2,1)}, bf16[1536,384]{1,0:T(8,128)(2,1)}, bf16[1536,384]{1,0:T(8,128)(2,1)}, bf16...) custom-call(s32[1]{0:T(128)} %constant.415.clone.1.order_ref, ...), custom_call_target="tpu_custom_call" | custom-call | tf_op jit(solution)/shard_map/pallas_call | solution.py:47
  464.3 9.6 %all_to_all.72 = f32[4,2,608]{2,1,0:T(2,128)S(1)} all-to-all(f32[4,2,608]{2,1,0:T(2,128)S(1)} %broadcast_in_dim.189), channel_id=1, replica_groups=mesh['dp'=4,'row'=2,'col'=4] {'col'}, dimensions={0} | all-to-all | bytes 38912 | tf_op jit(solution)/shard_map/all_to_all | solution.py:359
  485.7 24.6 %collective-permute-done.37.refs_1_ = bf16[768,768]{1,0:T(8,128)(2,1)} collective-permute-done((bf16[768,768]{1,0:T(8,128)(2,1)}, bf16[768,768]{1,0:T(8,128)(2,1)}, u32[]{:S(2)}, u32[]{:S(2)}) %collective-permute-start.37) | collective-permute-done | bytes 1179680 | tf_op jit(solution)/shard_map/ppermute | solution.py:353
  510.5 15.3 %all-to-all-done.8.columns_ref = bf16[4,608,384]{2,1,0:T(8,128)(2,1)} async-done(((bf16[4,608,384]{2,1,0:T(8,128)(2,1)}), bf16[4,608,384]{2,1,0:T(8,128)(2,1)}, u32[]{:S(2)}, u32[]{:S(2)}) %all-to-all-start.8) | async-done | bytes 1867808 | tf_op jit(solution)/shard_map/all_to_all | solution.py:359
  539.8 9.9 %shard_map.459.inputs_ref = bf16[608,1152]{1,0:T(8,128)(2,1)} custom-call(s32[8]{0:T(128)} %stack.381.order_ref, bf16[608,1152]{1,0:T(8,128)(2,1)} %shard_map.438.packed_ref, bf16[608,384]{1,0:T(8,128)(2,1)} %get-tuple-element.287.inputs_ref.attended_ref, f32[6,608]{1,0:T(8,128)} %get-tuple-element.231.log_ref, bf16[608,384]{1,0:T(8,128)(2,1)} %shard_map.458.d_ref), custom_call_target="tpu_custom_call" | custom-call | tf_op jit(solution)/shard_map/pallas_call | solution.py:47
  558.0 15.2 %all-to-all-done.9 = bf16[4,608,384]{2,1,0:T(8,128)(2,1)} async-done(((bf16[4,608,384]{2,1,0:T(8,128)(2,1)}), bf16[4,608,384]{2,1,0:T(8,128)(2,1)}, u32[]{:S(2)}, u32[]{:S(2)}) %all-to-all-start.9) | async-done | bytes 1867808 | tf_op jit(solution)/shard_map/all_to_all | solution.py:359
  630.2 11.7 %collective-permute-done.52.refs_7_ = bf16[384,768]{1,0:T(8,128)(2,1)} collective-permute-done((bf16[384,768]{1,0:T(8,128)(2,1)}, bf16[384,768]{1,0:T(8,128)(2,1)}, u32[]{:S(2)}, u32[]{:S(2)}) %collective-permute-start.52) | collective-permute-done | bytes 589856 | tf_op jit(solution)/shard_map/ppermute | solution.py:353
  659.4 9.9 %collective-permute-done.45 = bf16[768,576]{0,1:T(8,128)(2,1)} collective-permute-done((bf16[768,576]{0,1:T(8,128)(2,1)}, bf16[768,576]{0,1:T(8,128)(2,1)}, u32[]{:S(2)}, u32[]{:S(2)}) %collective-permute-start.45) | collective-permute-done | bytes 884768 | tf_op jit(solution)/shard_map/ppermute | solution.py:353
  685.8 9.1 %collective-permute-done.54 = bf16[2,2,14,384]{3,2,1,0:T(8,128)(2,1)S(1)} collective-permute-done((bf16[2,2,14,384]{3,2,1,0:T(8,128)(2,1)S(1)}, bf16[2,2,14,384]{3,2,1,0:T(8,128)(2,1)S(1)}, u32[]{:S(2)}, u32[]{:S(2)}) %collective-permute-start.54) | collective-permute-done | bytes 43040 | tf_op jit(solution)/shard_map/ppermute | solution.py:350
  751.4 10.4 %collective-permute-start.68 = (bf16[192,384]{1,0:T(8,128)(2,1)}, bf16[192,384]{1,0:T(8,128)(2,1)S(1)}, u32[]{:S(2)}, u32[]{:S(2)}) collective-permute-start(bf16[192,384]{1,0:T(8,128)(2,1)} %get-tuple-element.373), channel_id=1, source_target_pairs={{0,2},{1,11},{2,16},{3,25},{8,0},{9,9},{10,18},{11,27},{16,1},{17,... | collective-permute-start | bytes 442376 | tf_op jit(solution)/shard_map/ppermute | solution.py:398
  769.7 14.6 %all-to-all-start.13 = ((bf16[2,4,96,1344]{3,2,0,1:T(8,128)(2,1)}), bf16[2,4,96,1344]{3,2,0,1:T(8,128)(2,1)}, u32[]{:S(2)}, u32[]{:S(2)}) async-start(bf16[2,4,96,1344]{3,2,0,1:T(8,128)(2,1)} %copy.304), calls=%async_computation.13 | async-start | bytes 4325376 | tf_op jit(solution)/shard_map/all_to_all | solution.py:408
  789.2 21.6 %all-to-all-done.13 = bf16[2,4,96,1344]{3,2,0,1:T(8,128)(2,1)} async-done(((bf16[2,4,96,1344]{3,2,0,1:T(8,128)(2,1)}), bf16[2,4,96,1344]{3,2,0,1:T(8,128)(2,1)}, u32[]{:S(2)}, u32[]{:S(2)}) %all-to-all-start.13) | async-done | bytes 2064416 | tf_op jit(solution)/shard_map/all_to_all | solution.py:408
  (625 shorter events, 446.3 us)
Async XLA Ops:
  49.3 73.0 %all-to-all-start.1 = ((bf16[4,608,384]{2,1,0:T(8,128)(2,1)}), bf16[4,608,384]{2,1,0:T(8,128)(2,1)}, u32[]{:S(2)}, u32[]{:S(2)}) async-start(bf16[4,608,384]{2,1,0:T(8,128)(2,1)} %broadcast_in_dim.175), calls=%async_computation.1 | async-start | bytes 3735552 | tf_op jit(solution)/shard_map/all_to_all | solution.py:359
  71.9 41.7 %collective-permute-start.6 = (bf16[768,576]{0,1:T(8,128)(2,1)S(1)}, bf16[768,576]{0,1:T(8,128)(2,1)S(1)}, u32[]{:S(2)}, u32[]{:S(2)}) collective-permute-start(bf16[768,576]{0,1:T(8,128)(2,1)S(1)} %copy.272), channel_id=1, source_target_pairs={{0,4},{4,0},{1,5},{5,1},{2,6},{6,2},{3,7},{7,3},{8,12},{12,8},{9,1... | collective-permute-start | bytes 2654216 | tf_op jit(solution)/shard_map/ppermute | solution.py:353
  73.5 45.2 %collective-permute-start.5 = (bf16[384,1152]{1,0:T(8,128)(2,1)}, bf16[384,1152]{1,0:T(8,128)(2,1)}, u32[]{:S(2)}, u32[]{:S(2)}) collective-permute-start(bf16[384,1152]{1,0:T(8,128)(2,1)} %shard_map.432.first_ref), channel_id=1, source_target_pairs={{0,16},{8,24},{16,0},{24,8},{1,17},{9,25},{17,1},{25,9},{2,18},{10... | collective-permute-start | bytes 2654216 | tf_op jit(solution)/shard_map/ppermute | solution.py:350
  178.7 73.4 %all-to-all-start.2 = ((bf16[4,608,384]{2,1,0:T(8,128)(2,1)}), bf16[4,608,384]{2,1,0:T(8,128)(2,1)}, u32[]{:S(2)}, u32[]{:S(2)}) async-start(bf16[4,608,384]{2,1,0:T(8,128)(2,1)} %shard_map.442), calls=%async_computation.2 | async-start | bytes 3735552 | tf_op jit(solution)/shard_map/all_to_all | solution.py:359
  187.5 64.7 %collective-permute-start.22 = (bf16[768,384]{1,0:T(8,128)(2,1)}, bf16[768,384]{1,0:T(8,128)(2,1)S(1)}, u32[]{:S(2)}, u32[]{:S(2)}) collective-permute-start(bf16[768,384]{1,0:T(8,128)(2,1)} %get-tuple-element.229), channel_id=1, source_target_pairs={{0,2},{1,3},{2,0},{3,1},{8,8},{9,9},{10,10},{11,11},{16,19},{17,16... | collective-permute-start | bytes 1769480 | tf_op jit(solution)/shard_map/ppermute | solution.py:340
  266.5 61.7 %all-to-all-start.4 = ((bf16[4,608,384]{2,1,0:T(8,128)(2,1)}), bf16[4,608,384]{2,1,0:T(8,128)(2,1)}, u32[]{:S(2)}, u32[]{:S(2)}) async-start(bf16[4,608,384]{2,1,0:T(8,128)(2,1)} %broadcast_in_dim.187), calls=%async_computation.4 | async-start | bytes 3735552 | tf_op jit(solution)/shard_map/all_to_all | solution.py:359
  270.9 47.5 %collective-permute-start.25 = (bf16[384,1536]{1,0:T(8,128)(2,1)}, bf16[384,1536]{1,0:T(8,128)(2,1)S(1)}, u32[]{:S(2)}, u32[]{:S(2)}) collective-permute-start(bf16[384,1536]{1,0:T(8,128)(2,1)} %shard_map.443.first_ref), channel_id=1, source_target_pairs={{0,16},{8,24},{16,0},{24,8},{1,17},{9,25},{17,1},{25,9},{2,18},{10... | collective-permute-start | bytes 3538952 | tf_op jit(solution)/shard_map/ppermute | solution.py:350
  271.8 51.5 %collective-permute-start.26 = (bf16[768,768]{1,0:T(8,128)(2,1)}, bf16[768,768]{1,0:T(8,128)(2,1)S(1)}, u32[]{:S(2)}, u32[]{:S(2)}) collective-permute-start(bf16[768,768]{1,0:T(8,128)(2,1)} %shard_map.444.first_ref), channel_id=1, source_target_pairs={{0,4},{4,0},{1,5},{5,1},{2,6},{6,2},{3,7},{7,3},{8,12},{12,8},{9,1... | collective-permute-start | bytes 3538952 | tf_op jit(solution)/shard_map/ppermute | solution.py:353
  272.4 38.1 %collective-permute-start.23 = (bf16[768,384]{1,0:T(8,128)(2,1)}, bf16[768,384]{1,0:T(8,128)(2,1)S(1)}, u32[]{:S(2)}, u32[]{:S(2)}) collective-permute-start(bf16[768,384]{1,0:T(8,128)(2,1)} %copy-done.50), channel_id=1, source_target_pairs={{0,4},{4,0},{1,5},{5,1},{2,6},{6,2},{3,7},{7,3},{8,12},{12,8},{9,1... | collective-permute-start | bytes 1769480 | tf_op jit(solution)/shard_map/ppermute | solution.py:353
  273.9 40.5 %collective-permute-start.24 = (bf16[768,384]{1,0:T(8,128)(2,1)S(1)}, bf16[768,384]{1,0:T(8,128)(2,1)S(1)}, u32[]{:S(2)}, u32[]{:S(2)}) collective-permute-start(bf16[768,384]{1,0:T(8,128)(2,1)S(1)} %collective-permute-done.22.first_ref), channel_id=1, source_target_pairs={{0,16},{8,24},{16,0},{24,8},{1,17},{9,25},{17,1},{25,9},{2,18},{10... | collective-permute-start | bytes 1769480 | tf_op jit(solution)/shard_map/ppermute | solution.py:350
  329.6 53.5 %all-to-all-start.5 = ((bf16[4,608,384]{2,1,0:T(8,128)(2,1)}), bf16[4,608,384]{2,1,0:T(8,128)(2,1)}, u32[]{:S(2)}, u32[]{:S(2)}) async-start(bf16[4,608,384]{2,1,0:T(8,128)(2,1)} %broadcast_in_dim.188), calls=%async_computation.5 | async-start | bytes 3735552 | tf_op jit(solution)/shard_map/all_to_all | solution.py:359
  334.6 36.7 %collective-permute-start.27 = (bf16[768,1536]{1,0:T(8,128)(2,1)}, bf16[768,1536]{1,0:T(8,128)(2,1)}, u32[]{:S(2)}, u32[]{:S(2)}) collective-permute-start(bf16[768,1536]{1,0:T(8,128)(2,1)} %shard_map.447.refs_0_), channel_id=1, source_target_pairs={{0,8},{8,0},{16,24},{24,16},{1,9},{9,1},{17,25},{25,17},{2,10},{10... | collective-permute-start | bytes 7077896 | tf_op jit(solution)/shard_map/ppermute | solution.py:350
  334.7 36.6 %collective-permute-start.28 = (bf16[768,1536]{1,0:T(8,128)(2,1)}, bf16[768,1536]{1,0:T(8,128)(2,1)}, u32[]{:S(2)}, u32[]{:S(2)}) collective-permute-start(bf16[768,1536]{1,0:T(8,128)(2,1)} %shard_map.448.refs_2_), channel_id=1, source_target_pairs={{0,8},{8,0},{16,24},{24,16},{1,9},{9,1},{17,25},{25,17},{2,10},{10... | collective-permute-start | bytes 7077896 | tf_op jit(solution)/shard_map/ppermute | solution.py:350
  412.9 48.9 %all-to-all-start.6 = ((bf16[4,608,384]{2,1,0:T(8,128)(2,1)}), bf16[4,608,384]{2,1,0:T(8,128)(2,1)}, u32[]{:S(2)}, u32[]{:S(2)}) async-start(bf16[4,608,384]{2,1,0:T(8,128)(2,1)} %shard_map.453), calls=%async_computation.6 | async-start | bytes 3735552 | tf_op jit(solution)/shard_map/all_to_all | solution.py:359
  479.0 46.8 %all-to-all-start.8 = ((bf16[4,608,384]{2,1,0:T(8,128)(2,1)}), bf16[4,608,384]{2,1,0:T(8,128)(2,1)}, u32[]{:S(2)}, u32[]{:S(2)}) async-start(bf16[4,608,384]{2,1,0:T(8,128)(2,1)} %broadcast_in_dim.190), calls=%async_computation.8 | async-start | bytes 3735552 | tf_op jit(solution)/shard_map/all_to_all | solution.py:359
  525.8 47.4 %all-to-all-start.9 = ((bf16[4,608,384]{2,1,0:T(8,128)(2,1)}), bf16[4,608,384]{2,1,0:T(8,128)(2,1)}, u32[]{:S(2)}, u32[]{:S(2)}) async-start(bf16[4,608,384]{2,1,0:T(8,128)(2,1)} %shard_map.457), calls=%async_computation.9 | async-start | bytes 3735552 | tf_op jit(solution)/shard_map/all_to_all | solution.py:359
  573.2 49.4 %all-to-all-start.10 = ((bf16[4,608,384]{2,1,0:T(8,128)(2,1)}), bf16[4,608,384]{2,1,0:T(8,128)(2,1)}, u32[]{:S(2)}, u32[]{:S(2)}) async-start(bf16[4,608,384]{2,1,0:T(8,128)(2,1)} %shard_map.460), calls=%async_computation.10 | async-start | bytes 3735552 | tf_op jit(solution)/shard_map/all_to_all | solution.py:359
  697.4 50.5 %collective-permute-start.64 = (bf16[384,768]{1,0:T(8,128)(2,1)}, bf16[384,768]{1,0:T(8,128)(2,1)S(1)}, u32[]{:S(2)}, u32[]{:S(2)}) collective-permute-start(bf16[384,768]{1,0:T(8,128)(2,1)} %get-tuple-element.369), channel_id=1, source_target_pairs={{0,0},{1,1},{2,2},{3,3},{8,10},{9,11},{10,8},{11,9},{16,19},{17,16... | collective-permute-start | bytes 1769480 | tf_op jit(solution)/shard_map/ppermute | solution.py:345
  699.2 50.6 %collective-permute-start.65 = (bf16[384,768]{1,0:T(8,128)(2,1)}, bf16[384,768]{1,0:T(8,128)(2,1)S(1)}, u32[]{:S(2)}, u32[]{:S(2)}) collective-permute-start(bf16[384,768]{1,0:T(8,128)(2,1)} %get-tuple-element.370), channel_id=1, source_target_pairs={{0,2},{1,3},{2,0},{3,1},{8,8},{9,9},{10,10},{11,11},{16,17},{17,18... | collective-permute-start | bytes 1769480 | tf_op jit(solution)/shard_map/ppermute | solution.py:345
  704.0 83.0 %collective-permute-start.67 = (bf16[768,384]{1,0:T(8,128)(2,1)}, bf16[768,384]{1,0:T(8,128)(2,1)S(1)}, u32[]{:S(2)}, u32[]{:S(2)}) collective-permute-start(bf16[768,384]{1,0:T(8,128)(2,1)} %get-tuple-element.372), channel_id=1, source_target_pairs={{0,0},{1,9},{2,18},{3,27},{8,2},{9,11},{10,16},{11,25},{16,3},{17,... | collective-permute-start | bytes 1769480 | tf_op jit(solution)/shard_map/ppermute | solution.py:398
  719.5 50.2 %all-to-all-start.12 = ((f32[4,2,2,768]{3,2,1,0:T(2,128)}), f32[4,2,2,768]{3,2,1,0:T(2,128)S(1)}, u32[]{:S(2)}, u32[]{:S(2)}) async-start(f32[4,2,2,768]{3,2,1,0:T(2,128)} %broadcast_in_dim.194), calls=%async_computation.12 | async-start | bytes 98304 | tf_op jit(solution)/shard_map/all_to_all | solution.py:359
  730.2 36.3 %collective-permute-start.63 = (bf16[384,576]{1,0:T(8,128)(2,1)}, bf16[384,576]{1,0:T(8,128)(2,1)}, u32[]{:S(2)}, u32[]{:S(2)}) collective-permute-start(bf16[384,576]{1,0:T(8,128)(2,1)} %get-tuple-element.368), channel_id=1, source_target_pairs={{0,2},{1,3},{2,0},{3,1},{8,8},{9,9},{10,10},{11,11},{16,17},{17,18... | collective-permute-start | bytes 1327112 | tf_op jit(solution)/shard_map/ppermute | solution.py:345
  747.9 40.3 %collective-permute-start.69 = (bf16[768,384]{1,0:T(8,128)(2,1)}, bf16[768,384]{1,0:T(8,128)(2,1)S(1)}, u32[]{:S(2)}, u32[]{:S(2)}) collective-permute-start(bf16[768,384]{1,0:T(8,128)(2,1)} %get-tuple-element.374), channel_id=1, source_target_pairs={{0,2},{1,11},{2,16},{3,25},{8,0},{9,9},{10,18},{11,27},{16,1},{17,... | collective-permute-start | bytes 1769480 | tf_op jit(solution)/shard_map/ppermute | solution.py:398
  769.7 41.1 %all-to-all-start.13 = ((bf16[2,4,96,1344]{3,2,0,1:T(8,128)(2,1)}), bf16[2,4,96,1344]{3,2,0,1:T(8,128)(2,1)}, u32[]{:S(2)}, u32[]{:S(2)}) async-start(bf16[2,4,96,1344]{3,2,0,1:T(8,128)(2,1)} %copy.304), calls=%async_computation.13 | async-start | bytes 4325376 | tf_op jit(solution)/shard_map/all_to_all | solution.py:408
  (144 other events, 1792.6 us)

commit v3 on v2

--- a/solution.py
+++ b/solution.py
@@ -154,31 +154,27 @@
     return 3 if all(extent % (3 * tile) == 0 for extent in extents) else 1
 
 
-def beside(first, second, axis):
-    shape = list(first.shape)
-    shape[axis] *= 2
-    half = first.shape[axis]
-    steps = steps_for([first.shape[1 - axis]], axis == 0)
-    other = first.shape[1 - axis] // steps
-    spec = on_columns if axis == 0 else on_rows
-
-    def block(rows, columns):
-        return spec((rows, other) if axis == 0 else (other, columns))
-
-    def body(order_ref, first_ref, second_ref, out_ref):
-        if axis == 0:
-            out_ref[:half] = first_ref[...]
-            out_ref[half:] = second_ref[...]
-        else:
-            out_ref[...] = jnp.concatenate([first_ref[...], second_ref[...]], axis=1)
-
+def assemble(groups):
+    shapes = [(2 * group[0].shape[0], 2 * group[0].shape[1]) for group in groups]
+
+    def body(order_ref, *refs):
+        for item, (rows, _) in enumerate(shapes):
+            out_ref = refs[4 * len(groups) + item]
+            for side in range(2):
+
+                @pl.when(pl.program_id(0) == side)
+                def _():
+                    out_ref[: rows // 2] = refs[4 * item + side][...]
+                    out_ref[rows // 2 :] = refs[4 * item + 2 + side][...]
+
+    flat = [array for group in groups for array in group]
     return call(
         body,
-        (steps,),
-        [block(*first.shape)] * 2,
-        block(*shape),
-        jax.ShapeDtypeStruct(tuple(shape), first.dtype),
-        (jnp.zeros((1,), jnp.int32), first, second),
+        (2,),
+        [whole(array.shape) for array in flat],
+        [on_columns((rows, columns // 2)) for rows, columns in shapes],
+        [jax.ShapeDtypeStruct(shape, BF) for shape in shapes],
+        (jnp.zeros((1,), jnp.int32), *flat),
     )
 
 
@@ -231,6 +227,91 @@
         [jax.ShapeDtypeStruct(pair[0].shape, BF) for pair in pairs],
         (jnp.zeros((1,), jnp.int32), *[array for pair in pairs for array in pair]),
     )
+
+
+def unpack(fronts, width, by_row_first):
+    rows, columns = fronts[0].shape[0] // 4, fronts[0].shape[1]
+    deep = rows - width
+
+    def body(order_ref, *refs):
+        shorter = rows - width
+        for stream, by_row in enumerate(by_row_first):
+            front_ref, qkv_ref, out_ref = refs[stream], refs[2 + 2 * stream], refs[3 + 2 * stream]
+            for block in range(2):
+                qkv_halves = []
+                for half in range(2):
+                    start = rows * (2 * block + half if by_row else 2 * half + block)
+                    qkv_halves.append(front_ref[start : start + width])
+                    lanes = slice(block * width, (block + 1) * width)
+                    out_ref[half * shorter : (half + 1) * shorter, lanes] = front_ref[
+                        start + width : start + rows, :width
+                    ]
+                qkv_ref[block * width : (block + 1) * width] = jnp.concatenate(qkv_halves, axis=1)
+
+    shapes = [(2 * width, 2 * columns), (2 * deep, 2 * width)] * 2
+    return call(
+        body,
+        (1,),
+        [whole(front.shape) for front in fronts],
+        [whole(shape) for shape in shapes],
+        [jax.ShapeDtypeStruct(shape, BF) for shape in shapes],
+        (jnp.zeros((1,), jnp.int32), *fronts),
+    )
+
+
+def rows_for(values, rows):
+    gap = rows - values.shape[-2]
+    return jnp.pad(values, [(0, 0)] * (values.ndim - 2) + [(0, gap), (0, 0)])
+
+
+def modulation_grads(act, d_mod, mod_rows):
+    sequences, count = act.shape
+    width = d_mod.shape[-1]
+    act = act.astype(F32)
+    d_mod = jnp.moveaxis(d_mod, 0, 2).astype(F32).reshape(-1, sequences, width)
+
+    def body(order_ref, act_ref, d_ref, *refs):
+        for stream in range(2):
+            d_row = d_ref[stream * mod_rows + pl.program_id(0)].astype(BF)
+            refs[stream][0] = transposed_left(act_ref[...].astype(BF), d_row)
+
+    spec = pl.BlockSpec((1, count, width), lambda step, order: (step, 0, 0))
+    grads = call(
+        body,
+        (mod_rows,),
+        [whole(act.shape), whole(d_mod.shape)],
+        [spec] * 2,
+        [jax.ShapeDtypeStruct((mod_rows, count, width), F32)] * 2,
+        (jnp.zeros((1,), jnp.int32), act, d_mod),
+    )
+    return [jnp.transpose(grad, (1, 0, 2))[None] for grad in grads]
+
+
+def condition_part(d_mod, weights):
+    sequences, _, mod_rows, width = d_mod.shape
+    inputs = weights[0].shape[0]
+    d_mod = jnp.moveaxis(d_mod, 0, 2).astype(F32).reshape(-1, sequences, width)
+    d_mod = rows_for(d_mod, 8)
+
+    def body(order_ref, d_ref, image_ref, text_ref, out_ref):
+        @pl.when(pl.program_id(0) == 0)
+        def _():
+            out_ref[...] = jnp.zeros_like(out_ref)
+
+        for stream, weight_ref in enumerate((image_ref, text_ref)):
+            d_row = d_ref[stream * mod_rows + pl.program_id(0)].astype(BF)
+            out_ref[...] += transposed_right(d_row, weight_ref[0])
+
+    spec = pl.BlockSpec((1, inputs, width), lambda step, order: (step, 0, 0))
+    total = call(
+        body,
+        (mod_rows,),
+        [whole(d_mod.shape), spec, spec],
+        whole((8, inputs)),
+        jax.ShapeDtypeStruct((8, inputs), F32),
+        (jnp.zeros((1,), jnp.int32), d_mod, *[jnp.transpose(w, (1, 0, 2)) for w in weights]),
+    )
+    return total[:sequences]
 
 
 def head_parts(packed_ref, head, size):
@@ -352,6 +433,12 @@
     def swap_row(self, values):
         return lax.ppermute(values, "row", [(0, 1), (1, 0)])
 
+    def col_others(self, values):
+        return [
+            lax.ppermute(values, "col", [(c, (c + shift) % self.cols) for c in range(self.cols)])
+            for shift in range(1, self.cols)
+        ]
+
     def copies(self, values):
         return jnp.broadcast_to(values[None], (self.cols, *values.shape))
 
@@ -388,42 +475,32 @@
             bit //= 2
         return total.astype(BF)
 
-    def place_rows(self, parts):
+    def place(self, by_cols, by_rows):
         share = self.dps // self.cols
-        placed = []
-        for stream, part in enumerate(parts):
+        cols_placed, rows_placed = [], []
+        for stream, (wide, tall) in enumerate(zip(by_cols, by_rows)):
             pairs = self.along_plane(
                 lambda d, c: (c * share + d // self.cols, c - self.hop(d, 0, stream))
             )
-            placed.append(lax.ppermute(self.fold_rest(part), PLANE, pairs))
-        return placed
-
-    def place_cols(self, parts):
-        return [self.bring_back(part, stream) for stream, part in enumerate(parts)]
-
-    def place_cols_end(self, groups):
-        widths = [group[0].shape[1] for group in groups]
-        moved = jnp.concatenate([jnp.stack(group) for group in groups], axis=2)
-        moved = moved.reshape(moved.shape[0], self.dps, -1, moved.shape[2])
-        from_dp = lax.all_to_all(moved, "dp", 1, 1, tiled=True).astype(F32)
-        from_low = from_dp.reshape(from_dp.shape[0], -1, self.cols, *from_dp.shape[2:])
-        from_low = jnp.sum(from_low, axis=1)
-        placed = []
-        for place in range(self.cols):
-            streams = []
-            for stream in (IMAGE, TEXT):
-                hops = ((place - self.col) % self.cols) ^ (2 * stream)
-                low = (hops % 2) * 2 + hops // 2
-                streams.append(lax.dynamic_index_in_dim(from_low[stream], low, 0, False))
-            placed.append(jnp.stack(streams))
-        results, start = [], 0
-        for width in widths:
-            whole_rows = jnp.concatenate(
-                [item[:, :, start : start + width] for item in placed], axis=2
-            )
-            results.append([whole_rows[s][None] for s in range(whole_rows.shape[0])])
-            start += width
-        return results
+            rest = self.fold_rest(tall)
+            both = jnp.concatenate([wide, rest.reshape(-1, wide.shape[1])])
+            moved = lax.ppermute(both, PLANE, pairs)
+            cols_placed.append(moved[: wide.shape[0]])
+            rows_placed.append(moved[wide.shape[0] :].reshape(rest.shape))
+        return cols_placed, rows_placed
+
+    def place_end(self, parts):
+        moved = jnp.stack(parts)
+        moved = moved.reshape(len(parts), self.dps, -1, moved.shape[2])
+        return lax.all_to_all(moved, "dp", 1, 1, tiled=True)
+
+    def placed(self, moved):
+        total = moved.astype(F32).reshape(moved.shape[0], self.cols, -1, *moved.shape[2:])
+        total = jnp.sum(total, axis=2)
+        return [
+            jnp.concatenate([part[col] for col in range(self.cols)], axis=1)[None]
+            for part in total
+        ]
 
 
 def after(values, *earlier):
@@ -447,7 +524,7 @@
     mean = jnp.mean(everyone[:, 0], axis=0)
     squares = jnp.sum(everyone[:, 1] + width * (everyone[:, 0] - mean) ** 2, axis=0)
     inv_std = lax.rsqrt(squares / (width * grid.cols) + EPS)
-    return ((values - mean[:, None]) * inv_std[:, None], inv_std[:, None])
+    return ((values - mean[:, None]) * inv_std[:, None], inv_std[:, None], everyone)
 
 
 def norm_backward(grid, grad_hat, normed, inv_std):
@@ -498,13 +575,6 @@
     mod_weights = (image_mod_weight, text_mod_weight)
     mod_rows = image_mod_weight.shape[0]
 
-    def join(parts):
-        return jnp.concatenate(parts, axis=0)
-
-    def padded(parts):
-        zeros = jnp.zeros((padding, col_width), F32)
-        return join([part.astype(F32) for part in parts] + [zeros])
-
     def rows_of(values):
         return (values[:split], values[split:])
 
@@ -519,13 +589,16 @@
     def fetch(parts):
         return [grid.spread(part, s) for s, part in enumerate(parts)]
 
-    def fetch_pairs(parts, axis, first):
-        pairs = []
+    def fetch_even(parts, axis):
+        groups = []
         for s in streams:
-            by_row = by_row_first[s] == first
-            other = grid.move(parts[s], by_row)
-            pairs.append(beside(parts[s], other, axis if by_row else 1 - axis))
-        return pairs
+            by_row = by_row_first[s]
+            first, second = grid.move(parts[s], by_row), grid.move(parts[s], not by_row)
+            corner = grid.move(first, not by_row)
+            row_other, block_other = (first, second) if by_row else (second, first)
+            edges = (row_other, block_other) if axis == 1 else (block_other, row_other)
+            groups.append((parts[s], *edges, corner))
+        return assemble(groups)
 
     def fetch_last(evens):
         return [(even, grid.swap_dp(even, 1)) for even in evens]
@@ -551,10 +624,22 @@
         sums = add_up([pair for group in groups for pair in group])
         return [sums[2 * group : 2 * group + 2] for group in range(len(groups))]
 
+    def join(parts):
+        return jnp.concatenate(parts, axis=0)
+
     qkv_pieces = pieces((image_qkv_weight, text_qkv_weight), 1)
-    qkv_mine = fetch(qkv_pieces)
-    qkv_pair = fetch_pairs(qkv_mine, 1, True)
-    image_in, text_in, condition = after((image_in, text_in, condition), qkv_pieces)
+    out_pieces = pieces((image_out_weight, text_out_weight), 0)
+    front_pieces = [
+        join([qkv_piece, jnp.pad(out_piece, ((0, 0), (0, qkv_piece.shape[1] - col_width)))])
+        for qkv_piece, out_piece in zip(qkv_pieces, out_pieces)
+    ]
+    front_mine = fetch(front_pieces)
+    front_other = [grid.move(front_mine[s], by_row_first[s]) for s in streams]
+    image_in, text_in, condition = after((image_in, text_in, condition), front_pieces)
+
+    def padded(parts):
+        zeros = jnp.zeros((padding, col_width), F32)
+        return join([part.astype(F32) for part in parts] + [zeros])
 
     act_cond = (condition * jax.nn.sigmoid(condition)).astype(BF)
     partial_mod = jnp.stack(
@@ -573,7 +658,10 @@
     )
     to_row = [values.reshape(-1, col_width) for values in (other_mod, own_qv, own_up)]
     cuts = (to_row[0].shape[0], to_row[0].shape[0] + to_row[1].shape[0])
-    from_row = jnp.split(grid.swap_row(after(jnp.concatenate(to_row), qkv_mine)), cuts)
+    values = padded([image_in, text_in])
+    xhat1, inv1, statistics = norm_forward(grid, values)
+    to_row = after(jnp.concatenate(to_row), front_mine, statistics)
+    from_row = jnp.split(grid.swap_row(to_row), cuts)
     modulation = own_mod + from_row[0].reshape(own_mod.shape)
     modulation = modulation + jnp.stack([image_mod_bias, text_mod_bias])
 
@@ -615,69 +703,64 @@
         refs[1][rows] = d_hidden
         refs[2][stream : stream + 1] = jnp.sum(d_hidden.astype(F32), axis=0, keepdims=True)
 
-    values = padded([image_in, text_in])
-    xhat1, inv1 = norm_forward(grid, values)
     scale1 = 1.0 + field(1)
     normed1_own = (xhat1 * scale1 + field(0)).astype(BF)
-    normed1_copies = after(grid.copies(normed1_own), qkv_mine)
+    normed1_copies = after(grid.copies(normed1_own), front_mine)
     normed1 = grid.exchange(normed1_copies)
-    qkv_even = fetch_pairs(after(qkv_pair, normed1_copies), 1, False)
-    late_weights = after(
-        (
-            (image_out_weight, text_out_weight),
-            (image_up_weight, text_up_weight),
-            (image_down_weight, text_down_weight),
-        ),
-        qkv_mine,
-    )
-    out_mine = fetch(pieces(late_weights[0], 0))
-    up_pieces = pieces(late_weights[1], 1)
-    down_pieces = pieces(late_weights[2], 0)
-    out_pair = fetch_pairs(after(out_mine, normed1_copies), 0, True)
-    normed1, qkv_even, out_pair, up_pieces, down_pieces = lax.optimization_barrier(
-        (normed1, qkv_even, out_pair, up_pieces, down_pieces)
-    )
-    out_even = fetch_pairs(out_pair, 0, False)
-    qkv_w = fetch_last(qkv_even)
+    front_pairs = [
+        join([mine, other])
+        for mine, other in zip(front_mine, after(front_other, normed1_copies))
+    ]
+    front_even = [
+        join([front_pairs[s], grid.move(front_pairs[s], not by_row_first[s])]) for s in streams
+    ]
+    up_weights, down_weights = after(
+        ((image_up_weight, text_up_weight), (image_down_weight, text_down_weight)), front_mine
+    )
+    up_pieces, down_pieces = pieces(up_weights, 1), pieces(down_weights, 0)
     up_mine = fetch(up_pieces)
+    grad_out = padded([image_cotangent, text_cotangent])
+    gate2 = field(5)
+    d_branch2_own = (grad_out * gate2).astype(BF)
+    d_branch2_copies = grid.copies(after(d_branch2_own, normed1_copies))
+    normed1, front_even, up_mine, down_pieces, d_branch2_copies = lax.optimization_barrier(
+        (normed1, front_even, up_mine, down_pieces, d_branch2_copies)
+    )
+    front_odd = [grid.swap_dp(even, 1) for even in front_even]
+    evens = unpack(front_even, col_width, by_row_first)
+    odds = unpack(front_odd, col_width, by_row_first)
+    qkv_w = [(evens[2 * s], odds[2 * s]) for s in streams]
+    out_w = [(evens[2 * s + 1], odds[2 * s + 1]) for s in streams]
     down_mine = fetch(down_pieces)
+    d_branch2 = grid.exchange(d_branch2_copies)
     tokens = values.shape[0]
     (packed,) = mix(
         normed1, qkv_w, order, split, False, [bias_rows], [(tokens, BF)], add_bias
     )
     attn, log_total = attend(packed, order, head_size, count)
-    out_w = fetch_last(after(out_even, packed))
     attn_out = parts(attn, out_w, order, split, False)
-    attn_out, up_mine = lax.optimization_barrier((attn_out, up_mine))
+    attn_out, up_mine, down_mine, d_branch2 = lax.optimization_barrier(
+        (attn_out, up_mine, down_mine, d_branch2)
+    )
     parts_out = grid.exchange(attn_out)
-    up_pair = fetch_pairs(up_mine, 1, True)
-    parts_out, up_pair, down_mine = lax.optimization_barrier((parts_out, up_pair, down_mine))
+    up_even = fetch_even(up_mine, 1)
+    parts_out, up_even, down_mine = lax.optimization_barrier((parts_out, up_even, down_mine))
     branch1 = with_bias(column_sum(parts_out), out_bias)
 
     gate1 = field(2)
     middle = values + gate1 * branch1
-    xhat2, inv2 = norm_forward(grid, middle)
+    xhat2, inv2, _ = norm_forward(grid, middle)
     scale2 = 1.0 + field(4)
-    gate2 = field(5)
     normed2_copies = grid.copies((xhat2 * scale2 + field(3)).astype(BF))
     normed2 = grid.exchange(normed2_copies)
-    grad_out = padded([image_cotangent, text_cotangent])
-    d_branch2_own = (grad_out * gate2).astype(BF)
-    d_branch2_copies = grid.copies(after(d_branch2_own, normed2_copies))
-    up_even = fetch_pairs(up_pair, 1, False)
-    down_pair = fetch_pairs(down_mine, 0, True)
-    normed2, down_pair, d_branch2_copies, up_even = lax.optimization_barrier(
-        (normed2, down_pair, d_branch2_copies, up_even)
-    )
-    d_branch2 = grid.exchange(d_branch2_copies)
     up_w = fetch_last(up_even)
-    down_even = fetch_pairs(down_pair, 0, False)
+    down_even = fetch_even(after(down_mine, normed2_copies), 0)
+    normed2, up_w, down_even = lax.optimization_barrier((normed2, up_w, down_even))
+    down_w = fetch_last(down_even)
     gelu, slope = mix(
         normed2, up_w, order, split, False, [up_bias], [(tokens, BF), (tokens, F32)], into_gelu
     )
 
-    d_branch2, gelu, down_even = lax.optimization_barrier((d_branch2, gelu, down_even))
-    down_w = fetch_last(down_even)
     d_hidden, up_sums = mix(
         d_branch2, down_w, order, split, True, [slope], [(tokens, BF), (2, F32)], times_slope
     )
@@ -699,23 +782,25 @@
     d_branch1_own = (d_middle * gate1).astype(BF)
     d_branch1 = grid.exchange(grid.copies(d_branch1_own))
     down_fold, up_fold = folds
-    d_branch1, gelu_down, down_fold = lax.optimization_barrier((d_branch1, gelu_down, down_fold))
+    d_branch1, gelu_down, down_fold, up_fold = lax.optimization_barrier(
+        (d_branch1, gelu_down, down_fold, up_fold)
+    )
     parts_branch2 = grid.exchange(gelu_down)
     (d_attn,) = mix(d_branch1, out_w, order, split, True, [], [(tokens, BF)], keep_bf16)
-    down_fold = move(fold([down_fold], (0,), False), False)
+    folds = move(fold([down_fold, up_fold], (0, 1), False), False)
     d_qkv = attend_back(packed, attn, log_total, d_attn, order, head_size, count)
     qkv_back = parts(d_qkv, qkv_w, order, split, True)
-    qkv_back, parts_branch2, up_fold = lax.optimization_barrier((qkv_back, parts_branch2, up_fold))
-    folds = down_fold + move(fold([up_fold], (1,), False), False)
+    qkv_back, parts_branch2, folds = lax.optimization_barrier((qkv_back, parts_branch2, folds))
+    down_fold, up_fold = fold_end(folds)
     parts_normed1 = grid.exchange(qkv_back)
     d_qkv_late, attn_late = after((d_qkv, attn), qkv_back)
     qkv_fold = fold_core(weight_grads(normed1, d_qkv_late, order, split, True))
     out_fold = fold_core(weight_grads(d_branch1, attn_late, order, split, False))
     late_folds = fold([qkv_fold, out_fold], (1, 0), True)
     parts_normed1, late_folds = lax.optimization_barrier((parts_normed1, late_folds))
-    folds = after(folds, parts_normed1)
+    down_fold, up_fold = after((down_fold, up_fold), parts_normed1)
+    up_placed, down_placed = grid.place(up_fold, down_fold)
     late_folds = move(late_folds, True)
-    down_fold, up_fold = fold_end(folds)
     d_normed1 = column_sum(parts_normed1)
     d_shift1 = token_sums(d_normed1)
     d_scale1 = token_sums(d_normed1 * xhat1)
@@ -723,12 +808,6 @@
     branch2 = with_bias(column_sum(parts_branch2), down_bias)
     outputs = unpadded((middle + gate2 * branch2).astype(BF))
     d_gate2 = token_sums(grad_out * branch2)
-    norm_back1, late_folds, down_fold, up_fold, d_gate2 = lax.optimization_barrier(
-        (norm_back1, late_folds, down_fold, up_fold, d_gate2)
-    )
-    down_placed, up_placed = grid.place_rows(down_fold), grid.place_cols(up_fold)
-    late_folds = move(fold(late_folds, (1, 0), False), False)
-
     head_sums = token_sums(d_qkv.astype(F32))
     head_sums = head_sums.reshape(2, 2, heads, 3, head_size)
     head_sums = jnp.stack([head_sums[:, :, :, 0], head_sums[:, :, :, 2]], axis=3)
@@ -749,9 +828,17 @@
         everyone = jnp.concatenate([everyone, grid.swap_dp(everyone, bit)])
         act_all = jnp.concatenate([act_all, grid.swap_dp(after(act_all, vectors), bit)])
         bit //= 2
-    everyone, late_folds = lax.optimization_barrier((everyone, late_folds))
+    norm_back1, late_folds, everyone, act_all = lax.optimization_barrier(
+        (norm_back1, late_folds, everyone, act_all)
+    )
+    late_folds = move(fold(late_folds, (1, 0), False), False)
+    late_folds, up_placed, down_placed = lax.optimization_barrier(
+        (late_folds, up_placed, down_placed)
+    )
     qkv_fold, out_fold = fold_end(late_folds)
-    qkv_placed, out_placed = grid.place_cols(qkv_fold), grid.place_rows(out_fold)
+    qkv_placed, out_placed = grid.place(qkv_fold, out_fold)
+    up_moved = grid.place_end(up_placed)
+
     in_grads = unpadded(d_middle + norm_back1)
     vector_sums = jnp.sum(everyone.astype(F32), axis=0)
     feature_share = col_width // grid.dps
@@ -773,25 +860,22 @@
     d_mod = jnp.where(grid.row == 0, by_row, by_row[:, ::-1]).reshape(-1, 2, 6, col_width)
     mod_share = mod_rows // grid.dps
     act_share = lax.dynamic_slice_in_dim(act_all, grid.dp * mod_share, mod_share, 1)
-    mod_w_grad = [
-        jnp.stack([transposed_left(act_share, d_mod[:, s, j]) for j in range(6)], axis=1)[None]
-        for s in streams
-    ]
-    own_d_mod = d_mod[:seq_count]
-    cond_part = sum(
-        transposed_right(own_d_mod[:, s, j], mod_weights[s][:, j])
-        for s in streams
-        for j in range(6)
-    )
-    lasts = grid.everyone(jnp.stack([cond_part, up_total_own]))
-    cond_sum = jnp.sum(lasts[:, 0], axis=0)
+    mod_w_grad = modulation_grads(after(act_share, late_folds), d_mod, 6)
+    own_d_mod = after(d_mod[:seq_count], late_folds)
+    cond_part = condition_part(own_d_mod, mod_weights)
+    last = jnp.stack([cond_part, up_total_own])
+    lasts = [last] + grid.col_others(last)
+    lasts, qkv_placed, out_placed, up_moved = lax.optimization_barrier(
+        (lasts, qkv_placed, out_placed, up_moved)
+    )
+    qkv_moved = grid.place_end(qkv_placed)
+    cond_sum = sum(item[0] for item in lasts)
     up_share = up_count * grid.cols // grid.dps
-    up_chosen = lax.dynamic_index_in_dim(
-        lasts[:, 1], grid.dp * grid.cols // grid.dps, 0, False
-    )
+    up_from = (grid.col - grid.dp * grid.cols // grid.dps) % grid.cols
+    up_chosen = sum(jnp.where(up_from == j, lasts[j][1], 0.0) for j in range(grid.cols))
     up_start = (grid.dp % (grid.dps // grid.cols)) * up_share
     up_b_grad = lax.dynamic_slice_in_dim(up_chosen, up_start, up_share, 1)
-    qkv_total, up_total = grid.place_cols_end([qkv_placed, up_placed])
+    qkv_total, up_total = grid.placed(qkv_moved), grid.placed(up_moved)
     down_total = [down_placed[s].astype(F32)[None] for s in streams]
     out_total = [out_placed[s].astype(F32)[None] for s in streams]
     sigmoid_cond = jax.nn.sigmoid(condition)

time: 840 us -> 779 us (0.927)
  waiting for transfers between devices: 292 us -> 210 us
  local copies, waits for them, and re-layouts: 60.7 us -> 104 us
  other arithmetic: 43 us -> 70.3 us
  matrix products: 33.4 us -> 8.88 us
  Pallas kernels: 207 us -> 185 us
  blocking collectives: 28.9 us -> 19.7 us
  starting transfers between devices: 156 us -> 165 us
    ppermute x8 -> x6, waiting for transfers between devices: 83.6 us -> 20.6 us  [spread(): lax.ppermute(values, PLANE, self.along_plane(lambda d, c: (d, c + self.ho...]
    ppermute x36 -> x34, waiting for transfers between devices: 59.1 us -> 95.1 us  [swap_dp(): return lax.ppermute(values, 'dp', [(d, d ^ bit) for d in range(self.dps)])]
    all_to_all x10, waiting for transfers between devices: 32.4 us -> 2.37 us  [exchange(): return lax.all_to_all(values, 'col', 0, 0, tiled=True)]
    dot_general x24 -> x0, matrix products: 22.4 us -> none  [the longest x12 11.5 us: transposed_left(): lax.dot_general(left_side, right_side, (((0,), (0,)), ((), ())), preferre...]
    pallas_call x37 -> x26, Pallas kernels: 207 us -> 185 us  [call(): pl.pallas_call(body, grid_spec=pltpu.PrefetchScalarGridSpec(num_scalar_pr...]
    concatenate x3 -> x11, other arithmetic: 3.72 us -> 19.8 us  [the longest x6 13.4 us: join(): return jnp.concatenate(parts, axis=0)]
    all_to_all x1 -> x2, waiting for transfers between devices: 21.6 us -> 7.79 us  [place_end(): return lax.all_to_all(moved, 'dp', 1, 1, tiled=True)]
    ppermute x8 -> x6, starting transfers between devices: 21 us -> 34.3 us  [spread(): lax.ppermute(values, PLANE, self.along_plane(lambda d, c: (d, c + self.ho...]
  transfers between devices with their start and end apart: 81 -> 77, of which waited for: 27 -> 31; matrix products, arithmetic and copies ran while one was open for 11% -> 18% of each run, Pallas kernels for 22% -> 21%
where the time goes in v3:
time: 779 us; the launch traced here: 767 us
  waiting for transfers between devices  210 us (27%)
  Pallas kernels  185 us (24%)
  starting transfers between devices  165 us (21%)
  local copies, waits for them, and re-layouts  104 us (13%)
  other arithmetic  70.3 us (9%)
  blocking collectives  19.7 us (3%)
  matrix products  8.88 us (1%)
    pallas_call x26, Pallas kernels, call(): pl.pallas_call(body, grid_spec=pltpu.PrefetchScalarGridSpec(num_scalar_pr...  185 us
    ppermute x34, waiting for transfers between devices, swap_dp(): return lax.ppermute(values, 'dp', [(d, d ^ bit) for d in range(self.dps)])  95.1 us
    ppermute x18, waiting for transfers between devices, swap_row(): return lax.ppermute(values, 'row', [(0, 1), (1, 0)])  81.4 us
    all_to_all x10, starting transfers between devices, exchange(): return lax.all_to_all(values, 'col', 0, 0, tiled=True)  46.2 us
    ppermute x6, starting transfers between devices, spread(): lax.ppermute(values, PLANE, self.along_plane(lambda d, c: (d, c + self.ho...  34.3 us
    ppermute x4, starting transfers between devices, place(): moved = lax.ppermute(both, PLANE, pairs)  24.8 us
    ppermute x34, starting transfers between devices, swap_dp(): return lax.ppermute(values, 'dp', [(d, d ^ bit) for d in range(self.dps)])  22.3 us
    ppermute x6, waiting for transfers between devices, spread(): lax.ppermute(values, PLANE, self.along_plane(lambda d, c: (d, c + self.ho...  20.6 us
  transfers between devices with their start and end apart: 77, of which 31 were waited for; matrix products, arithmetic and copies ran while one was open for 18% of the time, Pallas kernels for 21%

profile of v3, /device:TPU:0, one launch (start us, length us, event | category | flops | bytes accessed | tf_op | source)
XLA Modules:
  0.0 766.9 jit_solution(2960236152312122988)
XLA Ops:
  112.6 16.4 %collective-permute-done.8.refs_4_ = bf16[384,768]{1,0:T(8,128)(2,1)} collective-permute-done((bf16[384,768]{1,0:T(8,128)(2,1)}, bf16[384,768]{1,0:T(8,128)(2,1)}, u32[]{:S(2)}, u32[]{:S(2)}) %collective-permute-start.8) | collective-permute-done | bytes 589856 | tf_op jit(solution)/shard_map/ppermute | solution.py:421
  177.1 8.4 %shard_map.434.packed_ref = bf16[608,1152]{1,0:T(8,128)(2,1)} custom-call(s32[8]{0:T(128)} %stack.321.order_ref, bf16[4,608,384]{2,1,0:T(8,128)(2,1)} %all-to-all-done.1.columns_ref, bf16[768,1152]{1,0:T(8,128)(2,1)} %get-tuple-element.239.refs_0_, bf16[768,1152]{1,0:T(8,128)(2,1)} %get-tuple-element.240.refs_1_, ...), custom_call_target="tpu_custom_call" | custom-call | tf_op jit(solution)/shard_map/pallas_call | solution.py:47
  210.9 12.3 %collective-permute-done.13.refs_1_ = bf16[384,768]{1,0:T(8,128)(2,1)S(1)} collective-permute-done((bf16[384,768]{1,0:T(8,128)(2,1)}, bf16[384,768]{1,0:T(8,128)(2,1)S(1)}, u32[]{:S(2)}, u32[]{:S(2)}) %collective-permute-start.13) | collective-permute-done | bytes 589856 | tf_op jit(solution)/shard_map/ppermute | solution.py:434
  225.3 12.6 %collective-permute-done.14.refs_2_ = bf16[384,768]{1,0:T(8,128)(2,1)S(1)} collective-permute-done((bf16[384,768]{1,0:T(8,128)(2,1)}, bf16[384,768]{1,0:T(8,128)(2,1)S(1)}, u32[]{:S(2)}, u32[]{:S(2)}) %collective-permute-start.14) | collective-permute-done | bytes 589856 | tf_op jit(solution)/shard_map/ppermute | solution.py:431
  237.9 10.4 %collective-permute-done.15.refs_3_ = bf16[384,768]{1,0:T(8,128)(2,1)S(1)} collective-permute-done((bf16[384,768]{1,0:T(8,128)(2,1)S(1)}, bf16[384,768]{1,0:T(8,128)(2,1)S(1)}, u32[]{:S(2)}, u32[]{:S(2)}) %collective-permute-start.15) | collective-permute-done | bytes 589856 | tf_op jit(solution)/shard_map/ppermute | solution.py:431
  258.1 10.1 %all_to_all.70 = f32[4,2,608]{2,1,0:T(2,128)S(1)} all-to-all(f32[4,2,608]{2,1,0:T(2,128)S(1)} %broadcast_in_dim.192), channel_id=1, replica_groups=mesh['dp'=4,'row'=2,'col'=4] {'col'}, dimensions={0} | all-to-all | bytes 38912 | tf_op jit(solution)/shard_map/all_to_all | solution.py:446
  278.1 13.2 %collective-permute-done.22.refs_2_ = bf16[768,384]{1,0:T(8,128)(2,1)S(1)} collective-permute-done((bf16[768,384]{1,0:T(8,128)(2,1)}, bf16[768,384]{1,0:T(8,128)(2,1)S(1)}, u32[]{:S(2)}, u32[]{:S(2)}) %collective-permute-start.22) | collective-permute-done | bytes 589856 | tf_op jit(solution)/shard_map/ppermute | solution.py:434
  292.8 12.4 %collective-permute-done.24.refs_5_ = bf16[768,384]{1,0:T(8,128)(2,1)S(1)} collective-permute-done((bf16[768,384]{1,0:T(8,128)(2,1)}, bf16[768,384]{1,0:T(8,128)(2,1)S(1)}, u32[]{:S(2)}, u32[]{:S(2)}) %collective-permute-start.24) | collective-permute-done | bytes 589856 | tf_op jit(solution)/shard_map/ppermute | solution.py:431
  306.9 9.7 %collective-permute-done.23.refs_3_ = bf16[768,384]{1,0:T(8,128)(2,1)S(1)} collective-permute-done((bf16[768,384]{1,0:T(8,128)(2,1)S(1)}, bf16[768,384]{1,0:T(8,128)(2,1)S(1)}, u32[]{:S(2)}, u32[]{:S(2)}) %collective-permute-start.23) | collective-permute-done | bytes 589856 | tf_op jit(solution)/shard_map/ppermute | solution.py:431
  326.4 11.8 %shard_map.439 = (bf16[608,1536]{1,0:T(8,128)(2,1)}, f32[608,1536]{1,0:T(8,128)}) custom-call(s32[8]{0:T(128)} %stack.321.order_ref, bf16[4,608,384]{2,1,0:T(8,128)(2,1)} %all-to-all-done.5.columns_ref, bf16[768,1536]{1,0:T(8,128)(2,1)} %get-tuple-element.274.refs_0_, bf16[768,1536]{1,0:T(8,128)(2,1)} %collective-permute-done.19.refs_1_, ...), custom_call_target="tpu_custom_call" | custom-call | tf_op jit(solution)/shard_map/pallas_call | solution.py:47
  338.2 10.4 %shard_map.440 = (bf16[608,1536]{1,0:T(8,128)(2,1)}, f32[2,1536]{1,0:T(2,128)}) custom-call(s32[8]{0:T(128)} %stack.321.order_ref, bf16[4,608,384]{2,1,0:T(8,128)(2,1)} %copy-done.3, bf16[1536,768]{1,0:T(8,128)(2,1)} %get-tuple-element.271.refs_0_, bf16[1536,768]{1,0:T(8,128)(2,1)} %collective-permute-done.27.refs_1_, ...), custom_call_target="tpu_custom_call" | custom-call | tf_op jit(solution)/shard_map/pallas_call | solution.py:47
  348.6 9.8 %shard_map.441 = bf16[4,608,384]{2,1,0:T(8,128)(2,1)} custom-call(s32[8]{0:T(128)} %stack.321.order_ref, bf16[608,1536]{1,0:T(8,128)(2,1)} %get-tuple-element.286.inputs_ref, bf16[768,1536]{1,0:T(8,128)(2,1)} %get-tuple-element.274.refs_0_, bf16[768,1536]{1,0:T(8,128)(2,1)} %collective-permute-done.19.refs_1_, bf16[768,1536]{1,0:T(8,128)(2,1)} %get-tuple-element.276.refs_2_, ...), custom_call_target="tpu_custom_call" | custom-call | tf_op jit(solution)/shard_map/pallas_call | solution.py:47
  363.5 8.7 %shard_map.443 = (bf16[768,1536]{1,0:T(8,128)(2,1)}, bf16[768,1536]{1,0:T(8,128)(2,1)}, bf16[768,1536]{1,0:T(8,128)(2,1)}, bf16[768,1536]{1,0:T(8,128)(2,1)}) custom-call(s32[8]{0:T(128)} %stack.321.order_ref, bf16[4,608,384]{2,1,0:T(8,128)(2,1)} %all-to-all-done.5.columns_ref, bf16[608,1536]{1,0:T(8,128)(2,1)} %get-tuple-element.286.inputs_ref), custom_call_target="tpu_custom_call" | custom-call | tf_op jit(solution)/shard_map/pallas_call | solution.py:47
  372.7 9.9 %shard_map.442 = (bf16[1536,768]{1,0:T(8,128)(2,1)}, bf16[1536,768]{1,0:T(8,128)(2,1)}, bf16[1536,768]{1,0:T(8,128)(2,1)}, bf16[1536,768]{1,0:T(8,128)(2,1)}) custom-call(s32[8]{0:T(128)} %stack.321.order_ref, bf16[4,608,384]{2,1,0:T(8,128)(2,1)} %copy-done.3, bf16[608,1536]{1,0:T(8,128)(2,1)} %get-tuple-element.281.inputs_ref), custom_call_target="tpu_custom_call" | custom-call | tf_op jit(solution)/shard_map/pallas_call | solution.py:47
  383.1 9.4 %shard_map.445 = bf16[4,608,384]{2,1,0:T(8,128)(2,1)} custom-call(s32[8]{0:T(128)} %stack.321.order_ref, bf16[608,1536]{1,0:T(8,128)(2,1)} %get-tuple-element.281.inputs_ref, bf16[1536,768]{1,0:T(8,128)(2,1)} %get-tuple-element.271.refs_0_, bf16[1536,768]{1,0:T(8,128)(2,1)} %collective-permute-done.27.refs_1_, bf16[1536,768]{1,0:T(8,128)(2,1)} %get-tuple-element.272.refs_2_, ...), custom_call_target="tpu_custom_call" | custom-call | tf_op jit(solution)/shard_map/pallas_call | solution.py:47
  394.7 11.4 %shard_map.444 = (bf16[768,768]{1,0:T(8,128)(2,1)}, bf16[768,768]{1,0:T(8,128)(2,1)}, bf16[1536,384]{1,0:T(8,128)(2,1)}, bf16[1536,384]{1,0:T(8,128)(2,1)}, bf16...) custom-call(s32[1]{0:T(128)} %constant.281.clone.1.order_ref, ...), custom_call_target="tpu_custom_call" | custom-call | tf_op jit(solution)/shard_map/pallas_call | solution.py:47
  409.6 9.6 %all_to_all.71 = f32[4,2,608]{2,1,0:T(2,128)} all-to-all(f32[4,2,608]{2,1,0:T(2,128)S(1)} %broadcast_in_dim.202), channel_id=1, replica_groups=mesh['dp'=4,'row'=2,'col'=4] {'col'}, dimensions={0} | all-to-all | bytes 38912 | tf_op jit(solution)/shard_map/all_to_all | solution.py:446
  434.8 25.2 %collective-permute-done.33.refs_1_ = bf16[768,768]{1,0:T(8,128)(2,1)} collective-permute-done((bf16[768,768]{1,0:T(8,128)(2,1)}, bf16[768,768]{1,0:T(8,128)(2,1)}, u32[]{:S(2)}, u32[]{:S(2)}) %collective-permute-start.33) | collective-permute-done | bytes 1179680 | tf_op jit(solution)/shard_map/ppermute | solution.py:434
  461.1 21.7 %collective-permute-done.35.refs_5_ = bf16[768,768]{1,0:T(8,128)(2,1)} collective-permute-done((bf16[768,768]{1,0:T(8,128)(2,1)}, bf16[768,768]{1,0:T(8,128)(2,1)}, u32[]{:S(2)}, u32[]{:S(2)}) %collective-permute-start.35) | collective-permute-done | bytes 1179680 | tf_op jit(solution)/shard_map/ppermute | solution.py:434
  511.9 9.9 %shard_map.447.inputs_ref = bf16[608,1152]{1,0:T(8,128)(2,1)} custom-call(s32[8]{0:T(128)} %stack.321.order_ref, bf16[608,1152]{1,0:T(8,128)(2,1)} %shard_map.434.packed_ref, bf16[608,384]{1,0:T(8,128)(2,1)} %get-tuple-element.334.inputs_ref.attended_ref, f32[6,608]{1,0:T(8,128)} %get-tuple-element.261.log_ref, bf16[608,384]{1,0:T(8,128)(2,1)} %shard_map.446.d_ref), custom_call_target="tpu_custom_call" | custom-call | tf_op jit(solution)/shard_map/pallas_call | solution.py:47
  521.8 8.4 %shard_map.448 = bf16[4,608,384]{2,1,0:T(8,128)(2,1)} custom-call(s32[8]{0:T(128)} %stack.321.order_ref, bf16[608,1152]{1,0:T(8,128)(2,1)} %shard_map.447.inputs_ref, bf16[768,1152]{1,0:T(8,128)(2,1)} %get-tuple-element.239.refs_0_, bf16[768,1152]{1,0:T(8,128)(2,1)} %get-tuple-element.240.refs_1_, bf16[768,1152]{1,0:T(8,128)(2,1)} %get-tuple-element.241.refs_2_, ...), custom_call_target="tpu_custom_call" | custom-call | tf_op jit(solution)/shard_map/pallas_call | solution.py:47
  627.6 10.6 %collective-permute-start.58 = (bf16[768,768]{1,0:T(8,128)(2,1)}, bf16[768,768]{1,0:T(8,128)(2,1)}, u32[]{:S(2)}, u32[]{:S(2)}) collective-permute-start(bf16[768,768]{1,0:T(8,128)(2,1)} %pad_maximum_fusion.4), channel_id=1, source_target_pairs={{0,0},{1,9},{2,18},{3,27},{8,2},{9,11},{10,16},{11,25},{16,3},{17,... | collective-permute-start | bytes 3538952 | tf_op jit(solution)/shard_map/ppermute | solution.py:487
  658.5 23.8 %collective-permute-done.54.refs_1_ = bf16[384,576]{1,0:T(8,128)(2,1)} collective-permute-done((bf16[384,576]{1,0:T(8,128)(2,1)}, bf16[384,576]{1,0:T(8,128)(2,1)}, u32[]{:S(2)}, u32[]{:S(2)}) %collective-permute-start.54) | collective-permute-done | bytes 442400 | tf_op jit(solution)/shard_map/ppermute | solution.py:431
  686.9 9.1 %all-to-all-start.12 = ((bf16[2,4,96,768]{3,2,0,1:T(8,128)(2,1)}), bf16[2,4,96,768]{3,2,0,1:T(8,128)(2,1)}, u32[]{:S(2)}, u32[]{:S(2)}) async-start(bf16[2,4,96,768]{3,2,0,1:T(8,128)(2,1)} %pad_maximum_fusion.6), calls=%async_computation.12 | async-start | bytes 2359296 | tf_op jit(solution)/shard_map/all_to_all | solution.py:495
  (676 shorter events, 468.1 us)
Async XLA Ops:
  4.1 38.8 %collective-permute-start.1 = (bf16[576,576]{1,0:T(8,128)(2,1)}, bf16[576,576]{1,0:T(8,128)(2,1)}, u32[]{:S(2)}, u32[]{:S(2)}) collective-permute-start(bf16[576,576]{1,0:T(8,128)(2,1)} %fusion.34), channel_id=1, source_target_pairs={{0,2},{1,3},{2,0},{3,1},{8,8},{9,9},{10,10},{11,11},{16,19},{17,16... | collective-permute-start | bytes 1990664 | tf_op jit(solution)/shard_map/ppermute | solution.py:421
  55.8 73.2 %all-to-all-start.1 = ((bf16[4,608,384]{2,1,0:T(8,128)(2,1)}), bf16[4,608,384]{2,1,0:T(8,128)(2,1)}, u32[]{:S(2)}, u32[]{:S(2)}) async-start(bf16[4,608,384]{2,1,0:T(8,128)(2,1)} %broadcast_in_dim.188), calls=%async_computation.1 | async-start | bytes 3735552 | tf_op jit(solution)/shard_map/all_to_all | solution.py:446
  78.6 50.4 %collective-permute-start.8 = (bf16[384,768]{1,0:T(8,128)(2,1)}, bf16[384,768]{1,0:T(8,128)(2,1)}, u32[]{:S(2)}, u32[]{:S(2)}) collective-permute-start(bf16[384,768]{1,0:T(8,128)(2,1)} %constant_dynamic-slice_fusion.6), channel_id=1, source_target_pairs={{0,2},{1,3},{2,0},{3,1},{8,8},{9,9},{10,10},{11,11},{16,19},{17,16... | collective-permute-start | bytes 1769480 | tf_op jit(solution)/shard_map/ppermute | solution.py:421
  84.6 44.4 %collective-permute-start.7 = (bf16[384,768]{1,0:T(8,128)(2,1)}, bf16[384,768]{1,0:T(8,128)(2,1)}, u32[]{:S(2)}, u32[]{:S(2)}) collective-permute-start(bf16[384,768]{1,0:T(8,128)(2,1)} %constant_dynamic-slice_fusion.7), channel_id=1, source_target_pairs={{0,0},{1,1},{2,2},{3,3},{8,10},{9,11},{10,8},{11,9},{16,17},{17,18... | collective-permute-start | bytes 1769480 | tf_op jit(solution)/shard_map/ppermute | solution.py:421
  130.5 71.7 %all-to-all-start.2 = ((bf16[4,608,384]{2,1,0:T(8,128)(2,1)}), bf16[4,608,384]{2,1,0:T(8,128)(2,1)S(1)}, u32[]{:S(2)}, u32[]{:S(2)}) async-start(bf16[4,608,384]{2,1,0:T(8,128)(2,1)} %broadcast_in_dim.191), calls=%async_computation.2 | async-start | bytes 3735552 | tf_op jit(solution)/shard_map/all_to_all | solution.py:446
  143.6 54.4 %collective-permute-start.11 = (bf16[768,384]{1,0:T(8,128)(2,1)}, bf16[768,384]{1,0:T(8,128)(2,1)}, u32[]{:S(2)}, u32[]{:S(2)}) collective-permute-start(bf16[768,384]{1,0:T(8,128)(2,1)} %get-tuple-element.250), channel_id=1, source_target_pairs={{0,0},{1,1},{2,2},{3,3},{8,10},{9,11},{10,8},{11,9},{16,17},{17,18... | collective-permute-start | bytes 1769480 | tf_op jit(solution)/shard_map/ppermute | solution.py:421
  149.6 52.6 %collective-permute-start.12 = (bf16[768,384]{1,0:T(8,128)(2,1)}, bf16[768,384]{1,0:T(8,128)(2,1)}, u32[]{:S(2)}, u32[]{:S(2)}) collective-permute-start(bf16[768,384]{1,0:T(8,128)(2,1)} %get-tuple-element.251), channel_id=1, source_target_pairs={{0,2},{1,3},{2,0},{3,1},{8,8},{9,9},{10,10},{11,11},{16,19},{17,16... | collective-permute-start | bytes 1769480 | tf_op jit(solution)/shard_map/ppermute | solution.py:421
  202.2 52.4 %all-to-all-start.3 = ((bf16[4,608,384]{2,1,0:T(8,128)(2,1)}), bf16[4,608,384]{2,1,0:T(8,128)(2,1)}, u32[]{:S(2)}, u32[]{:S(2)}) async-start(bf16[4,608,384]{2,1,0:T(8,128)(2,1)} %shard_map.436), calls=%async_computation.3 | async-start | bytes 3735552 | tf_op jit(solution)/shard_map/all_to_all | solution.py:446
  270.4 54.1 %all-to-all-start.5 = ((bf16[4,608,384]{2,1,0:T(8,128)(2,1)}), bf16[4,608,384]{2,1,0:T(8,128)(2,1)}, u32[]{:S(2)}, u32[]{:S(2)}) async-start(bf16[4,608,384]{2,1,0:T(8,128)(2,1)} %broadcast_in_dim.201), calls=%async_computation.5 | async-start | bytes 3735552 | tf_op jit(solution)/shard_map/all_to_all | solution.py:446
  275.2 49.2 %collective-permute-start.19 = (bf16[768,1536]{1,0:T(8,128)(2,1)}, bf16[768,1536]{1,0:T(8,128)(2,1)}, u32[]{:S(2)}, u32[]{:S(2)}) collective-permute-start(bf16[768,1536]{1,0:T(8,128)(2,1)} %get-tuple-element.274.refs_0_), channel_id=1, source_target_pairs={{0,8},{8,0},{16,24},{24,16},{1,9},{9,1},{17,25},{25,17},{2,10},{10... | collective-permute-start | bytes 7077896 | tf_op jit(solution)/shard_map/ppermute | solution.py:431
  275.3 49.1 %collective-permute-start.20 = (bf16[768,1536]{1,0:T(8,128)(2,1)}, bf16[768,1536]{1,0:T(8,128)(2,1)}, u32[]{:S(2)}, u32[]{:S(2)}) collective-permute-start(bf16[768,1536]{1,0:T(8,128)(2,1)} %get-tuple-element.276.refs_2_), channel_id=1, source_target_pairs={{0,8},{8,0},{16,24},{24,16},{1,9},{9,1},{17,25},{25,17},{2,10},{10... | collective-permute-start | bytes 7077896 | tf_op jit(solution)/shard_map/ppermute | solution.py:431
  358.3 48.8 %all-to-all-start.6 = ((bf16[4,608,384]{2,1,0:T(8,128)(2,1)}), bf16[4,608,384]{2,1,0:T(8,128)(2,1)}, u32[]{:S(2)}, u32[]{:S(2)}) async-start(bf16[4,608,384]{2,1,0:T(8,128)(2,1)} %shard_map.441), calls=%async_computation.6 | async-start | bytes 3735552 | tf_op jit(solution)/shard_map/all_to_all | solution.py:446
  426.3 57.4 %all-to-all-start.8 = ((bf16[4,608,384]{2,1,0:T(8,128)(2,1)}), bf16[4,608,384]{2,1,0:T(8,128)(2,1)}, u32[]{:S(2)}, u32[]{:S(2)}) async-start(bf16[4,608,384]{2,1,0:T(8,128)(2,1)} %broadcast_in_dim.203), calls=%async_computation.8 | async-start | bytes 3735552 | tf_op jit(solution)/shard_map/all_to_all | solution.py:446
  432.2 50.7 %collective-permute-start.35 = (bf16[768,768]{1,0:T(8,128)(2,1)}, bf16[768,768]{1,0:T(8,128)(2,1)}, u32[]{:S(2)}, u32[]{:S(2)}) collective-permute-start(bf16[768,768]{1,0:T(8,128)(2,1)} %get-tuple-element.306), channel_id=1, source_target_pairs={{0,4},{4,0},{1,5},{5,1},{2,6},{6,2},{3,7},{7,3},{8,12},{12,8},{9,1... | collective-permute-start | bytes 3538952 | tf_op jit(solution)/shard_map/ppermute | solution.py:434
  433.0 50.7 %collective-permute-start.36 = (bf16[384,1536]{1,0:T(8,128)(2,1)}, bf16[384,1536]{1,0:T(8,128)(2,1)}, u32[]{:S(2)}, u32[]{:S(2)}) collective-permute-start(bf16[384,1536]{1,0:T(8,128)(2,1)} %get-tuple-element.308), channel_id=1, source_target_pairs={{0,16},{8,24},{16,0},{24,8},{1,17},{9,25},{17,1},{25,9},{2,18},{10... | collective-permute-start | bytes 3538952 | tf_op jit(solution)/shard_map/ppermute | solution.py:431
  483.7 46.5 %all-to-all-start.9 = ((bf16[4,608,384]{2,1,0:T(8,128)(2,1)}), bf16[4,608,384]{2,1,0:T(8,128)(2,1)}, u32[]{:S(2)}, u32[]{:S(2)}) async-start(bf16[4,608,384]{2,1,0:T(8,128)(2,1)} %shard_map.445), calls=%async_computation.9 | async-start | bytes 3735552 | tf_op jit(solution)/shard_map/all_to_all | solution.py:446
  530.2 47.3 %all-to-all-start.10 = ((bf16[4,608,384]{2,1,0:T(8,128)(2,1)}), bf16[4,608,384]{2,1,0:T(8,128)(2,1)}, u32[]{:S(2)}, u32[]{:S(2)}) async-start(bf16[4,608,384]{2,1,0:T(8,128)(2,1)} %shard_map.448), calls=%async_computation.10 | async-start | bytes 3735552 | tf_op jit(solution)/shard_map/all_to_all | solution.py:446
  584.0 43.7 %collective-permute-start.47 = (bf16[192,768]{1,0:T(8,128)(2,1)}, bf16[192,768]{1,0:T(8,128)(2,1)}, u32[]{:S(2)}, u32[]{:S(2)}) collective-permute-start(bf16[192,768]{1,0:T(8,128)(2,1)} %get-tuple-element.353), channel_id=1, source_target_pairs={{0,4},{4,0},{1,5},{5,1},{2,6},{6,2},{3,7},{7,3},{8,12},{12,8},{9,1... | collective-permute-start | bytes 884744 | tf_op jit(solution)/shard_map/ppermute | solution.py:434
  584.9 53.4 %collective-permute-start.48 = (bf16[384,384]{1,0:T(8,128)(2,1)}, bf16[384,384]{1,0:T(8,128)(2,1)}, u32[]{:S(2)}, u32[]{:S(2)}) collective-permute-start(bf16[384,384]{1,0:T(8,128)(2,1)} %get-tuple-element.355), channel_id=1, source_target_pairs={{0,16},{8,24},{16,0},{24,8},{1,17},{9,25},{17,1},{25,9},{2,18},{10... | collective-permute-start | bytes 884744 | tf_op jit(solution)/shard_map/ppermute | solution.py:431
  590.4 47.9 %collective-permute-start.45 = (bf16[768,576]{0,1:T(8,128)(2,1)}, bf16[768,576]{0,1:T(8,128)(2,1)}, u32[]{:S(2)}, u32[]{:S(2)}) collective-permute-start(bf16[768,576]{0,1:T(8,128)(2,1)} %copy.335), channel_id=1, source_target_pairs={{0,4},{4,0},{1,5},{5,1},{2,6},{6,2},{3,7},{7,3},{8,12},{12,8},{9,1... | collective-permute-start | bytes 2654216 | tf_op jit(solution)/shard_map/ppermute | solution.py:434
  591.5 46.8 %collective-permute-start.46 = (bf16[384,1152]{1,0:T(8,128)(2,1)}, bf16[384,1152]{1,0:T(8,128)(2,1)}, u32[]{:S(2)}, u32[]{:S(2)}) collective-permute-start(bf16[384,1152]{1,0:T(8,128)(2,1)} %get-tuple-element.351), channel_id=1, source_target_pairs={{0,16},{8,24},{16,0},{24,8},{1,17},{9,25},{17,1},{25,9},{2,18},{10... | collective-permute-start | bytes 2654216 | tf_op jit(solution)/shard_map/ppermute | solution.py:431
  622.8 30.4 %collective-permute-start.59 = (bf16[768,768]{1,0:T(8,128)(2,1)}, bf16[768,768]{1,0:T(8,128)(2,1)}, u32[]{:S(2)}, u32[]{:S(2)}) collective-permute-start(bf16[768,768]{1,0:T(8,128)(2,1)} %pad_maximum_fusion.5), channel_id=1, source_target_pairs={{0,2},{1,11},{2,16},{3,25},{8,0},{9,9},{10,18},{11,27},{16,1},{17,... | collective-permute-start | bytes 3538952 | tf_op jit(solution)/shard_map/ppermute | solution.py:487
  649.8 32.5 %collective-permute-start.54 = (bf16[384,576]{1,0:T(8,128)(2,1)}, bf16[384,576]{1,0:T(8,128)(2,1)}, u32[]{:S(2)}, u32[]{:S(2)}) collective-permute-start(bf16[384,576]{1,0:T(8,128)(2,1)} %get-tuple-element.370), channel_id=1, source_target_pairs={{0,16},{8,24},{16,0},{24,8},{1,17},{9,25},{17,1},{25,9},{2,18},{10... | collective-permute-start | bytes 1327112 | tf_op jit(solution)/shard_map/ppermute | solution.py:431
  686.9 48.6 %all-to-all-start.12 = ((bf16[2,4,96,768]{3,2,0,1:T(8,128)(2,1)}), bf16[2,4,96,768]{3,2,0,1:T(8,128)(2,1)}, u32[]{:S(2)}, u32[]{:S(2)}) async-start(bf16[2,4,96,768]{3,2,0,1:T(8,128)(2,1)} %pad_maximum_fusion.6), calls=%async_computation.12 | async-start | bytes 2359296 | tf_op jit(solution)/shard_map/all_to_all | solution.py:495
  (165 other events, 2024.7 us)

commit v4 on v3

--- a/solution.py
+++ b/solution.py
@@ -70,7 +70,7 @@
 def mix(columns, weights, order, split, back, extra, outs, finish):
     tokens, width = columns.shape[1:]
     total = weights[0][0].shape[0 if back else 1]
-    block = width
+    block = 512 if total % 512 == 0 else width
     pair = (block, 2 * width) if back else (2 * width, block)
     ranges = ((0, split), (split, tokens))
 
@@ -210,22 +210,35 @@
     return [(halves[2 * item], halves[2 * item + 1]) for item in range(len(pairs))]
 
 
-def add_up(pairs):
-    steps = steps_for([pair[0].shape[0] for pair in pairs], False)
-    specs = [on_rows((pair[0].shape[0] // steps, pair[0].shape[1])) for pair in pairs]
+def add_and_stack(wides, talls):
+    shapes = []
+    for (wide, _), (tall, _) in zip(wides, talls):
+        beside = wide.shape[1] // tall.shape[1]
+        shapes.append((wide.shape[0] + tall.shape[0] // beside, wide.shape[1]))
 
     def body(order_ref, *refs):
-        for item in range(len(pairs)):
-            total = refs[2 * item][...].astype(F32) + refs[2 * item + 1][...].astype(F32)
-            refs[2 * len(pairs) + item][...] = total.astype(BF)
-
+        for item, (rows, columns) in enumerate(shapes):
+            wide, wide_other, tall, tall_other = refs[4 * item : 4 * item + 4]
+            out_ref = refs[4 * len(shapes) + item]
+            top, width = wide.shape[0], tall.shape[1]
+            out_ref[:top] = (wide[...].astype(F32) + wide_other[...].astype(F32)).astype(BF)
+            total = (tall[...].astype(F32) + tall_other[...].astype(F32)).astype(BF)
+            for part in range(columns // width):
+                piece = total[part * (rows - top) : (part + 1) * (rows - top)]
+                out_ref[top:, part * width : (part + 1) * width] = piece
+            if columns % width:
+                out_ref[top:, columns - columns % width :] = jnp.zeros(
+                    (rows - top, columns % width), BF
+                )
+
+    flat = [array for pairs in zip(wides, talls) for pair in pairs for array in pair]
     return call(
         body,
-        (steps,),
-        [spec for spec in specs for _ in range(2)],
-        specs,
-        [jax.ShapeDtypeStruct(pair[0].shape, BF) for pair in pairs],
-        (jnp.zeros((1,), jnp.int32), *[array for pair in pairs for array in pair]),
+        (1,),
+        [whole(array.shape) for array in flat],
+        [whole(shape) for shape in shapes],
+        [jax.ShapeDtypeStruct(shape, BF) for shape in shapes],
+        (jnp.zeros((1,), jnp.int32), *flat),
     )
 
 
@@ -464,29 +477,35 @@
     def move(self, values, by_row):
         return self.swap_row(values) if by_row else self.swap_dp(values, 2)
 
-    def fold_rest(self, total):
+    def fold_rest(self, pair):
         bit = self.dps // 2
         while bit >= self.cols:
+            total = pair[0].astype(F32) + pair[1].astype(F32)
             half = total.shape[0] // 2
             upper = (self.dp // bit) % 2
-            keep = lax.dynamic_slice_in_dim(total, upper * half, half, 0)
+            keep = lax.dynamic_slice_in_dim(total, upper * half, half, 0).astype(BF)
             send = lax.dynamic_slice_in_dim(total, (1 - upper) * half, half, 0).astype(BF)
-            total = keep + self.swap_dp(send, bit).astype(F32)
+            pair = (keep, self.swap_dp(send, bit))
             bit //= 2
-        return total.astype(BF)
-
-    def place(self, by_cols, by_rows):
+        return pair
+
+    def place(self, wides, talls):
         share = self.dps // self.cols
+        if share > 1:
+            talls = [self.fold_rest(pair) for pair in talls]
         cols_placed, rows_placed = [], []
-        for stream, (wide, tall) in enumerate(zip(by_cols, by_rows)):
+        for stream, both in enumerate(add_and_stack(wides, talls)):
             pairs = self.along_plane(
                 lambda d, c: (c * share + d // self.cols, c - self.hop(d, 0, stream))
             )
-            rest = self.fold_rest(tall)
-            both = jnp.concatenate([wide, rest.reshape(-1, wide.shape[1])])
             moved = lax.ppermute(both, PLANE, pairs)
-            cols_placed.append(moved[: wide.shape[0]])
-            rows_placed.append(moved[wide.shape[0] :].reshape(rest.shape))
+            top, width = wides[stream][0].shape[0], talls[stream][0].shape[1]
+            cols_placed.append(moved[:top])
+            parts = [
+                moved[top:, part * width : (part + 1) * width]
+                for part in range(moved.shape[1] // width)
+            ]
+            rows_placed.append(jnp.concatenate(parts))
         return cols_placed, rows_placed
 
     def place_end(self, parts):
@@ -620,10 +639,6 @@
             for group in groups
         ]
 
-    def fold_end(groups):
-        sums = add_up([pair for group in groups for pair in group])
-        return [sums[2 * group : 2 * group + 2] for group in range(len(groups))]
-
     def join(parts):
         return jnp.concatenate(parts, axis=0)
 
@@ -791,7 +806,7 @@
     d_qkv = attend_back(packed, attn, log_total, d_attn, order, head_size, count)
     qkv_back = parts(d_qkv, qkv_w, order, split, True)
     qkv_back, parts_branch2, folds = lax.optimization_barrier((qkv_back, parts_branch2, folds))
-    down_fold, up_fold = fold_end(folds)
+    down_fold, up_fold = folds
     parts_normed1 = grid.exchange(qkv_back)
     d_qkv_late, attn_late = after((d_qkv, attn), qkv_back)
     qkv_fold = fold_core(weight_grads(normed1, d_qkv_late, order, split, True))
@@ -821,23 +836,22 @@
         ],
         axis=1,
     ).astype(BF)
+    norm_back1, late_folds = lax.optimization_barrier((norm_back1, late_folds))
     act_all = act_cond
+    vectors = after(vectors, late_folds)
     everyone = jnp.stack([vectors, grid.swap_row(vectors)])
     bit = grid.dps // 2
     while bit:
         everyone = jnp.concatenate([everyone, grid.swap_dp(everyone, bit)])
         act_all = jnp.concatenate([act_all, grid.swap_dp(after(act_all, vectors), bit)])
         bit //= 2
-    norm_back1, late_folds, everyone, act_all = lax.optimization_barrier(
-        (norm_back1, late_folds, everyone, act_all)
-    )
     late_folds = move(fold(late_folds, (1, 0), False), False)
-    late_folds, up_placed, down_placed = lax.optimization_barrier(
-        (late_folds, up_placed, down_placed)
-    )
-    qkv_fold, out_fold = fold_end(late_folds)
+    up_moved = grid.place_end(up_placed)
+    late_folds, up_moved, down_placed, everyone, act_all = lax.optimization_barrier(
+        (late_folds, up_moved, down_placed, everyone, act_all)
+    )
+    qkv_fold, out_fold = late_folds
     qkv_placed, out_placed = grid.place(qkv_fold, out_fold)
-    up_moved = grid.place_end(up_placed)
 
     in_grads = unpadded(d_middle + norm_back1)
     vector_sums = jnp.sum(everyone.astype(F32), axis=0)
@@ -860,15 +874,13 @@
     d_mod = jnp.where(grid.row == 0, by_row, by_row[:, ::-1]).reshape(-1, 2, 6, col_width)
     mod_share = mod_rows // grid.dps
     act_share = lax.dynamic_slice_in_dim(act_all, grid.dp * mod_share, mod_share, 1)
-    mod_w_grad = modulation_grads(after(act_share, late_folds), d_mod, 6)
-    own_d_mod = after(d_mod[:seq_count], late_folds)
+    qkv_placed, out_placed = lax.optimization_barrier((qkv_placed, out_placed))
+    qkv_moved = grid.place_end(qkv_placed)
+    mod_w_grad = modulation_grads(after(act_share, up_moved), d_mod, 6)
+    own_d_mod = after(d_mod[:seq_count], qkv_placed)
     cond_part = condition_part(own_d_mod, mod_weights)
     last = jnp.stack([cond_part, up_total_own])
     lasts = [last] + grid.col_others(last)
-    lasts, qkv_placed, out_placed, up_moved = lax.optimization_barrier(
-        (lasts, qkv_placed, out_placed, up_moved)
-    )
-    qkv_moved = grid.place_end(qkv_placed)
     cond_sum = sum(item[0] for item in lasts)
     up_share = up_count * grid.cols // grid.dps
     up_from = (grid.col - grid.dp * grid.cols // grid.dps) % grid.cols

time: 779 us -> 773 us (level)
  waiting for transfers between devices: 210 us -> 230 us
  local copies, waits for them, and re-layouts: 104 us -> 91.5 us
    ppermute x3, starting transfers between devices: 4.26 us -> 20.1 us  [col_others(): lax.ppermute(values, 'col', [(c, (c + shift) % self.cols) for c in range(...]
    all_to_all x2, waiting for transfers between devices: 7.79 us -> 22 us  [place_end(): return lax.all_to_all(moved, 'dp', 1, 1, tiled=True)]
    all_to_all x10, waiting for transfers between devices: 2.37 us -> 15.8 us  [exchange(): return lax.all_to_all(values, 'col', 0, 0, tiled=True)]
    ppermute x4, starting transfers between devices: 24.8 us -> 15.9 us  [place(): moved = lax.ppermute(both, PLANE, pairs)]
    all_to_all x2, starting transfers between devices: 16 us -> 7.25 us  [place_end(): return lax.all_to_all(moved, 'dp', 1, 1, tiled=True)]
  transfers between devices with their start and end apart: 77 -> 77, of which waited for: 31 -> 29; matrix products, arithmetic and copies ran while one was open for 18% -> 16% of each run, Pallas kernels for 21% -> 20%
where the time goes in v4:
time: 773 us; the launch traced here: 761 us
  waiting for transfers between devices  230 us (30%)
  Pallas kernels  183 us (24%)
  starting transfers between devices  161 us (21%)
  local copies, waits for them, and re-layouts  91.5 us (12%)
  other arithmetic  63.4 us (8%)
  blocking collectives  19.8 us (3%)
  matrix products  8.88 us (1%)
    pallas_call x26, Pallas kernels, call(): pl.pallas_call(body, grid_spec=pltpu.PrefetchScalarGridSpec(num_scalar_pr...  183 us
    ppermute x34, waiting for transfers between devices, swap_dp(): return lax.ppermute(values, 'dp', [(d, d ^ bit) for d in range(self.dps)])  94.4 us
    ppermute x18, waiting for transfers between devices, swap_row(): return lax.ppermute(values, 'row', [(0, 1), (1, 0)])  76.9 us
    all_to_all x10, starting transfers between devices, exchange(): return lax.all_to_all(values, 'col', 0, 0, tiled=True)  43.4 us
    ppermute x6, starting transfers between devices, spread(): lax.ppermute(values, PLANE, self.along_plane(lambda d, c: (d, c + self.ho...  34.4 us
    ppermute x34, starting transfers between devices, swap_dp(): return lax.ppermute(values, 'dp', [(d, d ^ bit) for d in range(self.dps)])  22.9 us
    all_to_all x2, waiting for transfers between devices, place_end(): return lax.all_to_all(moved, 'dp', 1, 1, tiled=True)  22 us
    ppermute x6, waiting for transfers between devices, spread(): lax.ppermute(values, PLANE, self.along_plane(lambda d, c: (d, c + self.ho...  20.6 us
  transfers between devices with their start and end apart: 77, of which 29 were waited for; matrix products, arithmetic and copies ran while one was open for 16% of the time, Pallas kernels for 20%

profile of v4, /device:TPU:0, one launch (start us, length us, event | category | flops | bytes accessed | tf_op | source)
XLA Modules:
  0.0 760.7 jit_solution(10286959705772693450)
XLA Ops:
  112.7 16.3 %collective-permute-done.8.refs_4_ = bf16[384,768]{1,0:T(8,128)(2,1)} collective-permute-done((bf16[384,768]{1,0:T(8,128)(2,1)}, bf16[384,768]{1,0:T(8,128)(2,1)}, u32[]{:S(2)}, u32[]{:S(2)}) %collective-permute-start.8) | collective-permute-done | bytes 589856 | tf_op jit(solution)/shard_map/ppermute | solution.py:434
  210.9 12.3 %collective-permute-done.13.refs_1_ = bf16[384,768]{1,0:T(8,128)(2,1)S(1)} collective-permute-done((bf16[384,768]{1,0:T(8,128)(2,1)}, bf16[384,768]{1,0:T(8,128)(2,1)S(1)}, u32[]{:S(2)}, u32[]{:S(2)}) %collective-permute-start.13) | collective-permute-done | bytes 589856 | tf_op jit(solution)/shard_map/ppermute | solution.py:447
  225.3 12.6 %collective-permute-done.14.refs_2_ = bf16[384,768]{1,0:T(8,128)(2,1)S(1)} collective-permute-done((bf16[384,768]{1,0:T(8,128)(2,1)}, bf16[384,768]{1,0:T(8,128)(2,1)S(1)}, u32[]{:S(2)}, u32[]{:S(2)}) %collective-permute-start.14) | collective-permute-done | bytes 589856 | tf_op jit(solution)/shard_map/ppermute | solution.py:444
  237.9 10.4 %collective-permute-done.15.refs_3_ = bf16[384,768]{1,0:T(8,128)(2,1)S(1)} collective-permute-done((bf16[384,768]{1,0:T(8,128)(2,1)S(1)}, bf16[384,768]{1,0:T(8,128)(2,1)S(1)}, u32[]{:S(2)}, u32[]{:S(2)}) %collective-permute-start.15) | collective-permute-done | bytes 589856 | tf_op jit(solution)/shard_map/ppermute | solution.py:444
  258.2 10.1 %all_to_all.70 = f32[4,2,608]{2,1,0:T(2,128)S(1)} all-to-all(f32[4,2,608]{2,1,0:T(2,128)S(1)} %broadcast_in_dim.194), channel_id=1, replica_groups=mesh['dp'=4,'row'=2,'col'=4] {'col'}, dimensions={0} | all-to-all | bytes 38912 | tf_op jit(solution)/shard_map/all_to_all | solution.py:459
  278.0 13.2 %collective-permute-done.22.refs_2_ = bf16[768,384]{1,0:T(8,128)(2,1)S(1)} collective-permute-done((bf16[768,384]{1,0:T(8,128)(2,1)}, bf16[768,384]{1,0:T(8,128)(2,1)S(1)}, u32[]{:S(2)}, u32[]{:S(2)}) %collective-permute-start.22) | collective-permute-done | bytes 589856 | tf_op jit(solution)/shard_map/ppermute | solution.py:447
  292.7 12.4 %collective-permute-done.24.refs_5_ = bf16[768,384]{1,0:T(8,128)(2,1)S(1)} collective-permute-done((bf16[768,384]{1,0:T(8,128)(2,1)}, bf16[768,384]{1,0:T(8,128)(2,1)S(1)}, u32[]{:S(2)}, u32[]{:S(2)}) %collective-permute-start.24) | collective-permute-done | bytes 589856 | tf_op jit(solution)/shard_map/ppermute | solution.py:444
  306.8 9.7 %collective-permute-done.23.refs_3_ = bf16[768,384]{1,0:T(8,128)(2,1)S(1)} collective-permute-done((bf16[768,384]{1,0:T(8,128)(2,1)S(1)}, bf16[768,384]{1,0:T(8,128)(2,1)S(1)}, u32[]{:S(2)}, u32[]{:S(2)}) %collective-permute-start.23) | collective-permute-done | bytes 589856 | tf_op jit(solution)/shard_map/ppermute | solution.py:444
  326.2 11.4 %shard_map.439 = (bf16[608,1536]{1,0:T(8,128)(2,1)}, f32[608,1536]{1,0:T(8,128)}) custom-call(s32[8]{0:T(128)} %stack.348.order_ref, bf16[4,608,384]{2,1,0:T(8,128)(2,1)} %all-to-all-done.5.columns_ref, bf16[768,1536]{1,0:T(8,128)(2,1)} %get-tuple-element.269.refs_0_, bf16[768,1536]{1,0:T(8,128)(2,1)} %collective-permute-done.19.refs_1_, ...), custom_call_target="tpu_custom_call" | custom-call | tf_op jit(solution)/shard_map/pallas_call | solution.py:47
  337.6 10.4 %shard_map.440 = (bf16[608,1536]{1,0:T(8,128)(2,1)}, f32[2,1536]{1,0:T(2,128)}) custom-call(s32[8]{0:T(128)} %stack.348.order_ref, bf16[4,608,384]{2,1,0:T(8,128)(2,1)} %copy-done.3, bf16[1536,768]{1,0:T(8,128)(2,1)} %get-tuple-element.266.refs_0_, bf16[1536,768]{1,0:T(8,128)(2,1)} %collective-permute-done.27.refs_1_, ...), custom_call_target="tpu_custom_call" | custom-call | tf_op jit(solution)/shard_map/pallas_call | solution.py:47
  348.0 9.8 %shard_map.441 = bf16[4,608,384]{2,1,0:T(8,128)(2,1)} custom-call(s32[8]{0:T(128)} %stack.348.order_ref, bf16[608,1536]{1,0:T(8,128)(2,1)} %get-tuple-element.281.inputs_ref, bf16[768,1536]{1,0:T(8,128)(2,1)} %get-tuple-element.269.refs_0_, bf16[768,1536]{1,0:T(8,128)(2,1)} %collective-permute-done.19.refs_1_, bf16[768,1536]{1,0:T(8,128)(2,1)} %get-tuple-element.271.refs_2_, ...), custom_call_target="tpu_custom_call" | custom-call | tf_op jit(solution)/shard_map/pallas_call | solution.py:47
  362.8 8.8 %shard_map.443 = (bf16[768,1536]{1,0:T(8,128)(2,1)}, bf16[768,1536]{1,0:T(8,128)(2,1)}, bf16[768,1536]{1,0:T(8,128)(2,1)}, bf16[768,1536]{1,0:T(8,128)(2,1)}) custom-call(s32[8]{0:T(128)} %stack.348.order_ref, bf16[4,608,384]{2,1,0:T(8,128)(2,1)} %all-to-all-done.5.columns_ref, bf16[608,1536]{1,0:T(8,128)(2,1)} %get-tuple-element.281.inputs_ref), custom_call_target="tpu_custom_call" | custom-call | tf_op jit(solution)/shard_map/pallas_call | solution.py:47
  372.1 9.9 %shard_map.442 = (bf16[1536,768]{1,0:T(8,128)(2,1)}, bf16[1536,768]{1,0:T(8,128)(2,1)}, bf16[1536,768]{1,0:T(8,128)(2,1)}, bf16[1536,768]{1,0:T(8,128)(2,1)}) custom-call(s32[8]{0:T(128)} %stack.348.order_ref, bf16[4,608,384]{2,1,0:T(8,128)(2,1)} %copy-done.3, bf16[608,1536]{1,0:T(8,128)(2,1)} %get-tuple-element.276.inputs_ref), custom_call_target="tpu_custom_call" | custom-call | tf_op jit(solution)/shard_map/pallas_call | solution.py:47
  382.6 9.4 %shard_map.445 = bf16[4,608,384]{2,1,0:T(8,128)(2,1)} custom-call(s32[8]{0:T(128)} %stack.348.order_ref, bf16[608,1536]{1,0:T(8,128)(2,1)} %get-tuple-element.276.inputs_ref, bf16[1536,768]{1,0:T(8,128)(2,1)} %get-tuple-element.266.refs_0_, bf16[1536,768]{1,0:T(8,128)(2,1)} %collective-permute-done.27.refs_1_, bf16[1536,768]{1,0:T(8,128)(2,1)} %get-tuple-element.267.refs_2_, ...), custom_call_target="tpu_custom_call" | custom-call | tf_op jit(solution)/shard_map/pallas_call | solution.py:47
  394.1 11.4 %shard_map.444 = (bf16[768,768]{1,0:T(8,128)(2,1)}, bf16[768,768]{1,0:T(8,128)(2,1)}, bf16[1536,384]{1,0:T(8,128)(2,1)}, bf16[1536,384]{1,0:T(8,128)(2,1)}, bf16...) custom-call(s32[1]{0:T(128)} %constant.281.clone.1.order_ref, ...), custom_call_target="tpu_custom_call" | custom-call | tf_op jit(solution)/shard_map/pallas_call | solution.py:47
  409.0 9.7 %all_to_all.71 = f32[4,2,608]{2,1,0:T(2,128)} all-to-all(f32[4,2,608]{2,1,0:T(2,128)S(1)} %broadcast_in_dim.204), channel_id=1, replica_groups=mesh['dp'=4,'row'=2,'col'=4] {'col'}, dimensions={0} | all-to-all | bytes 38912 | tf_op jit(solution)/shard_map/all_to_all | solution.py:459
  434.3 25.2 %collective-permute-done.33.refs_1_ = bf16[768,768]{1,0:T(8,128)(2,1)} collective-permute-done((bf16[768,768]{1,0:T(8,128)(2,1)}, bf16[768,768]{1,0:T(8,128)(2,1)}, u32[]{:S(2)}, u32[]{:S(2)}) %collective-permute-start.33) | collective-permute-done | bytes 1179680 | tf_op jit(solution)/shard_map/ppermute | solution.py:447
  460.6 21.7 %collective-permute-done.35.refs_5_ = bf16[768,768]{1,0:T(8,128)(2,1)} collective-permute-done((bf16[768,768]{1,0:T(8,128)(2,1)}, bf16[768,768]{1,0:T(8,128)(2,1)}, u32[]{:S(2)}, u32[]{:S(2)}) %collective-permute-start.35) | collective-permute-done | bytes 1179680 | tf_op jit(solution)/shard_map/ppermute | solution.py:447
  504.1 9.9 %shard_map.447.inputs_ref = bf16[608,1152]{1,0:T(8,128)(2,1)} custom-call(s32[8]{0:T(128)} %stack.348.order_ref, bf16[608,1152]{1,0:T(8,128)(2,1)} %shard_map.434.packed_ref, bf16[608,384]{1,0:T(8,128)(2,1)} %get-tuple-element.329.inputs_ref.attended_ref, f32[6,608]{1,0:T(8,128)} %get-tuple-element.256.log_ref, bf16[608,384]{1,0:T(8,128)(2,1)} %shard_map.446.d_ref), custom_call_target="tpu_custom_call" | custom-call | tf_op jit(solution)/shard_map/pallas_call | solution.py:47
  596.4 10.3 %collective-permute-start.53 = (bf16[768,768]{1,0:T(8,128)(2,1)}, bf16[768,768]{1,0:T(8,128)(2,1)}, u32[]{:S(2)}, u32[]{:S(2)}) collective-permute-start(bf16[768,768]{1,0:T(8,128)(2,1)} %get-tuple-element.384), channel_id=1, source_target_pairs={{0,0},{1,9},{2,18},{3,27},{8,2},{9,11},{10,16},{11,25},{16,3},{17,... | collective-permute-start | bytes 3538952 | tf_op jit(solution)/shard_map/ppermute | solution.py:501
  630.6 23.9 %collective-permute-done.56 = bf16[2,2,14,384]{3,2,1,0:T(8,128)(2,1)S(1)} collective-permute-done((bf16[2,2,14,384]{3,2,1,0:T(8,128)(2,1)S(1)}, bf16[2,2,14,384]{3,2,1,0:T(8,128)(2,1)S(1)}, u32[]{:S(2)}, u32[]{:S(2)}) %collective-permute-start.56) | collective-permute-done | bytes 43040 | tf_op jit(solution)/shard_map/ppermute | solution.py:444
  670.2 11.0 %all-to-all-done.12 = bf16[2,4,96,768]{3,2,0,1:T(8,128)(2,1)S(1)} async-done(((bf16[2,4,96,768]{3,2,0,1:T(8,128)(2,1)}), bf16[2,4,96,768]{3,2,0,1:T(8,128)(2,1)S(1)}, u32[]{:S(2)}, u32[]{:S(2)}) %all-to-all-start.12) | async-done | bytes 1179680 | tf_op jit(solution)/shard_map/all_to_all | solution.py:514
  716.1 18.7 %collective-permute-start.64 = (f32[2,2,768]{2,1,0:T(2,128)S(1)}, f32[2,2,768]{2,1,0:T(2,128)S(1)}, u32[]{:S(2)}, u32[]{:S(2)}) collective-permute-start(f32[2,2,768]{2,1,0:T(2,128)S(1)} %pad_maximum_fusion.20), channel_id=1, source_target_pairs={{0,3},{1,0},{2,1},{3,2},{4,7},{5,4},{6,5},{7,6},{8,11},{9,8},{10,9... | collective-permute-start | bytes 36872 | tf_op jit(solution)/shard_map/ppermute | solution.py:451
  744.3 11.0 %all-to-all-done.13 = bf16[2,4,96,576]{3,2,0,1:T(8,128)(2,1)S(1)} async-done(((bf16[2,4,96,576]{3,2,0,1:T(8,128)(2,1)}), bf16[2,4,96,576]{3,2,0,1:T(8,128)(2,1)S(1)}, u32[]{:S(2)}, u32[]{:S(2)}) %all-to-all-start.13) | async-done | bytes 884768 | tf_op jit(solution)/shard_map/all_to_all | solution.py:514
  (609 shorter events, 448.0 us)
Async XLA Ops:
  4.1 38.8 %collective-permute-start.1 = (bf16[576,576]{1,0:T(8,128)(2,1)}, bf16[576,576]{1,0:T(8,128)(2,1)}, u32[]{:S(2)}, u32[]{:S(2)}) collective-permute-start(bf16[576,576]{1,0:T(8,128)(2,1)} %fusion.34), channel_id=1, source_target_pairs={{0,2},{1,3},{2,0},{3,1},{8,8},{9,9},{10,10},{11,11},{16,19},{17,16... | collective-permute-start | bytes 1990664 | tf_op jit(solution)/shard_map/ppermute | solution.py:434
  13.2 29.7 %collective-permute-start = (bf16[576,576]{1,0:T(8,128)(2,1)}, bf16[576,576]{1,0:T(8,128)(2,1)}, u32[]{:S(2)}, u32[]{:S(2)}) collective-permute-start(bf16[576,576]{1,0:T(8,128)(2,1)} %fusion.33), channel_id=1, source_target_pairs={{0,0},{1,1},{2,2},{3,3},{8,10},{9,11},{10,8},{11,9},{16,17},{17,18... | collective-permute-start | bytes 1990664 | tf_op jit(solution)/shard_map/ppermute | solution.py:434
  55.8 73.2 %all-to-all-start.1 = ((bf16[4,608,384]{2,1,0:T(8,128)(2,1)}), bf16[4,608,384]{2,1,0:T(8,128)(2,1)}, u32[]{:S(2)}, u32[]{:S(2)}) async-start(bf16[4,608,384]{2,1,0:T(8,128)(2,1)} %broadcast_in_dim.190), calls=%async_computation.1 | async-start | bytes 3735552 | tf_op jit(solution)/shard_map/all_to_all | solution.py:459
  71.2 29.9 %collective-permute-start.5 = (bf16[1152,576]{0,1:T(8,128)(2,1)}, bf16[1152,576]{0,1:T(8,128)(2,1)}, u32[]{:S(2)}, u32[]{:S(2)}) collective-permute-start(bf16[1152,576]{0,1:T(8,128)(2,1)} %copy.200), channel_id=1, source_target_pairs={{0,16},{8,24},{16,0},{24,8},{1,17},{9,25},{17,1},{25,9},{2,18},{10... | collective-permute-start | bytes 3981320 | tf_op jit(solution)/shard_map/ppermute | solution.py:444
  77.0 30.2 %collective-permute-start.6 = (bf16[1152,576]{0,1:T(8,128)(2,1)}, bf16[1152,576]{0,1:T(8,128)(2,1)}, u32[]{:S(2)}, u32[]{:S(2)}) collective-permute-start(bf16[1152,576]{0,1:T(8,128)(2,1)} %copy.202), channel_id=1, source_target_pairs={{0,4},{4,0},{1,5},{5,1},{2,6},{6,2},{3,7},{7,3},{8,12},{12,8},{9,1... | collective-permute-start | bytes 3981320 | tf_op jit(solution)/shard_map/ppermute | solution.py:447
  78.7 50.3 %collective-permute-start.8 = (bf16[384,768]{1,0:T(8,128)(2,1)}, bf16[384,768]{1,0:T(8,128)(2,1)}, u32[]{:S(2)}, u32[]{:S(2)}) collective-permute-start(bf16[384,768]{1,0:T(8,128)(2,1)} %constant_dynamic-slice_fusion.6), channel_id=1, source_target_pairs={{0,2},{1,3},{2,0},{3,1},{8,8},{9,9},{10,10},{11,11},{16,19},{17,16... | collective-permute-start | bytes 1769480 | tf_op jit(solution)/shard_map/ppermute | solution.py:434
  84.7 44.2 %collective-permute-start.7 = (bf16[384,768]{1,0:T(8,128)(2,1)}, bf16[384,768]{1,0:T(8,128)(2,1)}, u32[]{:S(2)}, u32[]{:S(2)}) collective-permute-start(bf16[384,768]{1,0:T(8,128)(2,1)} %constant_dynamic-slice_fusion.7), channel_id=1, source_target_pairs={{0,0},{1,1},{2,2},{3,3},{8,10},{9,11},{10,8},{11,9},{16,17},{17,18... | collective-permute-start | bytes 1769480 | tf_op jit(solution)/shard_map/ppermute | solution.py:434
  130.4 71.8 %all-to-all-start.2 = ((bf16[4,608,384]{2,1,0:T(8,128)(2,1)}), bf16[4,608,384]{2,1,0:T(8,128)(2,1)S(1)}, u32[]{:S(2)}, u32[]{:S(2)}) async-start(bf16[4,608,384]{2,1,0:T(8,128)(2,1)} %broadcast_in_dim.193), calls=%async_computation.2 | async-start | bytes 3735552 | tf_op jit(solution)/shard_map/all_to_all | solution.py:459
  143.6 54.2 %collective-permute-start.11 = (bf16[768,384]{1,0:T(8,128)(2,1)}, bf16[768,384]{1,0:T(8,128)(2,1)}, u32[]{:S(2)}, u32[]{:S(2)}) collective-permute-start(bf16[768,384]{1,0:T(8,128)(2,1)} %get-tuple-element.245), channel_id=1, source_target_pairs={{0,0},{1,1},{2,2},{3,3},{8,10},{9,11},{10,8},{11,9},{16,17},{17,18... | collective-permute-start | bytes 1769480 | tf_op jit(solution)/shard_map/ppermute | solution.py:434
  149.6 52.6 %collective-permute-start.12 = (bf16[768,384]{1,0:T(8,128)(2,1)}, bf16[768,384]{1,0:T(8,128)(2,1)}, u32[]{:S(2)}, u32[]{:S(2)}) collective-permute-start(bf16[768,384]{1,0:T(8,128)(2,1)} %get-tuple-element.246), channel_id=1, source_target_pairs={{0,2},{1,3},{2,0},{3,1},{8,8},{9,9},{10,10},{11,11},{16,19},{17,16... | collective-permute-start | bytes 1769480 | tf_op jit(solution)/shard_map/ppermute | solution.py:434
  202.2 52.6 %all-to-all-start.3 = ((bf16[4,608,384]{2,1,0:T(8,128)(2,1)}), bf16[4,608,384]{2,1,0:T(8,128)(2,1)}, u32[]{:S(2)}, u32[]{:S(2)}) async-start(bf16[4,608,384]{2,1,0:T(8,128)(2,1)} %shard_map.436), calls=%async_computation.3 | async-start | bytes 3735552 | tf_op jit(solution)/shard_map/all_to_all | solution.py:459
  270.5 53.8 %all-to-all-start.5 = ((bf16[4,608,384]{2,1,0:T(8,128)(2,1)}), bf16[4,608,384]{2,1,0:T(8,128)(2,1)}, u32[]{:S(2)}, u32[]{:S(2)}) async-start(bf16[4,608,384]{2,1,0:T(8,128)(2,1)} %broadcast_in_dim.203), calls=%async_computation.5 | async-start | bytes 3735552 | tf_op jit(solution)/shard_map/all_to_all | solution.py:459
  275.1 49.1 %collective-permute-start.19 = (bf16[768,1536]{1,0:T(8,128)(2,1)}, bf16[768,1536]{1,0:T(8,128)(2,1)}, u32[]{:S(2)}, u32[]{:S(2)}) collective-permute-start(bf16[768,1536]{1,0:T(8,128)(2,1)} %get-tuple-element.269.refs_0_), channel_id=1, source_target_pairs={{0,8},{8,0},{16,24},{24,16},{1,9},{9,1},{17,25},{25,17},{2,10},{10... | collective-permute-start | bytes 7077896 | tf_op jit(solution)/shard_map/ppermute | solution.py:444
  275.2 49.1 %collective-permute-start.20 = (bf16[768,1536]{1,0:T(8,128)(2,1)}, bf16[768,1536]{1,0:T(8,128)(2,1)}, u32[]{:S(2)}, u32[]{:S(2)}) collective-permute-start(bf16[768,1536]{1,0:T(8,128)(2,1)} %get-tuple-element.271.refs_2_), channel_id=1, source_target_pairs={{0,8},{8,0},{16,24},{24,16},{1,9},{9,1},{17,25},{25,17},{2,10},{10... | collective-permute-start | bytes 7077896 | tf_op jit(solution)/shard_map/ppermute | solution.py:444
  357.8 48.7 %all-to-all-start.6 = ((bf16[4,608,384]{2,1,0:T(8,128)(2,1)}), bf16[4,608,384]{2,1,0:T(8,128)(2,1)}, u32[]{:S(2)}, u32[]{:S(2)}) async-start(bf16[4,608,384]{2,1,0:T(8,128)(2,1)} %shard_map.441), calls=%async_computation.6 | async-start | bytes 3735552 | tf_op jit(solution)/shard_map/all_to_all | solution.py:459
  425.7 57.4 %all-to-all-start.8 = ((bf16[4,608,384]{2,1,0:T(8,128)(2,1)}), bf16[4,608,384]{2,1,0:T(8,128)(2,1)}, u32[]{:S(2)}, u32[]{:S(2)}) async-start(bf16[4,608,384]{2,1,0:T(8,128)(2,1)} %broadcast_in_dim.205), calls=%async_computation.8 | async-start | bytes 3735552 | tf_op jit(solution)/shard_map/all_to_all | solution.py:459
  431.7 50.6 %collective-permute-start.35 = (bf16[768,768]{1,0:T(8,128)(2,1)}, bf16[768,768]{1,0:T(8,128)(2,1)}, u32[]{:S(2)}, u32[]{:S(2)}) collective-permute-start(bf16[768,768]{1,0:T(8,128)(2,1)} %get-tuple-element.301), channel_id=1, source_target_pairs={{0,4},{4,0},{1,5},{5,1},{2,6},{6,2},{3,7},{7,3},{8,12},{12,8},{9,1... | collective-permute-start | bytes 3538952 | tf_op jit(solution)/shard_map/ppermute | solution.py:447
  432.5 50.6 %collective-permute-start.36 = (bf16[384,1536]{1,0:T(8,128)(2,1)}, bf16[384,1536]{1,0:T(8,128)(2,1)}, u32[]{:S(2)}, u32[]{:S(2)}) collective-permute-start(bf16[384,1536]{1,0:T(8,128)(2,1)} %get-tuple-element.303), channel_id=1, source_target_pairs={{0,16},{8,24},{16,0},{24,8},{1,17},{9,25},{17,1},{25,9},{2,18},{10... | collective-permute-start | bytes 3538952 | tf_op jit(solution)/shard_map/ppermute | solution.py:444
  483.1 46.0 %all-to-all-start.9 = ((bf16[4,608,384]{2,1,0:T(8,128)(2,1)}), bf16[4,608,384]{2,1,0:T(8,128)(2,1)}, u32[]{:S(2)}, u32[]{:S(2)}) async-start(bf16[4,608,384]{2,1,0:T(8,128)(2,1)} %shard_map.445), calls=%async_computation.9 | async-start | bytes 3735552 | tf_op jit(solution)/shard_map/all_to_all | solution.py:459
  529.1 47.6 %all-to-all-start.10 = ((bf16[4,608,384]{2,1,0:T(8,128)(2,1)}), bf16[4,608,384]{2,1,0:T(8,128)(2,1)}, u32[]{:S(2)}, u32[]{:S(2)}) async-start(bf16[4,608,384]{2,1,0:T(8,128)(2,1)} %shard_map.448), calls=%async_computation.10 | async-start | bytes 3735552 | tf_op jit(solution)/shard_map/all_to_all | solution.py:459
  596.4 60.7 %collective-permute-start.53 = (bf16[768,768]{1,0:T(8,128)(2,1)}, bf16[768,768]{1,0:T(8,128)(2,1)}, u32[]{:S(2)}, u32[]{:S(2)}) collective-permute-start(bf16[768,768]{1,0:T(8,128)(2,1)} %get-tuple-element.384), channel_id=1, source_target_pairs={{0,0},{1,9},{2,18},{3,27},{8,2},{9,11},{10,16},{11,25},{16,3},{17,... | collective-permute-start | bytes 3538952 | tf_op jit(solution)/shard_map/ppermute | solution.py:501
  607.4 51.5 %collective-permute-start.54 = (bf16[768,768]{1,0:T(8,128)(2,1)}, bf16[768,768]{1,0:T(8,128)(2,1)}, u32[]{:S(2)}, u32[]{:S(2)}) collective-permute-start(bf16[768,768]{1,0:T(8,128)(2,1)} %get-tuple-element.385), channel_id=1, source_target_pairs={{0,2},{1,11},{2,16},{3,25},{8,0},{9,9},{10,18},{11,27},{16,1},{17,... | collective-permute-start | bytes 3538952 | tf_op jit(solution)/shard_map/ppermute | solution.py:501
  627.8 42.1 %collective-permute-start.51 = (bf16[192,384]{1,0:T(8,128)(2,1)}, bf16[192,384]{1,0:T(8,128)(2,1)S(1)}, u32[]{:S(2)}, u32[]{:S(2)}) collective-permute-start(bf16[192,384]{1,0:T(8,128)(2,1)} %get-tuple-element.365), channel_id=1, source_target_pairs={{0,16},{8,24},{16,0},{24,8},{1,17},{9,25},{17,1},{25,9},{2,18},{10... | collective-permute-start | bytes 442376 | tf_op jit(solution)/shard_map/ppermute | solution.py:444
  629.8 40.1 %collective-permute-start.52 = (bf16[192,384]{1,0:T(8,128)(2,1)}, bf16[192,384]{1,0:T(8,128)(2,1)S(1)}, u32[]{:S(2)}, u32[]{:S(2)}) collective-permute-start(bf16[192,384]{1,0:T(8,128)(2,1)} %get-tuple-element.367), channel_id=1, source_target_pairs={{0,4},{4,0},{1,5},{5,1},{2,6},{6,2},{3,7},{7,3},{8,12},{12,8},{9,1... | collective-permute-start | bytes 442376 | tf_op jit(solution)/shard_map/ppermute | solution.py:447
  (150 other events, 1803.1 us)

commit v5 on v4

--- a/solution.py
+++ b/solution.py
@@ -43,11 +43,15 @@
 FREE = pl.CostEstimate(flops=0, bytes_accessed=0, transcendentals=0)
 
 
-def call(body, grid, in_specs, out_specs, out_shape, operands):
+def call(body, grid, in_specs, out_specs, out_shape, operands, scratch=()):
     return pl.pallas_call(
         body,
         grid_spec=pltpu.PrefetchScalarGridSpec(
-            num_scalar_prefetch=1, grid=grid, in_specs=in_specs, out_specs=out_specs
+            num_scalar_prefetch=1,
+            grid=grid,
+            in_specs=in_specs,
+            out_specs=out_specs,
+            scratch_shapes=scratch,
         ),
         out_shape=out_shape,
         cost_estimate=FREE,
@@ -76,12 +80,19 @@
 
     def body(order_ref, columns_ref, *refs):
         multiply = transposed_right if back else product
+        even_ref, odd_ref = refs[-2:]
+
+        @pl.when(pl.program_id(0) == 0)
+        def _():
+            for stream, (low, high) in enumerate(ranges):
+                for place, ref in enumerate((even_ref, odd_ref, even_ref, odd_ref)):
+                    lanes = slice(place // 2 * width, (place // 2 + 1) * width)
+                    ref[low:high, lanes] = columns_ref[order_ref[4 * stream + place], low:high]
+
         for stream, (low, high) in enumerate(ranges):
-            blocks = [columns_ref[order_ref[4 * stream + b], low:high] for b in range(4)]
-            even = jnp.concatenate([blocks[0], blocks[2]], axis=1)
-            odd = jnp.concatenate([blocks[1], blocks[3]], axis=1)
-            value = multiply(even, refs[2 * stream][...]) + multiply(odd, refs[2 * stream + 1][...])
-            finish(stream, slice(low, high), value, refs[4:])
+            value = multiply(even_ref[low:high], refs[2 * stream][...])
+            value += multiply(odd_ref[low:high], refs[2 * stream + 1][...])
+            finish(stream, slice(low, high), value, refs[4:-2])
 
     return call(
         body,
@@ -92,6 +103,7 @@
         [on_columns((rows, block)) for rows, _ in outs],
         [jax.ShapeDtypeStruct((rows, total), kind) for rows, kind in outs],
         (order, columns, *weights[0], *weights[1], *extra),
+        [pltpu.VMEM((tokens, 2 * width), BF)] * 2,
     )
 
 

time: 773 us -> 773 us (level)
  no operation moved by 1% of the time
where the time goes in v5:
time: 773 us; the launch traced here: 760 us
  waiting for transfers between devices  229 us (30%)
  Pallas kernels  183 us (24%)
  starting transfers between devices  161 us (21%)
  local copies, waits for them, and re-layouts  91.5 us (12%)
  other arithmetic  63.4 us (8%)
  blocking collectives  19.8 us (3%)
  matrix products  8.88 us (1%)
    pallas_call x26, Pallas kernels, call(): pl.pallas_call(body, grid_spec=pltpu.PrefetchScalarGridSpec(num_scalar_pr...  183 us
    ppermute x34, waiting for transfers between devices, swap_dp(): return lax.ppermute(values, 'dp', [(d, d ^ bit) for d in range(self.dps)])  94.4 us
    ppermute x18, waiting for transfers between devices, swap_row(): return lax.ppermute(values, 'row', [(0, 1), (1, 0)])  76.9 us
    all_to_all x10, starting transfers between devices, exchange(): return lax.all_to_all(values, 'col', 0, 0, tiled=True)  43.2 us
    ppermute x6, starting transfers between devices, spread(): lax.ppermute(values, PLANE, self.along_plane(lambda d, c: (d, c + self.ho...  34.4 us
    ppermute x34, starting transfers between devices, swap_dp(): return lax.ppermute(values, 'dp', [(d, d ^ bit) for d in range(self.dps)])  22.9 us
    all_to_all x2, waiting for transfers between devices, place_end(): return lax.all_to_all(moved, 'dp', 1, 1, tiled=True)  22 us
    ppermute x6, waiting for transfers between devices, spread(): lax.ppermute(values, PLANE, self.along_plane(lambda d, c: (d, c + self.ho...  20.4 us
  transfers between devices with their start and end apart: 77, of which 29 were waited for; matrix products, arithmetic and copies ran while one was open for 16% of the time, Pallas kernels for 20%

profile of v5, /device:TPU:0, one launch (start us, length us, event | category | flops | bytes accessed | tf_op | source)
XLA Modules:
  0.0 760.5 jit_solution(11044700644489328454)
XLA Ops:
  112.7 16.3 %collective-permute-done.8.refs_4_ = bf16[384,768]{1,0:T(8,128)(2,1)} collective-permute-done((bf16[384,768]{1,0:T(8,128)(2,1)}, bf16[384,768]{1,0:T(8,128)(2,1)}, u32[]{:S(2)}, u32[]{:S(2)}) %collective-permute-start.8) | collective-permute-done | bytes 589856 | tf_op jit(solution)/shard_map/ppermute | solution.py:446
  210.9 12.3 %collective-permute-done.13.refs_1_ = bf16[384,768]{1,0:T(8,128)(2,1)S(1)} collective-permute-done((bf16[384,768]{1,0:T(8,128)(2,1)}, bf16[384,768]{1,0:T(8,128)(2,1)S(1)}, u32[]{:S(2)}, u32[]{:S(2)}) %collective-permute-start.13) | collective-permute-done | bytes 589856 | tf_op jit(solution)/shard_map/ppermute | solution.py:459
  225.3 12.6 %collective-permute-done.14.refs_2_ = bf16[384,768]{1,0:T(8,128)(2,1)S(1)} collective-permute-done((bf16[384,768]{1,0:T(8,128)(2,1)}, bf16[384,768]{1,0:T(8,128)(2,1)S(1)}, u32[]{:S(2)}, u32[]{:S(2)}) %collective-permute-start.14) | collective-permute-done | bytes 589856 | tf_op jit(solution)/shard_map/ppermute | solution.py:456
  237.9 10.4 %collective-permute-done.15.refs_3_ = bf16[384,768]{1,0:T(8,128)(2,1)S(1)} collective-permute-done((bf16[384,768]{1,0:T(8,128)(2,1)S(1)}, bf16[384,768]{1,0:T(8,128)(2,1)S(1)}, u32[]{:S(2)}, u32[]{:S(2)}) %collective-permute-start.15) | collective-permute-done | bytes 589856 | tf_op jit(solution)/shard_map/ppermute | solution.py:456
  258.2 10.1 %all_to_all.70 = f32[4,2,608]{2,1,0:T(2,128)S(1)} all-to-all(f32[4,2,608]{2,1,0:T(2,128)S(1)} %broadcast_in_dim.194), channel_id=1, replica_groups=mesh['dp'=4,'row'=2,'col'=4] {'col'}, dimensions={0} | all-to-all | bytes 38912 | tf_op jit(solution)/shard_map/all_to_all | solution.py:471
  278.2 13.2 %collective-permute-done.22.refs_2_ = bf16[768,384]{1,0:T(8,128)(2,1)S(1)} collective-permute-done((bf16[768,384]{1,0:T(8,128)(2,1)}, bf16[768,384]{1,0:T(8,128)(2,1)S(1)}, u32[]{:S(2)}, u32[]{:S(2)}) %collective-permute-start.22) | collective-permute-done | bytes 589856 | tf_op jit(solution)/shard_map/ppermute | solution.py:459
  292.9 12.4 %collective-permute-done.24.refs_5_ = bf16[768,384]{1,0:T(8,128)(2,1)S(1)} collective-permute-done((bf16[768,384]{1,0:T(8,128)(2,1)}, bf16[768,384]{1,0:T(8,128)(2,1)S(1)}, u32[]{:S(2)}, u32[]{:S(2)}) %collective-permute-start.24) | collective-permute-done | bytes 589856 | tf_op jit(solution)/shard_map/ppermute | solution.py:456
  307.0 9.7 %collective-permute-done.23.refs_3_ = bf16[768,384]{1,0:T(8,128)(2,1)S(1)} collective-permute-done((bf16[768,384]{1,0:T(8,128)(2,1)S(1)}, bf16[768,384]{1,0:T(8,128)(2,1)S(1)}, u32[]{:S(2)}, u32[]{:S(2)}) %collective-permute-start.23) | collective-permute-done | bytes 589856 | tf_op jit(solution)/shard_map/ppermute | solution.py:456
  326.4 11.3 %shard_map.439 = (bf16[608,1536]{1,0:T(8,128)(2,1)}, f32[608,1536]{1,0:T(8,128)}) custom-call(s32[8]{0:T(128)} %stack.348.order_ref, bf16[4,608,384]{2,1,0:T(8,128)(2,1)} %all-to-all-done.5.columns_ref, bf16[768,1536]{1,0:T(8,128)(2,1)} %get-tuple-element.269.refs_0_, bf16[768,1536]{1,0:T(8,128)(2,1)} %collective-permute-done.19.refs_1_, ...), custom_call_target="tpu_custom_call" | custom-call | tf_op jit(solution)/shard_map/pallas_call | solution.py:47
  337.7 10.5 %shard_map.440 = (bf16[608,1536]{1,0:T(8,128)(2,1)}, f32[2,1536]{1,0:T(2,128)}) custom-call(s32[8]{0:T(128)} %stack.348.order_ref, bf16[4,608,384]{2,1,0:T(8,128)(2,1)} %copy-done.3, bf16[1536,768]{1,0:T(8,128)(2,1)} %get-tuple-element.266.refs_0_, bf16[1536,768]{1,0:T(8,128)(2,1)} %collective-permute-done.27.refs_1_, ...), custom_call_target="tpu_custom_call" | custom-call | tf_op jit(solution)/shard_map/pallas_call | solution.py:47
  348.3 9.8 %shard_map.441 = bf16[4,608,384]{2,1,0:T(8,128)(2,1)} custom-call(s32[8]{0:T(128)} %stack.348.order_ref, bf16[608,1536]{1,0:T(8,128)(2,1)} %get-tuple-element.281.inputs_ref, bf16[768,1536]{1,0:T(8,128)(2,1)} %get-tuple-element.269.refs_0_, bf16[768,1536]{1,0:T(8,128)(2,1)} %collective-permute-done.19.refs_1_, bf16[768,1536]{1,0:T(8,128)(2,1)} %get-tuple-element.271.refs_2_, ...), custom_call_target="tpu_custom_call" | custom-call | tf_op jit(solution)/shard_map/pallas_call | solution.py:47
  362.8 8.8 %shard_map.443 = (bf16[768,1536]{1,0:T(8,128)(2,1)}, bf16[768,1536]{1,0:T(8,128)(2,1)}, bf16[768,1536]{1,0:T(8,128)(2,1)}, bf16[768,1536]{1,0:T(8,128)(2,1)}) custom-call(s32[8]{0:T(128)} %stack.348.order_ref, bf16[4,608,384]{2,1,0:T(8,128)(2,1)} %all-to-all-done.5.columns_ref, bf16[608,1536]{1,0:T(8,128)(2,1)} %get-tuple-element.281.inputs_ref), custom_call_target="tpu_custom_call" | custom-call | tf_op jit(solution)/shard_map/pallas_call | solution.py:47
  372.1 9.9 %shard_map.442 = (bf16[1536,768]{1,0:T(8,128)(2,1)}, bf16[1536,768]{1,0:T(8,128)(2,1)}, bf16[1536,768]{1,0:T(8,128)(2,1)}, bf16[1536,768]{1,0:T(8,128)(2,1)}) custom-call(s32[8]{0:T(128)} %stack.348.order_ref, bf16[4,608,384]{2,1,0:T(8,128)(2,1)} %copy-done.3, bf16[608,1536]{1,0:T(8,128)(2,1)} %get-tuple-element.276.inputs_ref), custom_call_target="tpu_custom_call" | custom-call | tf_op jit(solution)/shard_map/pallas_call | solution.py:47
  382.5 9.4 %shard_map.445 = bf16[4,608,384]{2,1,0:T(8,128)(2,1)} custom-call(s32[8]{0:T(128)} %stack.348.order_ref, bf16[608,1536]{1,0:T(8,128)(2,1)} %get-tuple-element.276.inputs_ref, bf16[1536,768]{1,0:T(8,128)(2,1)} %get-tuple-element.266.refs_0_, bf16[1536,768]{1,0:T(8,128)(2,1)} %collective-permute-done.27.refs_1_, bf16[1536,768]{1,0:T(8,128)(2,1)} %get-tuple-element.267.refs_2_, ...), custom_call_target="tpu_custom_call" | custom-call | tf_op jit(solution)/shard_map/pallas_call | solution.py:47
  394.1 11.4 %shard_map.444 = (bf16[768,768]{1,0:T(8,128)(2,1)}, bf16[768,768]{1,0:T(8,128)(2,1)}, bf16[1536,384]{1,0:T(8,128)(2,1)}, bf16[1536,384]{1,0:T(8,128)(2,1)}, bf16...) custom-call(s32[1]{0:T(128)} %constant.281.clone.1.order_ref, ...), custom_call_target="tpu_custom_call" | custom-call | tf_op jit(solution)/shard_map/pallas_call | solution.py:47
  409.0 9.7 %all_to_all.71 = f32[4,2,608]{2,1,0:T(2,128)} all-to-all(f32[4,2,608]{2,1,0:T(2,128)S(1)} %broadcast_in_dim.204), channel_id=1, replica_groups=mesh['dp'=4,'row'=2,'col'=4] {'col'}, dimensions={0} | all-to-all | bytes 38912 | tf_op jit(solution)/shard_map/all_to_all | solution.py:471
  434.3 25.2 %collective-permute-done.33.refs_1_ = bf16[768,768]{1,0:T(8,128)(2,1)} collective-permute-done((bf16[768,768]{1,0:T(8,128)(2,1)}, bf16[768,768]{1,0:T(8,128)(2,1)}, u32[]{:S(2)}, u32[]{:S(2)}) %collective-permute-start.33) | collective-permute-done | bytes 1179680 | tf_op jit(solution)/shard_map/ppermute | solution.py:459
  460.5 21.7 %collective-permute-done.35.refs_5_ = bf16[768,768]{1,0:T(8,128)(2,1)} collective-permute-done((bf16[768,768]{1,0:T(8,128)(2,1)}, bf16[768,768]{1,0:T(8,128)(2,1)}, u32[]{:S(2)}, u32[]{:S(2)}) %collective-permute-start.35) | collective-permute-done | bytes 1179680 | tf_op jit(solution)/shard_map/ppermute | solution.py:459
  503.9 9.9 %shard_map.447.inputs_ref = bf16[608,1152]{1,0:T(8,128)(2,1)} custom-call(s32[8]{0:T(128)} %stack.348.order_ref, bf16[608,1152]{1,0:T(8,128)(2,1)} %shard_map.434.packed_ref, bf16[608,384]{1,0:T(8,128)(2,1)} %get-tuple-element.329.inputs_ref.attended_ref, f32[6,608]{1,0:T(8,128)} %get-tuple-element.256.log_ref, bf16[608,384]{1,0:T(8,128)(2,1)} %shard_map.446.d_ref), custom_call_target="tpu_custom_call" | custom-call | tf_op jit(solution)/shard_map/pallas_call | solution.py:47
  596.2 10.3 %collective-permute-start.53 = (bf16[768,768]{1,0:T(8,128)(2,1)}, bf16[768,768]{1,0:T(8,128)(2,1)}, u32[]{:S(2)}, u32[]{:S(2)}) collective-permute-start(bf16[768,768]{1,0:T(8,128)(2,1)} %get-tuple-element.384), channel_id=1, source_target_pairs={{0,0},{1,9},{2,18},{3,27},{8,2},{9,11},{10,16},{11,25},{16,3},{17,... | collective-permute-start | bytes 3538952 | tf_op jit(solution)/shard_map/ppermute | solution.py:513
  630.4 23.9 %collective-permute-done.56 = bf16[2,2,14,384]{3,2,1,0:T(8,128)(2,1)S(1)} collective-permute-done((bf16[2,2,14,384]{3,2,1,0:T(8,128)(2,1)S(1)}, bf16[2,2,14,384]{3,2,1,0:T(8,128)(2,1)S(1)}, u32[]{:S(2)}, u32[]{:S(2)}) %collective-permute-start.56) | collective-permute-done | bytes 43040 | tf_op jit(solution)/shard_map/ppermute | solution.py:456
  670.0 11.0 %all-to-all-done.12 = bf16[2,4,96,768]{3,2,0,1:T(8,128)(2,1)S(1)} async-done(((bf16[2,4,96,768]{3,2,0,1:T(8,128)(2,1)}), bf16[2,4,96,768]{3,2,0,1:T(8,128)(2,1)S(1)}, u32[]{:S(2)}, u32[]{:S(2)}) %all-to-all-start.12) | async-done | bytes 1179680 | tf_op jit(solution)/shard_map/all_to_all | solution.py:526
  715.9 18.7 %collective-permute-start.64 = (f32[2,2,768]{2,1,0:T(2,128)S(1)}, f32[2,2,768]{2,1,0:T(2,128)S(1)}, u32[]{:S(2)}, u32[]{:S(2)}) collective-permute-start(f32[2,2,768]{2,1,0:T(2,128)S(1)} %pad_maximum_fusion.20), channel_id=1, source_target_pairs={{0,3},{1,0},{2,1},{3,2},{4,7},{5,4},{6,5},{7,6},{8,11},{9,8},{10,9... | collective-permute-start | bytes 36872 | tf_op jit(solution)/shard_map/ppermute | solution.py:463
  744.1 11.0 %all-to-all-done.13 = bf16[2,4,96,576]{3,2,0,1:T(8,128)(2,1)S(1)} async-done(((bf16[2,4,96,576]{3,2,0,1:T(8,128)(2,1)}), bf16[2,4,96,576]{3,2,0,1:T(8,128)(2,1)S(1)}, u32[]{:S(2)}, u32[]{:S(2)}) %all-to-all-start.13) | async-done | bytes 884768 | tf_op jit(solution)/shard_map/all_to_all | solution.py:526
  (609 shorter events, 447.8 us)
Async XLA Ops:
  4.1 38.8 %collective-permute-start.1 = (bf16[576,576]{1,0:T(8,128)(2,1)}, bf16[576,576]{1,0:T(8,128)(2,1)}, u32[]{:S(2)}, u32[]{:S(2)}) collective-permute-start(bf16[576,576]{1,0:T(8,128)(2,1)} %fusion.34), channel_id=1, source_target_pairs={{0,2},{1,3},{2,0},{3,1},{8,8},{9,9},{10,10},{11,11},{16,19},{17,16... | collective-permute-start | bytes 1990664 | tf_op jit(solution)/shard_map/ppermute | solution.py:446
  13.2 29.7 %collective-permute-start = (bf16[576,576]{1,0:T(8,128)(2,1)}, bf16[576,576]{1,0:T(8,128)(2,1)}, u32[]{:S(2)}, u32[]{:S(2)}) collective-permute-start(bf16[576,576]{1,0:T(8,128)(2,1)} %fusion.33), channel_id=1, source_target_pairs={{0,0},{1,1},{2,2},{3,3},{8,10},{9,11},{10,8},{11,9},{16,17},{17,18... | collective-permute-start | bytes 1990664 | tf_op jit(solution)/shard_map/ppermute | solution.py:446
  55.8 73.2 %all-to-all-start.1 = ((bf16[4,608,384]{2,1,0:T(8,128)(2,1)}), bf16[4,608,384]{2,1,0:T(8,128)(2,1)}, u32[]{:S(2)}, u32[]{:S(2)}) async-start(bf16[4,608,384]{2,1,0:T(8,128)(2,1)} %broadcast_in_dim.190), calls=%async_computation.1 | async-start | bytes 3735552 | tf_op jit(solution)/shard_map/all_to_all | solution.py:471
  71.2 29.9 %collective-permute-start.5 = (bf16[1152,576]{0,1:T(8,128)(2,1)}, bf16[1152,576]{0,1:T(8,128)(2,1)}, u32[]{:S(2)}, u32[]{:S(2)}) collective-permute-start(bf16[1152,576]{0,1:T(8,128)(2,1)} %copy.200), channel_id=1, source_target_pairs={{0,16},{8,24},{16,0},{24,8},{1,17},{9,25},{17,1},{25,9},{2,18},{10... | collective-permute-start | bytes 3981320 | tf_op jit(solution)/shard_map/ppermute | solution.py:456
  77.0 30.2 %collective-permute-start.6 = (bf16[1152,576]{0,1:T(8,128)(2,1)}, bf16[1152,576]{0,1:T(8,128)(2,1)}, u32[]{:S(2)}, u32[]{:S(2)}) collective-permute-start(bf16[1152,576]{0,1:T(8,128)(2,1)} %copy.202), channel_id=1, source_target_pairs={{0,4},{4,0},{1,5},{5,1},{2,6},{6,2},{3,7},{7,3},{8,12},{12,8},{9,1... | collective-permute-start | bytes 3981320 | tf_op jit(solution)/shard_map/ppermute | solution.py:459
  78.7 50.3 %collective-permute-start.8 = (bf16[384,768]{1,0:T(8,128)(2,1)}, bf16[384,768]{1,0:T(8,128)(2,1)}, u32[]{:S(2)}, u32[]{:S(2)}) collective-permute-start(bf16[384,768]{1,0:T(8,128)(2,1)} %constant_dynamic-slice_fusion.6), channel_id=1, source_target_pairs={{0,2},{1,3},{2,0},{3,1},{8,8},{9,9},{10,10},{11,11},{16,19},{17,16... | collective-permute-start | bytes 1769480 | tf_op jit(solution)/shard_map/ppermute | solution.py:446
  84.7 44.2 %collective-permute-start.7 = (bf16[384,768]{1,0:T(8,128)(2,1)}, bf16[384,768]{1,0:T(8,128)(2,1)}, u32[]{:S(2)}, u32[]{:S(2)}) collective-permute-start(bf16[384,768]{1,0:T(8,128)(2,1)} %constant_dynamic-slice_fusion.7), channel_id=1, source_target_pairs={{0,0},{1,1},{2,2},{3,3},{8,10},{9,11},{10,8},{11,9},{16,17},{17,18... | collective-permute-start | bytes 1769480 | tf_op jit(solution)/shard_map/ppermute | solution.py:446
  130.4 71.8 %all-to-all-start.2 = ((bf16[4,608,384]{2,1,0:T(8,128)(2,1)}), bf16[4,608,384]{2,1,0:T(8,128)(2,1)S(1)}, u32[]{:S(2)}, u32[]{:S(2)}) async-start(bf16[4,608,384]{2,1,0:T(8,128)(2,1)} %broadcast_in_dim.193), calls=%async_computation.2 | async-start | bytes 3735552 | tf_op jit(solution)/shard_map/all_to_all | solution.py:471
  143.6 54.4 %collective-permute-start.11 = (bf16[768,384]{1,0:T(8,128)(2,1)}, bf16[768,384]{1,0:T(8,128)(2,1)}, u32[]{:S(2)}, u32[]{:S(2)}) collective-permute-start(bf16[768,384]{1,0:T(8,128)(2,1)} %get-tuple-element.245), channel_id=1, source_target_pairs={{0,0},{1,1},{2,2},{3,3},{8,10},{9,11},{10,8},{11,9},{16,17},{17,18... | collective-permute-start | bytes 1769480 | tf_op jit(solution)/shard_map/ppermute | solution.py:446
  149.6 52.6 %collective-permute-start.12 = (bf16[768,384]{1,0:T(8,128)(2,1)}, bf16[768,384]{1,0:T(8,128)(2,1)}, u32[]{:S(2)}, u32[]{:S(2)}) collective-permute-start(bf16[768,384]{1,0:T(8,128)(2,1)} %get-tuple-element.246), channel_id=1, source_target_pairs={{0,2},{1,3},{2,0},{3,1},{8,8},{9,9},{10,10},{11,11},{16,19},{17,16... | collective-permute-start | bytes 1769480 | tf_op jit(solution)/shard_map/ppermute | solution.py:446
  202.2 52.6 %all-to-all-start.3 = ((bf16[4,608,384]{2,1,0:T(8,128)(2,1)}), bf16[4,608,384]{2,1,0:T(8,128)(2,1)}, u32[]{:S(2)}, u32[]{:S(2)}) async-start(bf16[4,608,384]{2,1,0:T(8,128)(2,1)} %shard_map.436), calls=%async_computation.3 | async-start | bytes 3735552 | tf_op jit(solution)/shard_map/all_to_all | solution.py:471
  270.5 54.0 %all-to-all-start.5 = ((bf16[4,608,384]{2,1,0:T(8,128)(2,1)}), bf16[4,608,384]{2,1,0:T(8,128)(2,1)}, u32[]{:S(2)}, u32[]{:S(2)}) async-start(bf16[4,608,384]{2,1,0:T(8,128)(2,1)} %broadcast_in_dim.203), calls=%async_computation.5 | async-start | bytes 3735552 | tf_op jit(solution)/shard_map/all_to_all | solution.py:471
  275.3 49.1 %collective-permute-start.19 = (bf16[768,1536]{1,0:T(8,128)(2,1)}, bf16[768,1536]{1,0:T(8,128)(2,1)}, u32[]{:S(2)}, u32[]{:S(2)}) collective-permute-start(bf16[768,1536]{1,0:T(8,128)(2,1)} %get-tuple-element.269.refs_0_), channel_id=1, source_target_pairs={{0,8},{8,0},{16,24},{24,16},{1,9},{9,1},{17,25},{25,17},{2,10},{10... | collective-permute-start | bytes 7077896 | tf_op jit(solution)/shard_map/ppermute | solution.py:456
  275.4 49.1 %collective-permute-start.20 = (bf16[768,1536]{1,0:T(8,128)(2,1)}, bf16[768,1536]{1,0:T(8,128)(2,1)}, u32[]{:S(2)}, u32[]{:S(2)}) collective-permute-start(bf16[768,1536]{1,0:T(8,128)(2,1)} %get-tuple-element.271.refs_2_), channel_id=1, source_target_pairs={{0,8},{8,0},{16,24},{24,16},{1,9},{9,1},{17,25},{25,17},{2,10},{10... | collective-permute-start | bytes 7077896 | tf_op jit(solution)/shard_map/ppermute | solution.py:456
  358.0 48.4 %all-to-all-start.6 = ((bf16[4,608,384]{2,1,0:T(8,128)(2,1)}), bf16[4,608,384]{2,1,0:T(8,128)(2,1)}, u32[]{:S(2)}, u32[]{:S(2)}) async-start(bf16[4,608,384]{2,1,0:T(8,128)(2,1)} %shard_map.441), calls=%async_computation.6 | async-start | bytes 3735552 | tf_op jit(solution)/shard_map/all_to_all | solution.py:471
  425.7 57.4 %all-to-all-start.8 = ((bf16[4,608,384]{2,1,0:T(8,128)(2,1)}), bf16[4,608,384]{2,1,0:T(8,128)(2,1)}, u32[]{:S(2)}, u32[]{:S(2)}) async-start(bf16[4,608,384]{2,1,0:T(8,128)(2,1)} %broadcast_in_dim.205), calls=%async_computation.8 | async-start | bytes 3735552 | tf_op jit(solution)/shard_map/all_to_all | solution.py:471
  431.7 50.6 %collective-permute-start.35 = (bf16[768,768]{1,0:T(8,128)(2,1)}, bf16[768,768]{1,0:T(8,128)(2,1)}, u32[]{:S(2)}, u32[]{:S(2)}) collective-permute-start(bf16[768,768]{1,0:T(8,128)(2,1)} %get-tuple-element.301), channel_id=1, source_target_pairs={{0,4},{4,0},{1,5},{5,1},{2,6},{6,2},{3,7},{7,3},{8,12},{12,8},{9,1... | collective-permute-start | bytes 3538952 | tf_op jit(solution)/shard_map/ppermute | solution.py:459
  432.5 50.6 %collective-permute-start.36 = (bf16[384,1536]{1,0:T(8,128)(2,1)}, bf16[384,1536]{1,0:T(8,128)(2,1)}, u32[]{:S(2)}, u32[]{:S(2)}) collective-permute-start(bf16[384,1536]{1,0:T(8,128)(2,1)} %get-tuple-element.303), channel_id=1, source_target_pairs={{0,16},{8,24},{16,0},{24,8},{1,17},{9,25},{17,1},{25,9},{2,18},{10... | collective-permute-start | bytes 3538952 | tf_op jit(solution)/shard_map/ppermute | solution.py:456
  483.1 45.7 %all-to-all-start.9 = ((bf16[4,608,384]{2,1,0:T(8,128)(2,1)}), bf16[4,608,384]{2,1,0:T(8,128)(2,1)}, u32[]{:S(2)}, u32[]{:S(2)}) async-start(bf16[4,608,384]{2,1,0:T(8,128)(2,1)} %shard_map.445), calls=%async_computation.9 | async-start | bytes 3735552 | tf_op jit(solution)/shard_map/all_to_all | solution.py:471
  528.8 47.6 %all-to-all-start.10 = ((bf16[4,608,384]{2,1,0:T(8,128)(2,1)}), bf16[4,608,384]{2,1,0:T(8,128)(2,1)}, u32[]{:S(2)}, u32[]{:S(2)}) async-start(bf16[4,608,384]{2,1,0:T(8,128)(2,1)} %shard_map.448), calls=%async_computation.10 | async-start | bytes 3735552 | tf_op jit(solution)/shard_map/all_to_all | solution.py:471
  596.2 60.7 %collective-permute-start.53 = (bf16[768,768]{1,0:T(8,128)(2,1)}, bf16[768,768]{1,0:T(8,128)(2,1)}, u32[]{:S(2)}, u32[]{:S(2)}) collective-permute-start(bf16[768,768]{1,0:T(8,128)(2,1)} %get-tuple-element.384), channel_id=1, source_target_pairs={{0,0},{1,9},{2,18},{3,27},{8,2},{9,11},{10,16},{11,25},{16,3},{17,... | collective-permute-start | bytes 3538952 | tf_op jit(solution)/shard_map/ppermute | solution.py:513
  607.2 51.5 %collective-permute-start.54 = (bf16[768,768]{1,0:T(8,128)(2,1)}, bf16[768,768]{1,0:T(8,128)(2,1)}, u32[]{:S(2)}, u32[]{:S(2)}) collective-permute-start(bf16[768,768]{1,0:T(8,128)(2,1)} %get-tuple-element.385), channel_id=1, source_target_pairs={{0,2},{1,11},{2,16},{3,25},{8,0},{9,9},{10,18},{11,27},{16,1},{17,... | collective-permute-start | bytes 3538952 | tf_op jit(solution)/shard_map/ppermute | solution.py:513
  627.6 42.1 %collective-permute-start.51 = (bf16[192,384]{1,0:T(8,128)(2,1)}, bf16[192,384]{1,0:T(8,128)(2,1)S(1)}, u32[]{:S(2)}, u32[]{:S(2)}) collective-permute-start(bf16[192,384]{1,0:T(8,128)(2,1)} %get-tuple-element.365), channel_id=1, source_target_pairs={{0,16},{8,24},{16,0},{24,8},{1,17},{9,25},{17,1},{25,9},{2,18},{10... | collective-permute-start | bytes 442376 | tf_op jit(solution)/shard_map/ppermute | solution.py:456
  629.6 40.1 %collective-permute-start.52 = (bf16[192,384]{1,0:T(8,128)(2,1)}, bf16[192,384]{1,0:T(8,128)(2,1)S(1)}, u32[]{:S(2)}, u32[]{:S(2)}) collective-permute-start(bf16[192,384]{1,0:T(8,128)(2,1)} %get-tuple-element.367), channel_id=1, source_target_pairs={{0,4},{4,0},{1,5},{5,1},{2,6},{6,2},{3,7},{7,3},{8,12},{12,8},{9,1... | collective-permute-start | bytes 442376 | tf_op jit(solution)/shard_map/ppermute | solution.py:459
  (150 other events, 1803.1 us)
